TPU v7x, 32 devices: a whole 2x2x4 slice. The times are simulated.
32 devices in a mesh: dp: 2 (over x), seq: 4 (over z), tensor: 4 (over y, core).
Axes of the slice: x: 2, y: 2, z: 4, core: 2. Of those that a mesh axis runs over, the one named last changes fastest.
Arguments:
- inputs: bfloat16 [2, 2560, 2048], P('dp', 'seq'), may hold values from -6 to 6
- first_gain: bfloat16 [2048], P(('dp', 'seq')), may hold values from 0.099609375 to 1.8984375
- w_query: bfloat16 [2048, 2048], P(('dp', 'seq'), 'tensor'), may hold values from -0.125 to 0.125
- w_key: bfloat16 [2048, 2048], P(('dp', 'seq'), 'tensor'), may hold values from -0.125 to 0.125
- w_value: bfloat16 [2048, 2048], P(('dp', 'seq'), 'tensor'), may hold values from -0.125 to 0.125
- w_out: bfloat16 [2048, 2048], P('tensor', ('dp', 'seq')), may hold values from -6 to 6
- second_gain: bfloat16 [2048], P(('dp', 'seq')), may hold values from 0.099609375 to 1.8984375
- w_up: bfloat16 [2048, 8192], P(('dp', 'seq'), 'tensor'), may hold values from -0.125 to 0.125
- w_down: bfloat16 [8192, 2048], P('tensor', ('dp', 'seq')), may hold values from -0.0625 to 0.0625
- frame_mask: int32 [2, 4], P('dp'), may hold values from 0 to 1, as said below
- cotangent: bfloat16 [2, 2560, 2048], P('dp', 'seq'), may hold values from -6 to 6
Outputs:
- result: bfloat16 [2, 2560, 2048], P('dp', 'seq')
- grad_inputs: bfloat16 [2, 2560, 2048], P('dp', 'seq')
- grad_first_gain: float32 [2048], P(('dp', 'seq'))
- grad_query: float32 [2048, 2048], P(('dp', 'seq'), 'tensor')
- grad_key: float32 [2048, 2048], P(('dp', 'seq'), 'tensor')
- grad_value: float32 [2048, 2048], P(('dp', 'seq'), 'tensor')
- grad_out: float32 [2048, 2048], P('tensor', ('dp', 'seq'))
- grad_second_gain: float32 [2048], P(('dp', 'seq'))
- grad_up: float32 [2048, 8192], P(('dp', 'seq'), 'tensor')
- grad_down: float32 [8192, 2048], P('tensor', ('dp', 'seq'))
Inputs may be any that keep to these rules, and one draw needn't show every extreme that they name: `frame_mask`: frame 0 of every clip is valid. One clip, drawn from the seed, has all 4 frames valid; the other has exactly 1 invalid frame.
All inputs are finite; a program needn't handle non-finite values.
Results may differ from a plain program's by a relative error of at most 0.024.
Values may be sent and summed in bfloat16 or wider, within the bound.
A program may use at most 256 MiB of HBM per device.

v0:
```python
import jax
import jax.numpy as jnp
from jax import lax
from jax.sharding import PartitionSpec as P

HEAD_DIM = 128
FRAME_TOK = 640


NORM_EPS = 1e-05
MASK_FILL = -1e30


def norm_rows(values):
    center = values - jnp.mean(values, axis=-1, keepdims=True)
    spread = jnp.mean(center * center, axis=-1, keepdims=True)
    return center * lax.rsqrt(spread + NORM_EPS)


def gelu_exact(values):
    return jax.nn.gelu(values, approximate=False)


def heads_total(values):
    return lax.psum(values.astype(jnp.bfloat16), "tensor").astype(jnp.float32)


def local(
    inputs,
    first_gain,
    w_query,
    w_key,
    w_value,
    w_out,
    second_gain,
    w_up,
    w_down,
    frame_mask,
    cotangent,
):
    seq_pos = lax.axis_index("seq")
    gain_one, query_w, key_w, value_w, gain_two, up_w = (
        lax.all_gather(first_gain, ("dp", "seq"), axis=0, tiled=True),
        lax.all_gather(w_query, ("dp", "seq"), axis=0, tiled=True),
        lax.all_gather(w_key, ("dp", "seq"), axis=0, tiled=True),
        lax.all_gather(w_value, ("dp", "seq"), axis=0, tiled=True),
        lax.all_gather(second_gain, ("dp", "seq"), axis=0, tiled=True),
        lax.all_gather(w_up, ("dp", "seq"), axis=0, tiled=True),
    )
    out_w, down_w = (
        lax.all_gather(w_out, ("dp", "seq"), axis=1, tiled=True),
        lax.all_gather(w_down, ("dp", "seq"), axis=1, tiled=True),
    )
    tok_rows = inputs.shape[1]
    local_inner = query_w.shape[1]
    local_heads = local_inner // HEAD_DIM
    frames_dev = tok_rows // FRAME_TOK
    score_scale = HEAD_DIM ** (-0.5)
    clip_valid = frame_mask[0]
    frame_count = clip_valid.shape[0]
    resid_in = inputs[0].astype(jnp.float32)
    dout_rows = cotangent[0]
    row_frame = seq_pos * frames_dev + jnp.arange(tok_rows, dtype=jnp.int32) // FRAME_TOK
    frame_limit = (seq_pos + 1) * frames_dev
    normed_one = norm_rows(resid_in)
    first_in = (normed_one * gain_one.astype(jnp.float32)).astype(jnp.bfloat16)
    query = jnp.dot(first_in, query_w, preferred_element_type=jnp.float32).astype(jnp.bfloat16)
    key_local = jnp.dot(first_in, key_w, preferred_element_type=jnp.float32).astype(jnp.bfloat16)
    value_local = jnp.dot(first_in, value_w, preferred_element_type=jnp.float32).astype(
        jnp.bfloat16
    )
    key_all, value_all = (
        lax.all_gather(key_local, "seq", axis=0, tiled=True),
        lax.all_gather(value_local, "seq", axis=0, tiled=True),
    )
    query_heads = query.reshape(tok_rows, local_heads, HEAD_DIM)
    key_frames = key_all.reshape(frame_count, FRAME_TOK, local_heads, HEAD_DIM)
    value_frames = value_all.reshape(frame_count, FRAME_TOK, local_heads, HEAD_DIM)

    def frame_scores(frame_idx):
        key_block = lax.dynamic_index_in_dim(key_frames, frame_idx, 0, keepdims=False)
        value_block = lax.dynamic_index_in_dim(value_frames, frame_idx, 0, keepdims=False)
        scores = (
            jnp.einsum("qhd,khd->hqk", query_heads, key_block, preferred_element_type=jnp.float32)
            * score_scale
        )
        frame_ok = lax.dynamic_index_in_dim(clip_valid, frame_idx, 0, keepdims=False) == 1
        allowed = ((frame_idx <= row_frame) & frame_ok)[None, :, None]
        return (scores, allowed, key_block, value_block)

    def stats_step(frame_idx, running):
        row_max, row_sum = running
        scores, allowed, key_block, value_block = frame_scores(frame_idx)
        masked = jnp.where(allowed, scores, MASK_FILL)
        new_max = jnp.maximum(row_max, jnp.max(masked, axis=2))
        exp_terms = jnp.where(allowed, jnp.exp(masked - new_max[:, :, None]), 0.0)
        return (new_max, row_sum * jnp.exp(row_max - new_max) + jnp.sum(exp_terms, axis=2))

    start_stats = (
        jnp.full((local_heads, tok_rows), MASK_FILL, jnp.float32),
        jnp.zeros((local_heads, tok_rows), jnp.float32),
    )
    row_max, row_sum = lax.fori_loop(0, frame_limit, stats_step, start_stats)

    def soft_weights(scores, allowed):
        return jnp.where(allowed, jnp.exp(scores - row_max[:, :, None]) / row_sum[:, :, None], 0.0)

    def output_step(frame_idx, running):
        scores, allowed, key_block, value_block = frame_scores(frame_idx)
        attn_prob = soft_weights(scores, allowed).astype(jnp.bfloat16)
        return running + jnp.einsum(
            "hqk,khd->qhd", attn_prob, value_block, preferred_element_type=jnp.float32
        )

    attended = lax.fori_loop(
        0, frame_limit, output_step, jnp.zeros((tok_rows, local_heads, HEAD_DIM), jnp.float32)
    )
    attended_low = attended.reshape(tok_rows, local_inner).astype(jnp.bfloat16)
    resid_mid = resid_in + heads_total(
        jnp.dot(attended_low, out_w, preferred_element_type=jnp.float32)
    )
    normed_two = norm_rows(resid_mid)
    second_in = (normed_two * gain_two.astype(jnp.float32)).astype(jnp.bfloat16)
    up_pre = jnp.dot(second_in, up_w, preferred_element_type=jnp.float32)
    up_act = gelu_exact(up_pre).astype(jnp.bfloat16)
    resid_out = resid_mid + heads_total(jnp.dot(up_act, down_w, preferred_element_type=jnp.float32))
    result = resid_out.astype(jnp.bfloat16)[None]
    grad_down = jnp.einsum("tf,td->fd", up_act, dout_rows, preferred_element_type=jnp.float32)
    d_act = jnp.einsum("td,fd->tf", dout_rows, down_w, preferred_element_type=jnp.float32)
    gelu_pull = jax.vjp(gelu_exact, up_pre)[1]
    d_up_pre = gelu_pull(d_act)[0].astype(jnp.bfloat16)
    grad_up = jnp.einsum("td,tf->df", second_in, d_up_pre, preferred_element_type=jnp.float32)
    d_second = heads_total(
        jnp.einsum("tf,df->td", d_up_pre, up_w, preferred_element_type=jnp.float32)
    )
    grad_second_gain = jnp.sum(d_second * normed_two, axis=0)
    norm_pull_two = jax.vjp(norm_rows, resid_mid)[1]
    d_mid = (
        dout_rows.astype(jnp.float32) + norm_pull_two(d_second * gain_two.astype(jnp.float32))[0]
    )
    d_mix = d_mid.astype(jnp.bfloat16)
    grad_out = jnp.einsum("ti,td->id", attended_low, d_mix, preferred_element_type=jnp.float32)
    d_attended = jnp.einsum("td,id->ti", d_mix, out_w, preferred_element_type=jnp.float32).astype(
        jnp.bfloat16
    )
    dout_heads = d_attended.reshape(tok_rows, local_heads, HEAD_DIM)
    row_delta = jnp.sum(dout_heads.astype(jnp.float32) * attended, axis=2).T

    def query_step(frame_idx, running):
        scores, allowed, key_block, value_block = frame_scores(frame_idx)
        attn_prob = soft_weights(scores, allowed)
        d_prob = jnp.einsum(
            "qhd,khd->hqk", dout_heads, value_block, preferred_element_type=jnp.float32
        )
        d_scores = (attn_prob * (d_prob - row_delta[:, :, None])).astype(jnp.bfloat16)
        return running + jnp.einsum(
            "hqk,khd->qhd", d_scores, key_block, preferred_element_type=jnp.float32
        )

    query_sum = lax.fori_loop(
        0, frame_limit, query_step, jnp.zeros((tok_rows, local_heads, HEAD_DIM), jnp.float32)
    )
    d_query = (query_sum * score_scale).reshape(tok_rows, local_inner).astype(jnp.bfloat16)

    def one_frame(frame_step):
        scores, allowed, key_block, value_block = frame_scores(frame_step)
        attn_prob = soft_weights(scores, allowed)
        d_prob = jnp.einsum(
            "qhd,khd->hqk", dout_heads, value_block, preferred_element_type=jnp.float32
        )
        d_scores = (attn_prob * (d_prob - row_delta[:, :, None])).astype(jnp.bfloat16)
        key_term = (
            jnp.einsum("hqk,qhd->khd", d_scores, query_heads, preferred_element_type=jnp.float32)
            * score_scale
        )
        value_term = jnp.einsum(
            "hqk,qhd->khd",
            attn_prob.astype(jnp.bfloat16),
            dout_heads,
            preferred_element_type=jnp.float32,
        )
        return jnp.concatenate(
            [key_term.reshape(FRAME_TOK, local_inner), value_term.reshape(FRAME_TOK, local_inner)],
            axis=1,
        )

    blocks = lax.map(
        one_frame, jnp.arange(tok_rows * lax.axis_size("seq") // FRAME_TOK, dtype=jnp.int32)
    )
    kv_grad = lax.psum_scatter(
        blocks.reshape(tok_rows * lax.axis_size("seq"), 2 * local_inner).astype(jnp.bfloat16),
        "seq",
        scatter_dimension=0,
        tiled=True,
    ).astype(jnp.float32)
    d_key = kv_grad[:, :local_inner].astype(jnp.bfloat16)
    d_value = kv_grad[:, local_inner:].astype(jnp.bfloat16)
    grad_query = jnp.einsum("td,ti->di", first_in, d_query, preferred_element_type=jnp.float32)
    grad_key = jnp.einsum("td,ti->di", first_in, d_key, preferred_element_type=jnp.float32)
    grad_value = jnp.einsum("td,ti->di", first_in, d_value, preferred_element_type=jnp.float32)
    first_local = jnp.einsum("ti,di->td", d_query, query_w, preferred_element_type=jnp.float32)
    first_local = first_local + jnp.einsum(
        "ti,di->td", d_key, key_w, preferred_element_type=jnp.float32
    )
    first_local = first_local + jnp.einsum(
        "ti,di->td", d_value, value_w, preferred_element_type=jnp.float32
    )
    d_first = heads_total(first_local)
    grad_first_gain = jnp.sum(d_first * normed_one, axis=0)
    norm_pull_one = jax.vjp(norm_rows, resid_in)[1]
    grad_inputs = (d_mid + norm_pull_one(d_first * gain_one.astype(jnp.float32))[0]).astype(
        jnp.bfloat16
    )[None]
    summed_in = (
        lax.psum_scatter(
            grad_first_gain.astype(jnp.bfloat16), ("dp", "seq"), scatter_dimension=0, tiled=True
        ).astype(jnp.float32),
        lax.psum_scatter(
            grad_query.astype(jnp.bfloat16), ("dp", "seq"), scatter_dimension=0, tiled=True
        ).astype(jnp.float32),
        lax.psum_scatter(
            grad_key.astype(jnp.bfloat16), ("dp", "seq"), scatter_dimension=0, tiled=True
        ).astype(jnp.float32),
        lax.psum_scatter(
            grad_value.astype(jnp.bfloat16), ("dp", "seq"), scatter_dimension=0, tiled=True
        ).astype(jnp.float32),
        lax.psum_scatter(
            grad_second_gain.astype(jnp.bfloat16), ("dp", "seq"), scatter_dimension=0, tiled=True
        ).astype(jnp.float32),
        lax.psum_scatter(
            grad_up.astype(jnp.bfloat16), ("dp", "seq"), scatter_dimension=0, tiled=True
        ).astype(jnp.float32),
    )
    summed_out = (
        lax.psum_scatter(
            grad_out.astype(jnp.bfloat16), ("dp", "seq"), scatter_dimension=1, tiled=True
        ).astype(jnp.float32),
        lax.psum_scatter(
            grad_down.astype(jnp.bfloat16), ("dp", "seq"), scatter_dimension=1, tiled=True
        ).astype(jnp.float32),
    )
    return (
        result,
        grad_inputs,
        summed_in[0],
        summed_in[1],
        summed_in[2],
        summed_in[3],
        summed_out[0],
        summed_in[4],
        summed_in[5],
        summed_out[1],
    )


def solution(mesh):
    placed = (
        P("dp", "seq", None),
        P(("dp", "seq")),
        P(("dp", "seq"), "tensor"),
        P(("dp", "seq"), "tensor"),
        P(("dp", "seq"), "tensor"),
        P("tensor", ("dp", "seq")),
        P(("dp", "seq")),
        P(("dp", "seq"), "tensor"),
        P("tensor", ("dp", "seq")),
        P("dp", None),
        P("dp", "seq", None),
    )
    return jax.shard_map(
        local,
        mesh=mesh,
        in_specs=placed,
        out_specs=(
            P("dp", "seq", None),
            P("dp", "seq", None),
            P(("dp", "seq")),
            P(("dp", "seq"), "tensor"),
            P(("dp", "seq"), "tensor"),
            P(("dp", "seq"), "tensor"),
            P("tensor", ("dp", "seq")),
            P(("dp", "seq")),
            P(("dp", "seq"), "tensor"),
            P("tensor", ("dp", "seq")),
        ),
        check_vma=False,
    )
```

profile of v0, /device:TPU:0, one launch (start us, length us, event | category | flops | bytes accessed | tf_op | source)
XLA Modules:
  0.0 1617.9 jit_solution(10890351596134987313)
XLA Ops:
  10.1 22.3 %all-gather = bf16[8,1,256]{2,1,0:T(2,128)(2,1)S(1)} all-gather(bf16[1,1,256]{2,1,0:T(2,128)(2,1)S(1)} %reshape.153), channel_id=1, replica_groups=mesh['dp'=2,'seq'=4,'tensor'=4] {'dp','seq'}, dimensions={0}, use_global_device_ids=true | all-gather | bytes 4608 | tf_op jit(solution)/shard_map/all_gather | solution.py:43
  38.9 23.3 %all-gather.15.cloned.1.call-done = bf16[2048,512]{1,0:T(8,128)(2,1)} async-done(((bf16[256,512]{1,0:T(8,128)(2,1)}), bf16[2048,512]{1,0:T(8,128)(2,1)}) %all-gather.15.cloned.1.call-update) | async-done | bytes 2097168 | tf_op jit(solution)/shard_map/all_gather | solution.py:45
  67.0 45.1 %all-gather.11.cloned.1.call-done = bf16[2048,512]{1,0:T(8,128)(2,1)} async-done(((bf16[256,512]{1,0:T(8,128)(2,1)}), bf16[2048,512]{1,0:T(8,128)(2,1)}) %all-gather.11.cloned.1.call-update) | async-done | bytes 2097168 | tf_op jit(solution)/shard_map/all_gather | solution.py:46
  117.7 44.4 %all-gather.19.cloned.1.call-done = bf16[2048,512]{1,0:T(8,128)(2,1)} async-done(((bf16[256,512]{1,0:T(8,128)(2,1)}), bf16[2048,512]{1,0:T(8,128)(2,1)}) %all-gather.19.cloned.1.call-update) | async-done | bytes 2097168 | tf_op jit(solution)/shard_map/all_gather | solution.py:44
  168.6 48.8 %all-gather.17.cloned.1.call-done = bf16[2560,512]{1,0:T(8,128)(2,1)} async-done(((bf16[640,512]{1,0:T(8,128)(2,1)}), bf16[2560,512]{1,0:T(8,128)(2,1)}) %all-gather.17.cloned.1.call-update) | async-done | bytes 2621456 | tf_op jit(solution)/shard_map/all_gather | solution.py:73
  231.1 41.9 %all-gather.13.cloned.1.call-done = bf16[2560,512]{1,0:T(8,128)(2,1)} async-done(((bf16[640,512]{1,0:T(8,128)(2,1)}), bf16[2560,512]{1,0:T(8,128)(2,1)}) %all-gather.13.cloned.1.call-update) | async-done | bytes 2621456 | tf_op jit(solution)/shard_map/all_gather | solution.py:74
  292.0 32.7 %all-gather.21.cloned.1.call-done = bf16[512,2048]{1,0:T(8,128)(2,1)} async-done(((bf16[512,256]{1,0:T(8,128)(2,1)}), bf16[512,2048]{1,0:T(8,128)(2,1)}) %all-gather.21.cloned.1.call-update) | async-done | bytes 2097168 | tf_op jit(solution)/shard_map/all_gather | solution.py:51
  331.2 17.7 %all-gather.1 = bf16[8,1,256]{2,1,0:T(2,128)(2,1)S(1)} all-gather(bf16[1,1,256]{2,1,0:T(2,128)(2,1)S(1)} %reshape.155), channel_id=1, replica_groups=mesh['dp'=2,'seq'=4,'tensor'=4] {'dp','seq'}, dimensions={0}, use_global_device_ids=true | all-gather | bytes 4608 | tf_op jit(solution)/shard_map/all_gather | solution.py:47
  348.9 39.0 %all-reduce.8.cloned.1.call-done = bf16[640,2048]{1,0:T(8,128)(2,1)} async-done(((bf16[640,2048]{1,0:T(8,128)(2,1)}), bf16[640,2048]{1,0:T(8,128)(2,1)}) %all-reduce.8.cloned.1.call-update) | async-done | bytes 2621456 | tf_op jit(solution)/shard_map/psum | solution.py:25
  391.7 123.4 %all-gather.23.cloned.1.call-done = bf16[2048,2048]{1,0:T(8,128)(2,1)} async-done(((bf16[256,2048]{1,0:T(8,128)(2,1)}), bf16[2048,2048]{1,0:T(8,128)(2,1)}) %all-gather.23.cloned.1.call-update) | async-done | bytes 8388624 | tf_op jit(solution)/shard_map/all_gather | solution.py:48
  515.1 23.4 %multiply_convert_fusion.10 = (bf16[640,2048]{1,0:T(8,128)(2,1)}, f32[640,2048]{1,0:T(8,128)}, f32[640,2048]{1,0:T(8,128)}) fusion(bf16[2048,2048]{1,0:T(8,128)(2,1)} %all-gather.23.cloned.1.call-done, bf16[640,2048]{1,0:T(8,128)(2,1)} %all-reduce.8.cloned.1.call-done, bf16[1,640,2048]{2,1,0:T(8,128)(2,1)S(1)} %copy-done, f32[2048]{0:T(1024)S(1)} %bitcast.249, ...), kind=kOutput, calls=%fused_computation.132 | convolution fusion | flops 5463080960 | bytes 26752000 | tf_op jit(solution)/shard_map/dot_general | solution.py:124
  538.5 102.2 %all-gather.25.cloned.1.call-done = bf16[2048,2048]{1,0:T(8,128)(2,1)} async-done(((bf16[2048,256]{1,0:T(8,128)(2,1)}), bf16[2048,2048]{1,0:T(8,128)(2,1)}) %all-gather.25.cloned.1.call-update) | async-done | bytes 8388624 | tf_op jit(solution)/shard_map/all_gather | solution.py:52
  640.7 14.6 add_convert_fusion.2
  668.0 54.4 %all-reduce.10.cloned.1.call-done = bf16[640,2048]{1,0:T(8,128)(2,1)} async-done(((bf16[640,2048]{1,0:T(8,128)(2,1)}), bf16[640,2048]{1,0:T(8,128)(2,1)}) %all-reduce.10.cloned.1.call-update) | async-done | bytes 2621456 | tf_op jit(solution)/shard_map/psum | solution.py:25
  735.8 84.6 %while.50 = (s32[]{:T(128)}, bf16[4,640,1024]{2,1,0:T(8,128)(2,1)}, s32[4]{0:T(128)S(1)}, s32[4]{0:T(128)S(1)}, bf16[4,640,4,128]{3,1,2,0:T(8,128)(2,1)}, /*inde...) while((s32[]{:T(128)}, bf16[4,640,1024]{2,1,0:T(8,128)(2,1)}, ...), condition=%wide.region_19.20_spmd.clone, body=%wide.region_18.19_spmd.clone.sunk | while | flops 1694112000 | bytes 32800744 | solution.py:187
  861.1 53.4 %reduce-scatter.8.cloned.1.call-done = bf16[640,1024]{1,0:T(8,128)(2,1)} async-done(((bf16[2560,1024]{1,0:T(8,128)(2,1)}), bf16[640,1024]{1,0:T(8,128)(2,1)}) %reduce-scatter.8.cloned.1.call-update) | async-done | bytes 1310736 | tf_op jit(solution)/shard_map/reduce_scatter | solution.py:190
  957.9 28.7 %reduce-scatter.16.cloned.1.call-done = bf16[512,256]{1,0:T(8,128)(2,1)} async-done(((bf16[512,2048]{1,0:T(8,128)(2,1)}), bf16[512,256]{1,0:T(8,128)(2,1)}) %reduce-scatter.16.cloned.1.call-update) | async-done | bytes 262160 | tf_op jit(solution)/shard_map/reduce_scatter | solution.py:235
  988.4 69.2 %reduce-scatter.10.cloned.1.call-done = bf16[256,512]{1,0:T(8,128)(2,1)} async-done(((bf16[2048,512]{1,0:T(8,128)(2,1)}), bf16[256,512]{1,0:T(8,128)(2,1)}) %reduce-scatter.10.cloned.1.call-update) | async-done | bytes 262160 | tf_op jit(solution)/shard_map/reduce_scatter | solution.py:218
  1059.4 102.8 %all-reduce.12.cloned.1.call-done = (bf16[640,2048]{1,0:T(8,128)(2,1)}, bf16[640,2048]{1,0:T(8,128)(2,1)}) async-done(((bf16[640,2048]{1,0:T(8,128)(2,1)}, bf16[640,2048]{1,0:T(8,128)(2,1)}), (bf16[640,2048]{1,0:T(8,128)(2,1)}, bf16[640,2048]{1,0:T(8,128)(2,1)})) %all-reduce.12.cloned.1.call-update) | async-done | bytes 5242896 | tf_op jit(solution)/shard_map/psum | solution.py:25
  1167.7 22.5 %all-reduce.2 = (bf16[2048]{0:T(1024)(128)(2,1)S(1)}, bf16[2048]{0:T(1024)(128)(2,1)S(1)}) all-reduce(bf16[2048]{0:T(1024)(128)(2,1)S(1)} %get-tuple-element.486, bf16[2048]{0:T(1024)(128)(2,1)S(1)} %copy-done.33), channel_id=3, replica_groups=mesh['dp'=2,'seq'=4,'tensor'=4] {'dp','seq'}, use_global_device_ids=true, to_apply=%region_25.26.clone | all-reduce | flops 4096 | bytes 16384
  1199.7 34.4 %reduce-scatter.12.cloned.1.call-done = bf16[256,512]{1,0:T(8,128)(2,1)} async-done(((bf16[2048,512]{1,0:T(8,128)(2,1)}), bf16[256,512]{1,0:T(8,128)(2,1)}) %reduce-scatter.12.cloned.1.call-update) | async-done | bytes 262160 | tf_op jit(solution)/shard_map/reduce_scatter | solution.py:221
  1235.9 68.4 %reduce-scatter.14.cloned.1.call-done = bf16[256,512]{1,0:T(8,128)(2,1)} async-done(((bf16[2048,512]{1,0:T(8,128)(2,1)}), bf16[256,512]{1,0:T(8,128)(2,1)}) %reduce-scatter.14.cloned.1.call-update) | async-done | bytes 262160 | tf_op jit(solution)/shard_map/reduce_scatter | solution.py:224
  1306.1 149.7 %reduce-scatter.18.cloned.1.call-done = bf16[256,2048]{1,0:T(8,128)(2,1)} async-done(((bf16[2048,2048]{1,0:T(8,128)(2,1)}), bf16[256,2048]{1,0:T(8,128)(2,1)}) %reduce-scatter.18.cloned.1.call-update) | async-done | bytes 1048592 | tf_op jit(solution)/shard_map/reduce_scatter | solution.py:230
  1458.6 149.6 %reduce-scatter.20.cloned.1.call-done = bf16[2048,256]{1,0:T(8,128)(2,1)} async-done(((bf16[2048,2048]{1,0:T(8,128)(2,1)}), bf16[2048,256]{1,0:T(8,128)(2,1)}) %reduce-scatter.20.cloned.1.call-update) | async-done | bytes 1048592 | tf_op jit(solution)/shard_map/reduce_scatter | solution.py:238
  (230 shorter events, 306.6 us)
Async XLA Ops:
  7.2 55.0 %all-gather.15.cloned.1.call-start = ((), (), s32[]{:S(2)}) async-start(), calls=%async_computation.9 | async-start | bytes 2359296 | tf_op jit(solution)/shard_map/all_gather | solution.py:45
  7.9 104.2 %all-gather.11.cloned.1.call-start = ((), (), s32[]{:S(2)}) async-start(), calls=%async_computation.7 | async-start | bytes 2359296 | tf_op jit(solution)/shard_map/all_gather | solution.py:46
  8.7 153.4 %all-gather.19.cloned.1.call-start = ((), (), s32[]{:S(2)}) async-start(), calls=%async_computation.11 | async-start | bytes 2359296 | tf_op jit(solution)/shard_map/all_gather | solution.py:44
  9.4 208.0 %all-gather.17.cloned.1.call-start = ((), (), s32[]{:S(2)}) async-start(), calls=%async_computation.10 | async-start | bytes 3276800 | tf_op jit(solution)/shard_map/all_gather | solution.py:73
  67.0 206.1 %all-gather.13.cloned.1.call-start = ((), (), s32[]{:S(2)}) async-start(), calls=%async_computation.8 | async-start | bytes 3276800 | tf_op jit(solution)/shard_map/all_gather | solution.py:74
  116.9 207.9 %all-gather.21.cloned.1.call-start = ((), (), s32[]{:S(2)}) async-start(), calls=%async_computation.12 | async-start | bytes 2359296 | tf_op jit(solution)/shard_map/all_gather | solution.py:51
  117.5 270.4 %all-reduce.8.cloned.1.call-start = ((), (), s32[]{:S(2)}) async-start(), calls=%async_computation.13 | async-start | bytes 5242880 | tf_op jit(solution)/shard_map/psum | solution.py:25
  168.6 57.5 %copy-start.37 = (s32[1,4]{1,0:T(1,128)S(1)}, s32[1,4]{1,0:T(1,128)}, u32[]{:S(2)}) copy-start(s32[1,4]{1,0:T(1,128)} %param.28) | copy-start | bytes 52
  289.6 40.0 %copy-start.2 = (bf16[640,4,128]{2,0,1:T(8,128)(2,1)}, bf16[640,4,128]{2,0,1:T(8,128)(2,1)S(1)}, u32[]{:S(2)}) copy-start(bf16[640,4,128]{2,0,1:T(8,128)(2,1)S(1)} %get-tuple-element.1048) | copy-start | bytes 1966084
  329.6 185.4 %all-gather.23.cloned.1.call-start = ((), (), s32[]{:S(2)}) async-start(), calls=%async_computation.14 | async-start | bytes 9437184 | tf_op jit(solution)/shard_map/all_gather | solution.py:48
  330.4 310.3 %all-gather.25.cloned.1.call-start = ((), (), s32[]{:S(2)}) async-start(), calls=%async_computation.15 | async-start | bytes 9437184 | tf_op jit(solution)/shard_map/all_gather | solution.py:52
  331.1 391.3 %all-reduce.10.cloned.1.call-start = ((), (), s32[]{:S(2)}) async-start(), calls=%async_computation.16 | async-start | bytes 5242880 | tf_op jit(solution)/shard_map/psum | solution.py:25
  348.9 379.1 %copy-start.21 = (f32[8,1,256]{2,1,0:T(1,128)}, f32[8,1,256]{2,1,0:T(1,128)S(1)}, u32[]{:S(2)}) copy-start(f32[8,1,256]{2,1,0:T(1,128)S(1)} %convert_element_type.219) | copy-start | bytes 24580
  390.5 337.4 %copy-start.23 = (f32[640]{0:T(1024)}, f32[640]{0:T(1024)S(1)}, u32[]{:S(2)}) copy-start(f32[640]{0:T(1024)S(1)} %broadcast_multiply_fusion) | copy-start | bytes 7684
  391.7 336.3 %copy-start.27 = (f32[640]{0:T(1024)}, f32[640]{0:T(1024)S(1)}, u32[]{:S(2)}) copy-start(f32[640]{0:T(1024)S(1)} %fusion.131) | copy-start | bytes 7684
  664.2 250.2 %reduce-scatter.8.cloned.1.call-start = ((), (), s32[]{:S(2)}) async-start(), calls=%async_computation.17 | async-start | bytes 6553600 | tf_op jit(solution)/shard_map/reduce_scatter | solution.py:190
  820.4 166.2 %reduce-scatter.16.cloned.1.call-start = ((), (), s32[]{:S(2)}) async-start(), calls=%async_computation.21 | async-start | bytes 2359296 | tf_op jit(solution)/shard_map/reduce_scatter | solution.py:235
  826.6 231.1 %reduce-scatter.10.cloned.1.call-start = ((), (), s32[]{:S(2)}) async-start(), calls=%async_computation.18 | async-start | bytes 2359296 | tf_op jit(solution)/shard_map/reduce_scatter | solution.py:218
  846.4 315.8 %all-reduce.12.cloned.1.call-start = ((), (), s32[]{:S(2)}) async-start(), calls=%async_computation.24 | async-start | bytes 10485760 | tf_op jit(solution)/shard_map/psum | solution.py:25
  921.9 312.2 %reduce-scatter.12.cloned.1.call-start = ((), (), s32[]{:S(2)}) async-start(), calls=%async_computation.19 | async-start | bytes 2359296 | tf_op jit(solution)/shard_map/reduce_scatter | solution.py:221
  927.5 376.9 %reduce-scatter.14.cloned.1.call-start = ((), (), s32[]{:S(2)}) async-start(), calls=%async_computation.20 | async-start | bytes 2359296 | tf_op jit(solution)/shard_map/reduce_scatter | solution.py:224
  932.6 523.2 %reduce-scatter.18.cloned.1.call-start = ((), (), s32[]{:S(2)}) async-start(), calls=%async_computation.22 | async-start | bytes 9437184 | tf_op jit(solution)/shard_map/reduce_scatter | solution.py:230
  944.6 663.5 %reduce-scatter.20.cloned.1.call-start = ((), (), s32[]{:S(2)}) async-start(), calls=%async_computation.23 | async-start | bytes 9437184 | tf_op jit(solution)/shard_map/reduce_scatter | solution.py:238
  956.0 209.2 %copy-start.30 = (f32[640]{0:T(1024)S(1)}, f32[640]{0:T(1024)}, u32[]{:S(2)}) copy-start(f32[640]{0:T(1024)} %copy-done.29) | copy-start | bytes 7684
  (33 other events, 228.1 us)
Sparse Core Ops, SparseCore 0:
  10.1 51.9 all-gather.14
  64.3 47.7 all-gather.10
  114.3 47.7 all-gather.18
  164.1 53.2 all-gather.16
  219.4 53.5 all-gather.12
  274.9 49.8 all-gather.20
  329.8 58.0 all-reduce.7
  390.0 125.0 all-gather.22
  517.1 123.5 all-gather.24
  664.3 58.0 all-reduce.9
  820.6 93.8 reduce-scatter.7
  917.8 68.7 reduce-scatter.15
  990.7 66.8 reduce-scatter.9
  1060.4 101.7 all-reduce.11
  1166.2 67.8 reduce-scatter.11
  1237.5 66.7 reduce-scatter.13
  1307.8 147.9 reduce-scatter.17
  1459.7 148.3 reduce-scatter.19
where the time goes:
time: 1620 us
  waiting for transfers between devices  1220 us (75%)
  matrix products  209 us (13%)
  blocking collectives  62.5 us (4%)
  other arithmetic  53.4 us (3%)
  local copies, waits for them, and re-layouts  47.7 us (3%)
    psum x3, waiting for transfers between devices, heads_total(): return lax.psum(values.astype(jnp.bfloat16), 'tensor').astype(jnp.float32)  196 us
    reduce_scatter x1, waiting for transfers between devices, local(): lax.psum_scatter(grad_up.astype(jnp.bfloat16), ('dp', 'seq'), scatter_dim...  150 us
    reduce_scatter x1, waiting for transfers between devices, local(): lax.psum_scatter(grad_down.astype(jnp.bfloat16), ('dp', 'seq'), scatter_d...  150 us
    all_gather x1, waiting for transfers between devices, local(): lax.all_gather(w_up, ('dp', 'seq'), axis=0, tiled=True)  123 us
    all_gather x1, waiting for transfers between devices, local(): lax.all_gather(w_down, ('dp', 'seq'), axis=1, tiled=True)  102 us
    reduce_scatter x1, waiting for transfers between devices, local(): lax.psum_scatter(grad_query.astype(jnp.bfloat16), ('dp', 'seq'), scatter_...  69.2 us
    reduce_scatter x1, waiting for transfers between devices, local(): lax.psum_scatter(grad_value.astype(jnp.bfloat16), ('dp', 'seq'), scatter_...  68.4 us
    reduce_scatter x1, waiting for transfers between devices, local(): lax.psum_scatter(blocks.reshape(tok_rows * lax.axis_size('seq'), 2 * loca...  53.4 us
  transfers between devices with their start and end apart: 18, of which 18 were waited for; matrix products, arithmetic and copies ran while one was open for 12% of the time, Pallas kernels for 0%

commit v1 on v0

--- a/solution.py
+++ b/solution.py
@@ -1,6 +1,10 @@
+import functools
+
 import jax
 import jax.numpy as jnp
 from jax import lax
+from jax.experimental import pallas as pl
+from jax.experimental.pallas import tpu as pltpu
 from jax.sharding import PartitionSpec as P
 
 HEAD_DIM = 128
@@ -253,6 +257,319 @@
     )
 
 
+def shift(values, k):
+    return lax.ppermute(values, "seq", [(i, (i + k) % SEQ) for i in range(SEQ)])
+
+
+def swap_dp(values):
+    return lax.ppermute(values, "dp", [(0, 1), (1, 0)])
+
+
+def swap_chip(values):
+    return lax.ppermute(values, "tensor", [(i, i ^ 2) for i in range(4)])
+
+
+def swap_core(values):
+    return lax.ppermute(values, "tensor", [(i, i ^ 1) for i in range(4)])
+
+
+def tied(value, *others):
+    return lax.optimization_barrier((value, *others))[0]
+
+
+def gather_tensor(own):
+    half = jnp.concatenate([own, swap_chip(own)], axis=0)
+    return jnp.concatenate([half, swap_core(half)], axis=0)
+
+
+def scatter_tensor(part):
+    n = part.shape[0] // 4
+    low = part.astype(jnp.bfloat16)
+    half = part[: 2 * n].astype(jnp.float32) + swap_core(low[2 * n :]).astype(jnp.float32)
+    other = swap_chip(half[n:].astype(jnp.bfloat16))
+    return half[:n] + other.astype(jnp.float32)
+
+
+def gather_blocks(own):
+    mine = [own]
+    for _ in range(SEQ - 1):
+        mine.append(shift(mine[-1], 1))
+    return mine, [swap_dp(block) for block in mine]
+
+
+def scatter_blocks(parts):
+    running = None
+    for k in (1, 2, 3, 0):
+        total = parts[k].astype(jnp.float32) + swap_dp(parts[SEQ + k]).astype(jnp.float32)
+        if running is not None:
+            total = total + running.astype(jnp.float32)
+        if k:
+            running = shift(total.astype(jnp.bfloat16), 1)
+    return total
+
+
+def dyn(stack, index):
+    return lax.dynamic_index_in_dim(stack, index, 0, keepdims=False)
+
+
+def attend_kernel(place_ref, valid_ref, q_ref, k_ref, v_ref, out_ref, lse_ref, peak, total, acc):
+    place = place_ref[0]
+    scale = HEAD_DIM ** (-0.5)
+
+    def query_frame(i, carry):
+        at = lax.rem(place - i + SEQ, SEQ)
+        query = q_ref[at]
+        peak[...] = jnp.full_like(peak, MASK_FILL)
+        total[...] = jnp.zeros_like(total)
+        acc[...] = jnp.zeros_like(acc)
+
+        def key_frame(j, inner):
+            @pl.when(valid_ref[j] == 1)
+            def _():
+                here = lax.rem(place - j + SEQ, SEQ)
+                scores = lax.dot_general(k_ref[here], query, (((1,), (1,)), ((), ())), preferred_element_type=jnp.float32) * scale
+                before = peak[...]
+                after = jnp.maximum(before, jnp.max(scores, axis=0, keepdims=True))
+                terms = jnp.exp(scores - after)
+                fix = jnp.exp(before - after)
+                peak[...] = after
+                total[...] = total[...] * fix + jnp.sum(terms, axis=0, keepdims=True)
+                acc[...] = acc[...] * fix + lax.dot_general(v_ref[here], terms.astype(jnp.bfloat16), (((0,), (0,)), ((), ())), preferred_element_type=jnp.float32)
+
+            return inner
+
+        lax.fori_loop(0, i + 1, key_frame, 0)
+        out_ref[at] = (acc[...] / total[...]).T
+        lse_ref[at] = peak[...] + jnp.log(total[...])
+        return carry
+
+    lax.fori_loop(0, SEQ, query_frame, 0)
+
+
+def attend(place, valid, query, key, value):
+    rows = query.shape[1]
+    smem = pl.BlockSpec(memory_space=pltpu.SMEM)
+    vmem = pl.BlockSpec(memory_space=pltpu.VMEM)
+    return pl.pallas_call(
+        attend_kernel,
+        out_shape=(jax.ShapeDtypeStruct(query.shape, jnp.float32), jax.ShapeDtypeStruct((SEQ, 1, rows), jnp.float32)),
+        in_specs=[smem, smem, vmem, vmem, vmem],
+        out_specs=(vmem, vmem),
+        scratch_shapes=[pltpu.VMEM((1, rows), jnp.float32), pltpu.VMEM((1, rows), jnp.float32), pltpu.VMEM((HEAD_DIM, rows), jnp.float32)],
+        compiler_params=pltpu.CompilerParams(vmem_limit_bytes=40 * 2**20),
+        cost_estimate=pl.CostEstimate(flops=4 * 10 * rows * rows * HEAD_DIM * 2, bytes_accessed=6 * query.size, transcendentals=10 * rows * rows),
+    )(place, valid, query, key, value)
+
+
+def attend_back_kernel(place_ref, valid_ref, q_ref, k_ref, v_ref, out_ref, lse_ref, do_ref, grad_ref, delta, dq, dk, dv):
+    place = place_ref[0]
+    scale = HEAD_DIM ** (-0.5)
+    dq[...] = jnp.zeros_like(dq)
+    for f in range(SEQ):
+        delta[f] = jnp.sum((do_ref[f].astype(jnp.float32) * out_ref[f]).T, axis=0, keepdims=True)
+
+    def key_frame(j, carry):
+        here = lax.rem(place - j + SEQ, SEQ)
+        dk[...] = jnp.zeros_like(dk)
+        dv[...] = jnp.zeros_like(dv)
+
+        @pl.when(valid_ref[j] == 1)
+        def _():
+            def query_frame(i, inner):
+                at = lax.rem(place - i + SEQ, SEQ)
+                query, key, value, d_out = q_ref[at], k_ref[here], v_ref[here], do_ref[at]
+                scores = lax.dot_general(key, query, (((1,), (1,)), ((), ())), preferred_element_type=jnp.float32) * scale
+                prob = jnp.exp(scores - lse_ref[at])
+                d_prob = lax.dot_general(value, d_out, (((1,), (1,)), ((), ())), preferred_element_type=jnp.float32)
+                d_scores = (prob * (d_prob - delta[at])).astype(jnp.bfloat16)
+                dv[...] += jnp.dot(prob.astype(jnp.bfloat16), d_out, preferred_element_type=jnp.float32)
+                dk[...] += jnp.dot(d_scores, query, preferred_element_type=jnp.float32)
+                dq[at] += lax.dot_general(key, d_scores, (((0,), (0,)), ((), ())), preferred_element_type=jnp.float32)
+                return inner
+
+            lax.fori_loop(j, SEQ, query_frame, 0)
+
+        grad_ref[here, :, HEAD_DIM : 2 * HEAD_DIM] = (dk[...] * scale).astype(jnp.bfloat16)
+        grad_ref[here, :, 2 * HEAD_DIM :] = dv[...].astype(jnp.bfloat16)
+        return carry
+
+    lax.fori_loop(0, SEQ, key_frame, 0)
+    for f in range(SEQ):
+        grad_ref[f, :, :HEAD_DIM] = (dq[f] * scale).T.astype(jnp.bfloat16)
+
+
+def attend_back(place, valid, query, key, value, out, lse, d_out):
+    rows = query.shape[1]
+    smem = pl.BlockSpec(memory_space=pltpu.SMEM)
+    vmem = pl.BlockSpec(memory_space=pltpu.VMEM)
+    return pl.pallas_call(
+        attend_back_kernel,
+        out_shape=jax.ShapeDtypeStruct((SEQ, rows, 3 * HEAD_DIM), jnp.bfloat16),
+        in_specs=[smem, smem] + [vmem] * 6,
+        out_specs=vmem,
+        scratch_shapes=[
+            pltpu.VMEM((SEQ, 1, rows), jnp.float32),
+            pltpu.VMEM((SEQ, HEAD_DIM, rows), jnp.float32),
+            pltpu.VMEM((rows, HEAD_DIM), jnp.float32),
+            pltpu.VMEM((rows, HEAD_DIM), jnp.float32),
+        ],
+        compiler_params=pltpu.CompilerParams(vmem_limit_bytes=48 * 2**20),
+        cost_estimate=pl.CostEstimate(flops=10 * 10 * rows * rows * HEAD_DIM * 2, bytes_accessed=12 * query.size, transcendentals=10 * rows * rows),
+    )(place, valid, query, key, value, out, lse, d_out)
+
+
+def norm_parts(values):
+    center = values - jnp.mean(values, axis=-1, keepdims=True)
+    rate = lax.rsqrt(jnp.mean(center * center, axis=-1, keepdims=True) + NORM_EPS)
+    return center * rate, rate
+
+
+def norm_back(normed, rate, grad):
+    return rate * (grad - jnp.mean(grad, axis=-1, keepdims=True) - normed * jnp.mean(grad * normed, axis=-1, keepdims=True))
+
+
+def mm(left, right, dims=((1,), (0,)), out=jnp.bfloat16):
+    return lax.dot_general(left, right, (dims, ((), ())), preferred_element_type=jnp.float32).astype(out)
+
+
+def local_fast(inputs, first_gain, w_query, w_key, w_value, w_out, second_gain, w_up, w_down, frame_mask, cotangent):
+    dp, z, t = lax.axis_index("dp"), lax.axis_index("seq"), lax.axis_index("tensor")
+    rows = inputs.shape[1]
+    quarter = rows // 4
+    width = inputs.shape[2]
+    part = width // (2 * SEQ)
+    heads = w_query.shape[1] // HEAD_DIM
+    f32, bf16 = jnp.float32, jnp.bfloat16
+
+    def rel_block(b):
+        return (dp ^ (b // SEQ)) * SEQ + lax.rem(z - b % SEQ + SEQ, SEQ)
+
+    def rel_cols(values):
+        return jnp.concatenate([lax.dynamic_slice_in_dim(values, rel_block(b) * part, part, 1) for b in range(2 * SEQ)], axis=1)
+
+    def can_cols(values):
+        picks = []
+        for c in range(2 * SEQ):
+            b = (dp ^ (c // SEQ)) * SEQ + lax.rem(z - c % SEQ + SEQ, SEQ)
+            picks.append(lax.dynamic_slice_in_dim(values, b * part, part, 1))
+        return jnp.concatenate(picks, axis=1)
+
+    def rel_rows(values):
+        return jnp.concatenate([lax.dynamic_slice_in_dim(values, (t ^ p) * quarter, quarter, 0) for p in (0, 2, 1, 3)], axis=0)
+
+    def can_rows(values):
+        picks = []
+        for c in range(4):
+            d = t ^ c
+            p = (d % 2) * 2 + d // 2
+            picks.append(lax.dynamic_slice_in_dim(values, p * quarter, quarter, 0))
+        return jnp.concatenate(picks, axis=0)
+
+    own_in = inputs[0]
+    normed_one_all = norm_parts(own_in.astype(f32))[0].astype(bf16)
+    frame0 = rel_rows(normed_one_all)
+    first = [frame0[:quarter]]
+    for _ in range(SEQ - 1):
+        first.append(shift(first[-1], 1))
+    frames = [frame0] + [gather_tensor(first[k]) for k in range(1, SEQ)]
+
+    w_three = jnp.stack([w_query, w_key, w_value], axis=1).reshape(part, 3, heads, HEAD_DIM)
+    w_three = (w_three.astype(f32) * first_gain.astype(f32)[:, None, None, None]).astype(bf16)
+    w_three = w_three.transpose(2, 0, 1, 3).reshape(heads, part, 3 * HEAD_DIM)
+    mine = [dyn(w_three, z)] + [shift(dyn(w_three, lax.rem(z + k, SEQ)), k) for k in range(1, SEQ)]
+    mine = jnp.stack(mine)
+    both = jnp.concatenate([mine, swap_dp(mine)], axis=0)
+    w_head = jnp.concatenate([dyn(both, (dp ^ (c // SEQ)) * SEQ + lax.rem(z - c % SEQ + SEQ, SEQ)) for c in range(2 * SEQ)], axis=0)
+
+    out_mine, out_other = gather_blocks(w_out)
+    out_rel = jnp.concatenate(out_mine + out_other, axis=1)
+    w_up_scaled = (w_up.astype(f32) * second_gain.astype(f32)[:, None]).astype(bf16)
+    up_mine, up_other = gather_blocks(w_up_scaled)
+    up_rel = jnp.concatenate(up_mine + up_other, axis=0)
+    down_mine, down_other = gather_blocks(w_down)
+    down_rel = jnp.concatenate(down_mine + down_other, axis=1)
+
+    qkv = [mm(frame, w_head) for frame in frames]
+    query, key, value = (jnp.stack([one[:, n * HEAD_DIM : (n + 1) * HEAD_DIM] for one in qkv]) for n in range(3))
+    place = z.reshape(1)
+    valid = frame_mask[0]
+    attended_f, lse = attend(place, valid, query, key, value)
+    attended_low = attended_f.astype(bf16)
+    came = jnp.stack([attended_low[0]] + [shift(attended_low[k], -k) for k in range(1, SEQ)])
+    attended = jnp.concatenate([dyn(came, lax.rem(h - z + SEQ, SEQ)) for h in range(heads)], axis=1)
+
+    own_rel = rel_cols(lax.dynamic_slice_in_dim(own_in, t * quarter, quarter, 0)).astype(f32)
+    resid_mid = own_rel + scatter_tensor(mm(attended, out_rel))
+    normed_two, rate_two = norm_parts(resid_mid)
+    second_in = gather_tensor(normed_two.astype(bf16))
+
+    cot_rel = rel_cols(rel_rows(cotangent[0]))
+    up_pre = mm(second_in, up_rel, out=f32)
+    cdf = 0.5 * (1.0 + lax.erf(up_pre * (0.5**0.5)))
+    up_act = (up_pre * cdf).astype(bf16)
+    slope = cdf + up_pre * jnp.exp(-0.5 * up_pre * up_pre) * ((2.0 * jnp.pi) ** -0.5)
+    grad_down = mm(up_act, cot_rel, ((0,), (0,)))
+    d_up = (mm(cot_rel, down_rel, ((1,), (1,)), f32) * slope).astype(bf16)
+    result = resid_mid + scatter_tensor(mm(up_act, down_rel))
+    result = can_rows(gather_tensor(can_cols(result.astype(bf16))))[None]
+    grad_up = mm(second_in, d_up, ((0,), (0,)))
+    d_normed_two = scatter_tensor(mm(d_up, up_rel, ((1,), (1,))))
+    cot_own = cot_rel[:quarter].astype(f32)
+    d_mid = cot_own + norm_back(normed_two, rate_two, d_normed_two)
+    d_mix = gather_tensor(d_mid.astype(bf16))
+    grad_out = mm(attended, d_mix, ((0,), (0,)))
+    d_attended = mm(d_mix, out_rel, ((1,), (1,)))
+    d_heads = jnp.stack([d_attended[:, h * HEAD_DIM : (h + 1) * HEAD_DIM] for h in range(heads)])
+    d_out = jnp.stack([dyn(d_heads, z)] + [shift(dyn(d_heads, lax.rem(z + k, SEQ)), k) for k in range(1, SEQ)])
+
+    d_three = attend_back(place, valid, query, key, value, attended_f, lse, d_out)
+    whole = jnp.concatenate(frames, axis=0)
+    grad_head = mm(whole, d_three.reshape(SEQ * rows, 3 * HEAD_DIM), ((0,), (0,)))
+    grad_head = grad_head.reshape(2, SEQ * part, 3 * HEAD_DIM)
+    grad_rows = dyn(grad_head, dp).astype(f32) + swap_dp(dyn(grad_head, 1 - dp)).astype(f32)
+    grad_rows = grad_rows.astype(bf16).reshape(SEQ, part, 3 * HEAD_DIM)
+    arrived = jnp.stack([dyn(grad_rows, z)] + [shift(dyn(grad_rows, lax.rem(z + k, SEQ)), k) for k in range(1, SEQ)])
+    by_head = [dyn(arrived, lax.rem(z - h + SEQ, SEQ)).astype(f32) for h in range(heads)]
+    gain_one = first_gain.astype(f32)[:, None]
+    raw = [jnp.concatenate([one[:, n * HEAD_DIM : (n + 1) * HEAD_DIM] for one in by_head], axis=1) for n in range(3)]
+    d_gain_one = sum(jnp.sum(weight.astype(f32) * one, axis=1) for weight, one in zip((w_query, w_key, w_value), raw))
+
+    running = None
+    for k in (1, 2, 3, 0):
+        total = scatter_tensor(mm(d_three[k], w_head, ((1,), (1,))))
+        if running is not None:
+            total = total + running.astype(f32)
+        if k:
+            running = shift(total.astype(bf16), 1)
+    own_quarter = lax.dynamic_slice_in_dim(own_in, t * quarter, quarter, 0).astype(f32)
+    normed_one, rate_one = norm_parts(own_quarter)
+    d_in = can_cols(d_mid) + norm_back(normed_one, rate_one, total)
+    grad_inputs = can_rows(gather_tensor(d_in.astype(bf16)))[None]
+
+    down_sum = scatter_blocks([grad_down[:, b * part : (b + 1) * part] for b in range(2 * SEQ)])
+    up_raw = scatter_blocks([grad_up[b * part : (b + 1) * part] for b in range(2 * SEQ)])
+    out_sum = scatter_blocks([grad_out[:, b * part : (b + 1) * part] for b in range(2 * SEQ)])
+    d_gain_two = jnp.sum(w_up.astype(f32) * up_raw, axis=1)
+    gains = jnp.stack([d_gain_one, d_gain_two])
+    gains = gains + swap_core(gains)
+    gains = gains + swap_chip(gains)
+    return (
+        result,
+        grad_inputs,
+        gains[0],
+        raw[0] * gain_one,
+        raw[1] * gain_one,
+        raw[2] * gain_one,
+        out_sum,
+        gains[1],
+        up_raw * second_gain.astype(f32)[:, None],
+        down_sum,
+    )
+
+
+SEQ = 4
+
+
 def solution(mesh):
     placed = (
         P("dp", "seq", None),
@@ -267,8 +584,10 @@
         P("dp", None),
         P("dp", "seq", None),
     )
+    sizes = dict(mesh.shape)
+    spread = sizes == {"dp": 2, "seq": SEQ, "tensor": 4}
     return jax.shard_map(
-        local,
+        local_fast if spread else local,
         mesh=mesh,
         in_specs=placed,
         out_specs=(

time: 1620 us -> 868 us (0.54)
  waiting for transfers between devices: 1220 us -> 572 us
  matrix products: 209 us -> 80.7 us
  starting transfers between devices: 1.48 us -> 73.8 us
  blocking collectives: 62.5 us -> 0 us
  Pallas kernels: 0 us -> 26.3 us
    ppermute x0 -> x92, waiting for transfers between devices: none -> 572 us  [the longest x36 258 us: shift(): return lax.ppermute(values, 'seq', [(i, (i + k) % SEQ) for i in range(SEQ)])]
    reduce_scatter x7 -> x0, waiting for transfers between devices: 553 us -> none  [the longest x1 150 us: local(): lax.psum_scatter(grad_up.astype(jnp.bfloat16), ('dp', 'seq'), scatter_dim...]
    all_gather x8 -> x0, waiting for transfers between devices: 462 us -> none  [the longest x1 123 us: local(): lax.all_gather(w_up, ('dp', 'seq'), axis=0, tiled=True)]
    psum x3 -> x0, waiting for transfers between devices: 196 us -> none  [heads_total(): return lax.psum(values.astype(jnp.bfloat16), 'tensor').astype(jnp.float32)]
    dot_general x34 -> x18, matrix products: 209 us -> 80.7 us  [mm(): lax.dot_general(left, right, (dims, ((), ())), preferred_element_type=jnp...]
    ppermute x0 -> x92, starting transfers between devices: none -> 73.8 us  [the longest x36 30.7 us: shift(): return lax.ppermute(values, 'seq', [(i, (i + k) % SEQ) for i in range(SEQ)])]
    all_gather x2 -> x0, blocking collectives: 40 us -> none  [the longest x1 22.3 us: local(): lax.all_gather(first_gain, ('dp', 'seq'), axis=0, tiled=True)]
    unnamed x85 -> x171, local copies, waits for them, and re-layouts: 17.2 us -> 47.1 us
  transfers between devices with their start and end apart: 18 -> 92, of which waited for: 18 -> 38; matrix products, arithmetic and copies ran while one was open for 12% -> 16% of each run, Pallas kernels for 0% -> 3%
where the time goes in v1:
time: 868 us; the launch traced here: 861 us
  waiting for transfers between devices  572 us (66%)
  matrix products  80.7 us (9%)
  starting transfers between devices  73.8 us (9%)
  local copies, waits for them, and re-layouts  61 us (7%)
  other arithmetic  43.8 us (5%)
  Pallas kernels  26.3 us (3%)
    ppermute x36, waiting for transfers between devices, shift(): return lax.ppermute(values, 'seq', [(i, (i + k) % SEQ) for i in range(SEQ)])  258 us
    ppermute x26, waiting for transfers between devices, swap_dp(): return lax.ppermute(values, 'dp', [(0, 1), (1, 0)])  223 us
    ppermute x15, waiting for transfers between devices, swap_chip(): return lax.ppermute(values, 'tensor', [(i, i ^ 2) for i in range(4)])  90.6 us
    dot_general x18, matrix products, mm(): lax.dot_general(left, right, (dims, ((), ())), preferred_element_type=jnp...  80.7 us
    unnamed x171, local copies, waits for them, and re-layouts  47.1 us
    ppermute x36, starting transfers between devices, shift(): return lax.ppermute(values, 'seq', [(i, (i + k) % SEQ) for i in range(SEQ)])  30.7 us
    ppermute x26, starting transfers between devices, swap_dp(): return lax.ppermute(values, 'dp', [(0, 1), (1, 0)])  28.8 us
  transfers between devices with their start and end apart: 92, of which 38 were waited for; matrix products, arithmetic and copies ran while one was open for 16% of the time, Pallas kernels for 3%

profile of v1, /device:TPU:0, one launch (start us, length us, event | category | flops | bytes accessed | tf_op | source)
XLA Modules:
  0.0 860.7 jit_solution(1797499831923812151)
XLA Ops:
  42.4 39.8 %collective-permute-done.17 = bf16[512,256]{1,0:T(8,128)(2,1)S(1)} collective-permute-done((bf16[512,256]{1,0:T(8,128)(2,1)}, bf16[512,256]{1,0:T(8,128)(2,1)S(1)}, u32[]{:S(2)}, u32[]{:S(2)}) %collective-permute-start.17) | collective-permute-done | bytes 262176 | tf_op jit(solution)/shard_map/ppermute | solution.py:261
  100.2 28.2 %collective-permute-done.7 = bf16[160,2048]{1,0:T(8,128)(2,1)S(1)} collective-permute-done((bf16[160,2048]{1,0:T(8,128)(2,1)S(1)}, bf16[160,2048]{1,0:T(8,128)(2,1)S(1)}, u32[]{:S(2)}, u32[]{:S(2)}) %collective-permute-start.7) | collective-permute-done | bytes 655392 | tf_op jit(solution)/shard_map/ppermute | solution.py:261
  162.5 12.6 %shard_map.186 = (f32[4,640,128]{2,1,0:T(8,128)S(1)}, f32[4,1,640]{2,1,0:T(1,128)S(1)}) custom-call(s32[1]{0:T(128)} %bitcast.8.place_ref, s32[4]{0:T(128)S(1)} %bitcast.225, bf16[4,640,128]{2,1,0:T(8,128)(2,1)S(1)} %get-tuple-element.146.q_ref, bf16[4,640,128]{2,1,0:T(8,128)(2,1)S(1)} %get-tuple-element.147.k_ref, ...), custom_call_target="tpu_custom_call" | custom-call | flops 4194304000 | bytes 1966080 | tf_op jit(solution)/shard_map/pallas_call | solution.py:353
  186.0 19.3 %collective-permute-done.15 = bf16[640,128]{1,0:T(8,128)(2,1)S(1)} collective-permute-done((bf16[640,128]{1,0:T(8,128)(2,1)S(1)}, bf16[640,128]{1,0:T(8,128)(2,1)S(1)}, u32[]{:S(2)}, u32[]{:S(2)}) %collective-permute-start.15) | collective-permute-done | bytes 163872 | tf_op jit(solution)/shard_map/ppermute | solution.py:261
  219.0 17.8 %collective-permute-done.36 = bf16[2048,256]{1,0:T(8,128)(2,1)S(1)} collective-permute-done((bf16[2048,256]{1,0:T(8,128)(2,1)S(1)}, bf16[2048,256]{1,0:T(8,128)(2,1)S(1)}, u32[]{:S(2)}, u32[]{:S(2)}) %collective-permute-start.36) | collective-permute-done | bytes 1048608 | tf_op jit(solution)/shard_map/ppermute | solution.py:261
  248.4 40.6 %collective-permute-done.39 = bf16[2048,256]{1,0:T(8,128)(2,1)S(1)} collective-permute-done((bf16[2048,256]{1,0:T(8,128)(2,1)S(1)}, bf16[2048,256]{1,0:T(8,128)(2,1)S(1)}, u32[]{:S(2)}, u32[]{:S(2)}) %collective-permute-start.39) | collective-permute-done | bytes 1048608 | tf_op jit(solution)/shard_map/ppermute | solution.py:265
  299.3 16.2 %collective-permute-done.32 = bf16[256,2048]{0,1:T(8,128)(2,1)S(1)} collective-permute-done((bf16[256,2048]{0,1:T(8,128)(2,1)S(1)}, bf16[256,2048]{0,1:T(8,128)(2,1)S(1)}, u32[]{:S(2)}, u32[]{:S(2)}) %collective-permute-start.32) | collective-permute-done | bytes 1048608 | tf_op jit(solution)/shard_map/ppermute | solution.py:265
  321.1 16.8 %collective-permute-done.40 = bf16[2048,256]{1,0:T(8,128)(2,1)S(1)} collective-permute-done((bf16[2048,256]{1,0:T(8,128)(2,1)S(1)}, bf16[2048,256]{1,0:T(8,128)(2,1)S(1)}, u32[]{:S(2)}, u32[]{:S(2)}) %collective-permute-start.40) | collective-permute-done | bytes 1048608 | tf_op jit(solution)/shard_map/ppermute | solution.py:265
  339.1 15.8 %collective-permute-done.33 = bf16[256,2048]{0,1:T(8,128)(2,1)S(1)} collective-permute-done((bf16[256,2048]{0,1:T(8,128)(2,1)S(1)}, bf16[256,2048]{0,1:T(8,128)(2,1)S(1)}, u32[]{:S(2)}, u32[]{:S(2)}) %collective-permute-start.33) | collective-permute-done | bytes 1048608 | tf_op jit(solution)/shard_map/ppermute | solution.py:265
  421.0 11.6 %collective-permute-done.72 = bf16[256,2048]{0,1:T(8,128)(2,1)S(1)} collective-permute-done((bf16[256,2048]{0,1:T(8,128)(2,1)S(1)}, bf16[256,2048]{0,1:T(8,128)(2,1)S(1)}, u32[]{:S(2)}, u32[]{:S(2)}) %collective-permute-start.72) | collective-permute-done | bytes 1048608 | tf_op jit(solution)/shard_map/ppermute | solution.py:265
  436.7 63.3 %collective-permute-done.88 = bf16[2048,256]{1,0:T(8,128)(2,1)S(1)} collective-permute-done((bf16[2048,256]{1,0:T(8,128)(2,1)S(1)}, bf16[2048,256]{1,0:T(8,128)(2,1)S(1)}, u32[]{:S(2)}, u32[]{:S(2)}) %collective-permute-start.88) | collective-permute-done | bytes 1048608 | tf_op jit(solution)/shard_map/ppermute | solution.py:265
  501.4 14.4 %collective-permute-done.46 = bf16[160,2048]{1,0:T(8,128)(2,1)S(1)} collective-permute-done((bf16[160,2048]{1,0:T(8,128)(2,1)S(1)}, bf16[160,2048]{1,0:T(8,128)(2,1)S(1)}, u32[]{:S(2)}, u32[]{:S(2)}) %collective-permute-start.46) | collective-permute-done | bytes 655392 | tf_op jit(solution)/shard_map/ppermute | solution.py:269
  516.8 14.1 %collective-permute-done.42 = bf16[160,2048]{1,0:T(8,128)(2,1)S(1)} collective-permute-done((bf16[160,2048]{1,0:T(8,128)(2,1)S(1)}, bf16[160,2048]{1,0:T(8,128)(2,1)S(1)}, u32[]{:S(2)}, u32[]{:S(2)}) %collective-permute-start.42) | collective-permute-done | bytes 655392 | tf_op jit(solution)/shard_map/ppermute | solution.py:269
  538.4 16.7 %collective-permute-done.89 = bf16[2048,256]{1,0:T(8,128)(2,1)S(1)} collective-permute-done((bf16[2048,256]{1,0:T(8,128)(2,1)S(1)}, bf16[2048,256]{1,0:T(8,128)(2,1)S(1)}, u32[]{:S(2)}, u32[]{:S(2)}) %collective-permute-start.89) | collective-permute-done | bytes 1048608 | tf_op jit(solution)/shard_map/ppermute | solution.py:261
  563.3 19.7 %collective-permute-done.74 = bf16[256,2048]{0,1:T(8,128)(2,1)S(1)} collective-permute-done((bf16[256,2048]{0,1:T(8,128)(2,1)S(1)}, bf16[256,2048]{0,1:T(8,128)(2,1)S(1)}, u32[]{:S(2)}, u32[]{:S(2)}) %collective-permute-start.74) | collective-permute-done | bytes 1048608 | tf_op jit(solution)/shard_map/ppermute | solution.py:261
  585.6 20.1 %collective-permute-done.90 = bf16[2048,256]{1,0:T(8,128)(2,1)S(1)} collective-permute-done((bf16[2048,256]{1,0:T(8,128)(2,1)S(1)}, bf16[2048,256]{1,0:T(8,128)(2,1)S(1)}, u32[]{:S(2)}, u32[]{:S(2)}) %collective-permute-start.90) | collective-permute-done | bytes 1048608 | tf_op jit(solution)/shard_map/ppermute | solution.py:261
  616.2 10.3 %collective-permute-done.51 = bf16[640,128]{1,0:T(8,128)(2,1)S(1)} collective-permute-done((bf16[640,128]{1,0:T(8,128)(2,1)S(1)}, bf16[640,128]{1,0:T(8,128)(2,1)S(1)}, u32[]{:S(2)}, u32[]{:S(2)}) %collective-permute-start.51) | collective-permute-done | bytes 163872 | tf_op jit(solution)/shard_map/ppermute | solution.py:261
  639.1 13.8 %shard_map.187 = bf16[4,640,384]{2,1,0:T(8,128)(2,1)S(1)} custom-call(s32[1]{0:T(128)} %bitcast.8.place_ref, s32[4]{0:T(128)S(1)} %bitcast.226, bf16[4,640,128]{2,1,0:T(8,128)(2,1)S(1)} %get-tuple-element.146.q_ref, bf16[4,640,128]{2,1,0:T(8,128)(2,1)S(1)} %get-tuple-element.147.k_ref, bf16[4,640,128]{2,1,0:T(8,128)(2,1)S(1)} %pad_maximum_fusion.20.v_ref, ...), custom_call_target="tpu_custom_call" | custom-call | flops 10485760000 | bytes 3932160 | tf_op jit(solution)/shard_map/pallas_call | solution.py:405
  677.3 41.6 %collective-permute-done.79 = bf16[512,256]{1,0:T(8,128)(2,1)S(1)} collective-permute-done((bf16[512,256]{1,0:T(8,128)(2,1)S(1)}, bf16[512,256]{1,0:T(8,128)(2,1)S(1)}, u32[]{:S(2)}, u32[]{:S(2)}) %collective-permute-start.79) | collective-permute-done | bytes 262176 | tf_op jit(solution)/shard_map/ppermute | solution.py:265
  729.9 33.5 %collective-permute-done.67 = bf16[256,384]{1,0:T(8,128)(2,1)S(1)} collective-permute-done((bf16[256,384]{1,0:T(8,128)(2,1)S(1)}, bf16[256,384]{1,0:T(8,128)(2,1)S(1)}, u32[]{:S(2)}, u32[]{:S(2)}) %collective-permute-start.67) | collective-permute-done | bytes 196640 | tf_op jit(solution)/shard_map/ppermute | solution.py:261
  766.2 14.7 %collective-permute-done.59 = bf16[160,2048]{1,0:T(8,128)(2,1)S(1)} collective-permute-done((bf16[160,2048]{1,0:T(8,128)(2,1)S(1)}, bf16[160,2048]{1,0:T(8,128)(2,1)S(1)}, u32[]{:S(2)}, u32[]{:S(2)}) %collective-permute-start.59) | collective-permute-done | bytes 655392 | tf_op jit(solution)/shard_map/ppermute | solution.py:269
  782.0 12.6 %collective-permute-done.57 = bf16[160,2048]{1,0:T(8,128)(2,1)S(1)} collective-permute-done((bf16[160,2048]{1,0:T(8,128)(2,1)S(1)}, bf16[160,2048]{1,0:T(8,128)(2,1)S(1)}, u32[]{:S(2)}, u32[]{:S(2)}) %collective-permute-start.57) | collective-permute-done | bytes 655392 | tf_op jit(solution)/shard_map/ppermute | solution.py:269
  800.3 10.6 %collective-permute-done.55 = bf16[160,2048]{1,0:T(8,128)(2,1)S(1)} collective-permute-done((bf16[160,2048]{1,0:T(8,128)(2,1)S(1)}, bf16[160,2048]{1,0:T(8,128)(2,1)S(1)}, u32[]{:S(2)}, u32[]{:S(2)}) %collective-permute-start.55) | collective-permute-done | bytes 655392 | tf_op jit(solution)/shard_map/ppermute | solution.py:269
  816.6 9.8 %collective-permute-done.53 = bf16[160,2048]{1,0:T(8,128)(2,1)S(1)} collective-permute-done((bf16[160,2048]{1,0:T(8,128)(2,1)S(1)}, bf16[160,2048]{1,0:T(8,128)(2,1)S(1)}, u32[]{:S(2)}, u32[]{:S(2)}) %collective-permute-start.53) | collective-permute-done | bytes 655392 | tf_op jit(solution)/shard_map/ppermute | solution.py:269
  (473 shorter events, 343.7 us)
Async XLA Ops:
  3.7 87.2 %collective-permute-start.19 = (bf16[512,256]{1,0:T(8,128)(2,1)}, bf16[512,256]{1,0:T(8,128)(2,1)}, u32[]{:S(2)}, u32[]{:S(2)}) collective-permute-start(bf16[512,256]{1,0:T(8,128)(2,1)} %param.16), channel_id=1, source_target_pairs={{0,16},{16,0},{1,17},{17,1},{2,18},{18,2},{3,19},{19,3},{4,20},{20... | collective-permute-start | bytes 786440 | tf_op jit(solution)/shard_map/ppermute | solution.py:265
  37.2 94.5 %collective-permute-start.34 = (bf16[2048,256]{1,0:T(8,128)(2,1)S(1)}, bf16[2048,256]{1,0:T(8,128)(2,1)S(1)}, u32[]{:S(2)}, u32[]{:S(2)}) collective-permute-start(bf16[2048,256]{1,0:T(8,128)(2,1)S(1)} %copy-done.14), channel_id=1, source_target_pairs={{0,4},{4,8},{8,12},{12,0},{1,5},{5,9},{9,13},{13,1},{2,6},{6,10},{... | collective-permute-start | bytes 3145736 | tf_op jit(solution)/shard_map/ppermute | solution.py:261
  38.5 59.7 %collective-permute-start.3 = (bf16[4,256,384]{1,2,0:T(8,128)(2,1)S(1)}, bf16[4,256,384]{1,2,0:T(8,128)(2,1)S(1)}, u32[]{:S(2)}, u32[]{:S(2)}) collective-permute-start(bf16[4,256,384]{1,2,0:T(8,128)(2,1)S(1)} %pad_maximum_fusion.16), channel_id=1, source_target_pairs={{0,16},{16,0},{1,17},{17,1},{2,18},{18,2},{3,19},{19,3},{4,20},{20... | collective-permute-start | bytes 2359304 | tf_op jit(solution)/shard_map/ppermute | solution.py:265
  90.9 54.2 %collective-permute-start.27 = (bf16[256,2048]{0,1:T(8,128)(2,1)S(1)}, bf16[256,2048]{0,1:T(8,128)(2,1)S(1)}, u32[]{:S(2)}, u32[]{:S(2)}) collective-permute-start(bf16[256,2048]{0,1:T(8,128)(2,1)S(1)} %get-tuple-element.51), channel_id=1, source_target_pairs={{0,4},{4,8},{8,12},{12,0},{1,5},{5,9},{9,13},{13,1},{2,6},{6,10},{... | collective-permute-start | bytes 3145736 | tf_op jit(solution)/shard_map/ppermute | solution.py:261
  130.0 108.5 %collective-permute-start.37 = (bf16[2048,256]{1,0:T(8,128)(2,1)S(1)}, bf16[2048,256]{1,0:T(8,128)(2,1)S(1)}, u32[]{:S(2)}, u32[]{:S(2)}) collective-permute-start(bf16[2048,256]{1,0:T(8,128)(2,1)S(1)} %copy-done.14), channel_id=1, source_target_pairs={{0,16},{16,0},{1,17},{17,1},{2,18},{18,2},{3,19},{19,3},{4,20},{20... | collective-permute-start | bytes 3145736 | tf_op jit(solution)/shard_map/ppermute | solution.py:265
  156.3 58.4 %collective-permute-start.28 = (bf16[256,2048]{0,1:T(8,128)(2,1)S(1)}, bf16[256,2048]{0,1:T(8,128)(2,1)S(1)}, u32[]{:S(2)}, u32[]{:S(2)}) collective-permute-start(bf16[256,2048]{0,1:T(8,128)(2,1)S(1)} %collective-permute-done.27), channel_id=1, source_target_pairs={{0,4},{4,8},{8,12},{12,0},{1,5},{5,9},{9,13},{13,1},{2,6},{6,10},{... | collective-permute-start | bytes 3145736 | tf_op jit(solution)/shard_map/ppermute | solution.py:261
  205.3 91.2 %collective-permute-start.30 = (bf16[256,2048]{0,1:T(8,128)(2,1)S(1)}, bf16[256,2048]{0,1:T(8,128)(2,1)S(1)}, u32[]{:S(2)}, u32[]{:S(2)}) collective-permute-start(bf16[256,2048]{0,1:T(8,128)(2,1)S(1)} %get-tuple-element.51), channel_id=1, source_target_pairs={{0,16},{16,0},{1,17},{17,1},{2,18},{18,2},{3,19},{19,3},{4,20},{20... | collective-permute-start | bytes 3145736 | tf_op jit(solution)/shard_map/ppermute | solution.py:265
  236.8 61.4 %collective-permute-start.31 = (bf16[256,2048]{0,1:T(8,128)(2,1)S(1)}, bf16[256,2048]{0,1:T(8,128)(2,1)S(1)}, u32[]{:S(2)}, u32[]{:S(2)}) collective-permute-start(bf16[256,2048]{0,1:T(8,128)(2,1)S(1)} %collective-permute-done.27), channel_id=1, source_target_pairs={{0,16},{16,0},{1,17},{17,1},{2,18},{18,2},{3,19},{19,3},{4,20},{20... | collective-permute-start | bytes 3145736 | tf_op jit(solution)/shard_map/ppermute | solution.py:265
  238.5 50.5 %collective-permute-start.39 = (bf16[2048,256]{1,0:T(8,128)(2,1)S(1)}, bf16[2048,256]{1,0:T(8,128)(2,1)S(1)}, u32[]{:S(2)}, u32[]{:S(2)}) collective-permute-start(bf16[2048,256]{1,0:T(8,128)(2,1)S(1)} %collective-permute-done.35), channel_id=1, source_target_pairs={{0,16},{16,0},{1,17},{17,1},{2,18},{18,2},{3,19},{19,3},{4,20},{20... | collective-permute-start | bytes 3145736 | tf_op jit(solution)/shard_map/ppermute | solution.py:265
  241.0 51.5 %collective-permute-start.29 = (bf16[256,2048]{0,1:T(8,128)(2,1)S(1)}, bf16[256,2048]{0,1:T(8,128)(2,1)S(1)}, u32[]{:S(2)}, u32[]{:S(2)}) collective-permute-start(bf16[256,2048]{0,1:T(8,128)(2,1)S(1)} %collective-permute-done.28), channel_id=1, source_target_pairs={{0,4},{4,8},{8,12},{12,0},{1,5},{5,9},{9,13},{13,1},{2,6},{6,10},{... | collective-permute-start | bytes 3145736 | tf_op jit(solution)/shard_map/ppermute | solution.py:261
  293.6 61.3 %collective-permute-start.33 = (bf16[256,2048]{0,1:T(8,128)(2,1)S(1)}, bf16[256,2048]{0,1:T(8,128)(2,1)S(1)}, u32[]{:S(2)}, u32[]{:S(2)}) collective-permute-start(bf16[256,2048]{0,1:T(8,128)(2,1)S(1)} %collective-permute-done.29), channel_id=1, source_target_pairs={{0,16},{16,0},{1,17},{17,1},{2,18},{18,2},{3,19},{19,3},{4,20},{20... | collective-permute-start | bytes 3145736 | tf_op jit(solution)/shard_map/ppermute | solution.py:265
  417.1 83.7 %collective-permute-start.41 = (bf16[320,2048]{1,0:T(8,128)(2,1)S(1)}, bf16[320,2048]{1,0:T(8,128)(2,1)S(1)}, u32[]{:S(2)}, u32[]{:S(2)}) collective-permute-start(bf16[320,2048]{1,0:T(8,128)(2,1)S(1)} %slice.392), channel_id=1, source_target_pairs={{0,1},{1,0},{2,3},{3,2},{4,5},{5,4},{6,7},{7,6},{8,9},{9,8},{10,11... | collective-permute-start | bytes 3932168 | tf_op jit(solution)/shard_map/ppermute | solution.py:273
  417.3 115.8 %collective-permute-start.71 = (bf16[256,2048]{0,1:T(8,128)(2,1)S(1)}, bf16[256,2048]{0,1:T(8,128)(2,1)S(1)}, u32[]{:S(2)}, u32[]{:S(2)}) collective-permute-start(bf16[256,2048]{0,1:T(8,128)(2,1)S(1)} %get-tuple-element.62), channel_id=1, source_target_pairs={{0,16},{16,0},{1,17},{17,1},{2,18},{18,2},{3,19},{19,3},{4,20},{20... | collective-permute-start | bytes 3145736 | tf_op jit(solution)/shard_map/ppermute | solution.py:265
  417.9 144.8 %collective-permute-start.70 = (bf16[256,2048]{0,1:T(8,128)(2,1)S(1)}, bf16[256,2048]{0,1:T(8,128)(2,1)S(1)}, u32[]{:S(2)}, u32[]{:S(2)}) collective-permute-start(bf16[256,2048]{0,1:T(8,128)(2,1)S(1)} %get-tuple-element.63), channel_id=1, source_target_pairs={{0,16},{16,0},{1,17},{17,1},{2,18},{18,2},{3,19},{19,3},{4,20},{20... | collective-permute-start | bytes 3145736 | tf_op jit(solution)/shard_map/ppermute | solution.py:265
  432.5 67.4 %collective-permute-start.88 = (bf16[2048,256]{1,0:T(8,128)(2,1)S(1)}, bf16[2048,256]{1,0:T(8,128)(2,1)S(1)}, u32[]{:S(2)}, u32[]{:S(2)}) collective-permute-start(bf16[2048,256]{1,0:T(8,128)(2,1)S(1)} %get-tuple-element.57), channel_id=1, source_target_pairs={{0,16},{16,0},{1,17},{17,1},{2,18},{18,2},{3,19},{19,3},{4,20},{20... | collective-permute-start | bytes 3145736 | tf_op jit(solution)/shard_map/ppermute | solution.py:265
  435.5 101.3 %collective-permute-start.87 = (bf16[2048,256]{1,0:T(8,128)(2,1)}, bf16[2048,256]{1,0:T(8,128)(2,1)S(1)}, u32[]{:S(2)}, u32[]{:S(2)}) collective-permute-start(bf16[2048,256]{1,0:T(8,128)(2,1)} %get-tuple-element.58), channel_id=1, source_target_pairs={{0,16},{16,0},{1,17},{17,1},{2,18},{18,2},{3,19},{19,3},{4,20},{20... | collective-permute-start | bytes 3145736 | tf_op jit(solution)/shard_map/ppermute | solution.py:265
  533.2 52.5 %collective-permute-start.86 = (bf16[2048,256]{1,0:T(8,128)(2,1)S(1)}, bf16[2048,256]{1,0:T(8,128)(2,1)S(1)}, u32[]{:S(2)}, u32[]{:S(2)}) collective-permute-start(bf16[2048,256]{1,0:T(8,128)(2,1)S(1)} %get-tuple-element.59), channel_id=1, source_target_pairs={{0,16},{16,0},{1,17},{17,1},{2,18},{18,2},{3,19},{19,3},{4,20},{20... | collective-permute-start | bytes 3145736 | tf_op jit(solution)/shard_map/ppermute | solution.py:265
  555.6 50.1 %collective-permute-start.90 = (bf16[2048,256]{1,0:T(8,128)(2,1)S(1)}, bf16[2048,256]{1,0:T(8,128)(2,1)S(1)}, u32[]{:S(2)}, u32[]{:S(2)}) collective-permute-start(bf16[2048,256]{1,0:T(8,128)(2,1)S(1)} %add_convert_fusion.1), channel_id=1, source_target_pairs={{0,4},{4,8},{8,12},{12,0},{1,5},{5,9},{9,13},{13,1},{2,6},{6,10},{... | collective-permute-start | bytes 3145736 | tf_op jit(solution)/shard_map/ppermute | solution.py:261
  562.7 111.3 %collective-permute-start.69 = (bf16[256,2048]{0,1:T(8,128)(2,1)}, bf16[256,2048]{0,1:T(8,128)(2,1)}, u32[]{:S(2)}, u32[]{:S(2)}) collective-permute-start(bf16[256,2048]{0,1:T(8,128)(2,1)} %get-tuple-element.60), channel_id=1, source_target_pairs={{0,16},{16,0},{1,17},{17,1},{2,18},{18,2},{3,19},{19,3},{4,20},{20... | collective-permute-start | bytes 3145736 | tf_op jit(solution)/shard_map/ppermute | solution.py:265
  585.6 89.2 %collective-permute-start.75 = (bf16[256,2048]{0,1:T(8,128)(2,1)}, bf16[256,2048]{0,1:T(8,128)(2,1)}, u32[]{:S(2)}, u32[]{:S(2)}) collective-permute-start(bf16[256,2048]{0,1:T(8,128)(2,1)} %add_convert_fusion.3), channel_id=1, source_target_pairs={{0,4},{4,8},{8,12},{12,0},{1,5},{5,9},{9,13},{13,1},{2,6},{6,10},{... | collective-permute-start | bytes 3145736 | tf_op jit(solution)/shard_map/ppermute | solution.py:261
  659.1 65.5 %collective-permute-start.58 = (bf16[320,2048]{1,0:T(8,128)(2,1)S(1)}, bf16[320,2048]{1,0:T(8,128)(2,1)S(1)}, u32[]{:S(2)}, u32[]{:S(2)}) collective-permute-start(bf16[320,2048]{1,0:T(8,128)(2,1)S(1)} %slice.421), channel_id=1, source_target_pairs={{0,1},{1,0},{2,3},{3,2},{4,5},{5,4},{6,7},{7,6},{8,9},{9,8},{10,11... | collective-permute-start | bytes 3932168 | tf_op jit(solution)/shard_map/ppermute | solution.py:273
  670.9 177.6 %collective-permute-start.85 = (bf16[2048,256]{1,0:T(8,128)(2,1)S(1)}, bf16[2048,256]{1,0:T(8,128)(2,1)S(1)}, u32[]{:S(2)}, u32[]{:S(2)}) collective-permute-start(bf16[2048,256]{1,0:T(8,128)(2,1)S(1)} %copy-done.18), channel_id=1, source_target_pairs={{0,16},{16,0},{1,17},{17,1},{2,18},{18,2},{3,19},{19,3},{4,20},{20... | collective-permute-start | bytes 3145736 | tf_op jit(solution)/shard_map/ppermute | solution.py:265
  729.9 119.1 %collective-permute-start.91 = (bf16[2048,256]{1,0:T(8,128)(2,1)S(1)}, bf16[2048,256]{1,0:T(8,128)(2,1)S(1)}, u32[]{:S(2)}, u32[]{:S(2)}) collective-permute-start(bf16[2048,256]{1,0:T(8,128)(2,1)S(1)} %copy-done.15), channel_id=1, source_target_pairs={{0,4},{4,8},{8,12},{12,0},{1,5},{5,9},{9,13},{13,1},{2,6},{6,10},{... | collective-permute-start | bytes 3145736 | tf_op jit(solution)/shard_map/ppermute | solution.py:261
  799.4 53.8 %collective-permute-start.78 = (bf16[512,256]{1,0:T(8,128)(2,1)}, bf16[512,256]{1,0:T(8,128)(2,1)}, u32[]{:S(2)}, u32[]{:S(2)}) collective-permute-start(bf16[512,256]{1,0:T(8,128)(2,1)} %get-tuple-element.76), channel_id=1, source_target_pairs={{0,16},{16,0},{1,17},{17,1},{2,18},{18,2},{3,19},{19,3},{4,20},{20... | collective-permute-start | bytes 786440 | tf_op jit(solution)/shard_map/ppermute | solution.py:265
  (116 other events, 2253.5 us)

commit v2 on v1

--- a/solution.py
+++ b/solution.py
@@ -13,6 +13,7 @@
 
 NORM_EPS = 1e-05
 MASK_FILL = -1e30
+MESH = pl.DeviceIdType.MESH
 
 
 def norm_rows(values):
@@ -312,56 +313,284 @@
     return lax.dynamic_index_in_dim(stack, index, 0, keepdims=False)
 
 
-def attend_kernel(place_ref, valid_ref, q_ref, k_ref, v_ref, out_ref, lse_ref, peak, total, acc):
-    place = place_ref[0]
+def front_kernel(
+    f0_ref, w_three_ref, w_out_ref, w_up_ref, w_down_ref, own_ref, bias_ref,
+    whole_ref, w_head_ref, qkv_ref, att_ref, lse_ref, attended_ref, out_ref, resid_ref, normed_ref, rate_ref, second_ref, up_ref, down_ref,
+    frames, w_stack, out_all, att_low, came, part_low, core_in, half_low, chip_in, second, peak, total, acc, send, recv, local_sem,
+):
+    dp, z, t = lax.axis_index("dp"), lax.axis_index("seq"), lax.axis_index("tensor")
+    other_dp, chip, core = {"dp": 1 - dp}, {"tensor": lax.rem(t + 2, 4)}, {"tensor": t + 1 - 2 * lax.rem(t, 2)}
+
+    def along(k):
+        return {"seq": lax.rem(z + k + SEQ, SEQ)}
+
+    rows, width = f0_ref.shape
+    quarter = rows // 4
+    half = rows // 2
+    part = w_out_ref.shape[1]
+    used = []
+
+    def remote(src, dst, device):
+        i = len(used)
+        copy = pltpu.make_async_remote_copy(src_ref=src, dst_ref=dst, send_sem=send.at[i], recv_sem=recv.at[i], device_id=device, device_id_type=MESH)
+        used.append(copy)
+        return copy
+
+    kept = []
+
+    def keep(src, dst):
+        copy = pltpu.make_async_copy(src, dst, local_sem.at[len(kept)])
+        kept.append(copy)
+        copy.start()
+        return copy
+
+    barrier = pltpu.get_barrier_semaphore()
+    peers = [other_dp, chip, core] + [along(k) for k in range(1, SEQ)]
+    for peer in peers:
+        pl.semaphore_signal(barrier, inc=1, device_id=peer, device_id_type=MESH)
+    pl.semaphore_wait(barrier, len(peers))
+
+    def out_at(b):
+        return out_all.at[:, pl.ds(b * part, part)]
+
+    def up_at(b):
+        return up_ref.at[pl.ds(b * part, part), :]
+
+    def down_at(b):
+        return down_ref.at[:, pl.ds(b * part, part)]
+
+    ring = along(1)
+    token = [None] + [remote(f0_ref.at[pl.ds(0, quarter), :] if k == 1 else frames.at[k - 1, pl.ds(0, quarter), :], frames.at[k, pl.ds(0, quarter), :], ring) for k in range(1, SEQ)]
+    token_chip = [None] + [remote(frames.at[k, pl.ds(0, quarter), :], frames.at[k, pl.ds(quarter, quarter), :], chip) for k in range(1, SEQ)]
+    token_core = [None] + [remote(frames.at[k, pl.ds(0, half), :], frames.at[k, pl.ds(half, half), :], core) for k in range(1, SEQ)]
+    head = [None] + [remote(w_three_ref.at[lax.rem(z + k, SEQ)], w_stack.at[k], along(k)) for k in range(1, SEQ)]
+    head_dp = remote(w_stack.at[pl.ds(0, SEQ)], w_stack.at[pl.ds(SEQ, SEQ)], other_dp)
+
+    def gather(shard, at):
+        step = [None] + [remote(shard if k == 1 else at(k - 1), at(k), ring) for k in range(1, SEQ)]
+        cross = [remote(shard if k == 0 else at(k), at(SEQ + k), other_dp) for k in range(SEQ)]
+        return step, cross
+
+    out_step, out_dp = gather(w_out_ref, out_at)
+    up_step, up_dp = gather(w_up_ref, up_at)
+    down_step, down_dp = gather(w_down_ref, down_at)
+    first_back = len(used) - 1
+    back = [None] + [remote(att_low.at[k], came.at[k], along(-k)) for k in range(1, SEQ)]
+    sum_core = remote(part_low.at[pl.ds(half, half), :], core_in, core)
+    sum_chip = remote(half_low, chip_in, chip)
+    second_chip = remote(second.at[pl.ds(0, quarter), :], second.at[pl.ds(quarter, quarter), :], chip)
+    second_core = remote(second.at[pl.ds(0, half), :], second.at[pl.ds(half, half), :], core)
+
+    def pass_on(steps, cross, k):
+        steps[k].wait_recv()
+        if k + 1 < SEQ:
+            steps[k + 1].start()
+        cross[k].start()
+
+    token[1].start()
+    for k in range(1, SEQ):
+        head[k].start()
+    up_dp[0].start()
+    out_dp[0].start()
+    own_frame = keep(f0_ref, frames.at[0])
+    own_head = keep(w_three_ref.at[z], w_stack.at[0])
+    own_out = keep(w_out_ref, out_at(0))
+    keep(w_up_ref, up_at(0))
+    keep(w_down_ref, down_at(0))
+    own_head.wait()
+    own_frame.wait()
+    token[1].wait_recv()
+    token[2].start()
+    token_chip[1].start()
+    for k in range(1, SEQ):
+        head[k].wait_recv()
+    head_dp.start()
+    token[2].wait_recv()
+    token[3].start()
+    token_chip[2].start()
+    token_chip[1].wait_recv()
+    token_core[1].start()
+    out_step[1].start()
+    up_step[1].start()
+    head_dp.wait_recv()
+    down_dp[0].start()
+    for c in range(2 * SEQ):
+        b = lax.rem(dp + c // SEQ, 2) * SEQ + lax.rem(z - c % SEQ + SEQ, SEQ)
+        w_head_ref[c * part : (c + 1) * part, :] = w_stack[b]
+
+    def project(k):
+        def piece(n, carry):
+            at = pl.ds(n * quarter, quarter)
+            qkv_ref[k, at, :] = jnp.dot(frames[k, at, :], w_head_ref[...], preferred_element_type=jnp.float32).astype(jnp.bfloat16)
+            return carry
+
+        lax.fori_loop(0, 4, piece, 0)
+
+    project(0)
+    token_core[1].wait_recv()
+    keep(frames.at[1], whole_ref.at[1])
+    project(1)
+    token_chip[2].wait_recv()
+    token_core[2].start()
+    token[3].wait_recv()
+    token_chip[3].start()
+    token_core[2].wait_recv()
+    keep(frames.at[2], whole_ref.at[2])
+    project(2)
+    pass_on(out_step, out_dp, 1)
+    token_chip[3].wait_recv()
+    token_core[3].start()
+    token_core[3].wait_recv()
+    keep(frames.at[0], whole_ref.at[0])
+    keep(frames.at[3], whole_ref.at[3])
+    project(3)
+
     scale = HEAD_DIM ** (-0.5)
 
-    def query_frame(i, carry):
-        at = lax.rem(place - i + SEQ, SEQ)
-        query = q_ref[at]
+    def query_frame(i):
+        at = lax.rem(z - i + SEQ, SEQ)
+        query = qkv_ref[at, :, 0:HEAD_DIM]
         peak[...] = jnp.full_like(peak, MASK_FILL)
         total[...] = jnp.zeros_like(total)
         acc[...] = jnp.zeros_like(acc)
 
         def key_frame(j, inner):
-            @pl.when(valid_ref[j] == 1)
-            def _():
-                here = lax.rem(place - j + SEQ, SEQ)
-                scores = lax.dot_general(k_ref[here], query, (((1,), (1,)), ((), ())), preferred_element_type=jnp.float32) * scale
-                before = peak[...]
-                after = jnp.maximum(before, jnp.max(scores, axis=0, keepdims=True))
-                terms = jnp.exp(scores - after)
-                fix = jnp.exp(before - after)
-                peak[...] = after
-                total[...] = total[...] * fix + jnp.sum(terms, axis=0, keepdims=True)
-                acc[...] = acc[...] * fix + lax.dot_general(v_ref[here], terms.astype(jnp.bfloat16), (((0,), (0,)), ((), ())), preferred_element_type=jnp.float32)
-
+            here = lax.rem(z - j + SEQ, SEQ)
+            scores = lax.dot_general(qkv_ref[here, :, HEAD_DIM : 2 * HEAD_DIM], query, (((1,), (1,)), ((), ())), preferred_element_type=jnp.float32) * scale + bias_ref[j]
+            before = peak[...]
+            after = jnp.maximum(before, jnp.max(scores, axis=0, keepdims=True))
+            terms = jnp.exp(scores - after)
+            fix = jnp.exp(before - after)
+            peak[...] = after
+            total[...] = total[...] * fix + jnp.sum(terms, axis=0, keepdims=True)
+            acc[...] = acc[...] * fix + lax.dot_general(qkv_ref[here, :, 2 * HEAD_DIM :], terms.astype(jnp.bfloat16), (((0,), (0,)), ((), ())), preferred_element_type=jnp.float32)
             return inner
 
         lax.fori_loop(0, i + 1, key_frame, 0)
-        out_ref[at] = (acc[...] / total[...]).T
+        outcome = (acc[...] / total[...]).T
+        att_ref[at] = outcome
+        att_low[at] = outcome.astype(jnp.bfloat16)
         lse_ref[at] = peak[...] + jnp.log(total[...])
-        return carry
-
-    lax.fori_loop(0, SEQ, query_frame, 0)
-
-
-def attend(place, valid, query, key, value):
-    rows = query.shape[1]
-    smem = pl.BlockSpec(memory_space=pltpu.SMEM)
-    vmem = pl.BlockSpec(memory_space=pltpu.VMEM)
+
+        @pl.when(at != 0)
+        def _():
+            pltpu.make_async_remote_copy(
+                src_ref=att_low.at[at], dst_ref=came.at[at], send_sem=send.at[first_back + at], recv_sem=recv.at[first_back + at],
+                device_id={"seq": i}, device_id_type=MESH,
+            ).start()
+
+    query_frame(0)
+    query_frame(1)
+    pass_on(out_step, out_dp, 2)
+    query_frame(2)
+    pass_on(up_step, up_dp, 1)
+    query_frame(3)
+    pass_on(out_step, out_dp, 3)
+    came[0] = att_low[0]
+    for k in range(1, SEQ):
+        back[k].wait_recv()
+    for h in range(SEQ):
+        attended_ref[:, h * HEAD_DIM : (h + 1) * HEAD_DIM] = came[lax.rem(h - z + SEQ, SEQ)]
+    own_out.wait()
+    for k in range(SEQ):
+        out_dp[k].wait_recv()
+    keep(out_all, out_ref)
+
+    def mix(start):
+        def piece(n, carry):
+            at = pl.ds(pl.multiple_of(n * 512, 512), 512)
+            part_low[pl.ds(start, half), at] = jnp.dot(attended_ref[pl.ds(start, half), :], out_all[:, at], preferred_element_type=jnp.float32).astype(jnp.bfloat16)
+            return carry
+
+        lax.fori_loop(0, width // 512, piece, 0)
+
+    mix(half)
+    sum_core.start()
+    mix(0)
+    sum_core.wait_recv()
+    half_low[...] = (part_low[quarter:half, :].astype(jnp.float32) + core_in[quarter:half, :].astype(jnp.float32)).astype(jnp.bfloat16)
+    sum_chip.start()
+    pass_on(up_step, up_dp, 2)
+    down_step[1].start()
+    sum_chip.wait_recv()
+    resid = own_ref[...] + (part_low[0:quarter, :].astype(jnp.float32) + core_in[0:quarter, :].astype(jnp.float32)) + chip_in[...].astype(jnp.float32)
+    center = resid - jnp.mean(resid, axis=1, keepdims=True)
+    rate = lax.rsqrt(jnp.mean(center * center, axis=1, keepdims=True) + NORM_EPS)
+    normed = center * rate
+    resid_ref[...] = resid
+    rate_ref[...] = rate
+    normed_ref[...] = normed
+    second[0:quarter, :] = normed.astype(jnp.bfloat16)
+    second_chip.start()
+    pass_on(up_step, up_dp, 3)
+    second_chip.wait_recv()
+    second_core.start()
+    second_core.wait_recv()
+    keep(second, second_ref)
+    for k in range(1, SEQ):
+        pass_on(down_step, down_dp, k)
+    for copy in up_dp + down_dp:
+        copy.wait_recv()
+    for copy in used:
+        copy.wait_send()
+    for copy in kept:
+        if not any(copy is done for done in (own_frame, own_head, own_out)):
+            copy.wait()
+
+
+def front(f0, w_three, w_out, w_up, w_down, own, bias):
+    rows, width = f0.shape
+    quarter, half = rows // 4, rows // 2
+    part = w_out.shape[1]
+    inner = w_out.shape[0]
+    f32, bf16 = jnp.float32, jnp.bfloat16
+    any_, vmem = pl.BlockSpec(memory_space=pl.ANY), pl.BlockSpec(memory_space=pltpu.VMEM)
+    shape = jax.ShapeDtypeStruct
+    outs = [
+        (shape((SEQ, rows, width), bf16), any_),
+        (shape((width, 3 * HEAD_DIM), bf16), vmem),
+        (shape((SEQ, rows, 3 * HEAD_DIM), bf16), vmem),
+        (shape((SEQ, rows, HEAD_DIM), f32), vmem),
+        (shape((SEQ, 1, rows), f32), vmem),
+        (shape((rows, inner), bf16), vmem),
+        (shape((inner, width), bf16), any_),
+        (shape((quarter, width), f32), vmem),
+        (shape((quarter, width), f32), vmem),
+        (shape((quarter, 1), f32), vmem),
+        (shape((rows, width), bf16), any_),
+        (shape((width, w_up.shape[1]), bf16), any_),
+        (shape((w_down.shape[0], width), bf16), any_),
+    ]
+    copies = 3 * (SEQ - 1) + SEQ + 3 * (2 * SEQ - 1) + (SEQ - 1) + 4
     return pl.pallas_call(
-        attend_kernel,
-        out_shape=(jax.ShapeDtypeStruct(query.shape, jnp.float32), jax.ShapeDtypeStruct((SEQ, 1, rows), jnp.float32)),
-        in_specs=[smem, smem, vmem, vmem, vmem],
-        out_specs=(vmem, vmem),
-        scratch_shapes=[pltpu.VMEM((1, rows), jnp.float32), pltpu.VMEM((1, rows), jnp.float32), pltpu.VMEM((HEAD_DIM, rows), jnp.float32)],
-        compiler_params=pltpu.CompilerParams(vmem_limit_bytes=40 * 2**20),
-        cost_estimate=pl.CostEstimate(flops=4 * 10 * rows * rows * HEAD_DIM * 2, bytes_accessed=6 * query.size, transcendentals=10 * rows * rows),
-    )(place, valid, query, key, value)
-
-
-def attend_back_kernel(place_ref, valid_ref, q_ref, k_ref, v_ref, out_ref, lse_ref, do_ref, grad_ref, delta, dq, dk, dv):
+        front_kernel,
+        out_shape=[o[0] for o in outs],
+        in_specs=[any_] * 5 + [vmem] * 2,
+        out_specs=[o[1] for o in outs],
+        scratch_shapes=[
+            pltpu.VMEM((SEQ, rows, width), bf16),
+            pltpu.VMEM((2 * SEQ, part, 3 * HEAD_DIM), bf16),
+            pltpu.VMEM((inner, width), bf16),
+            pltpu.VMEM((SEQ, rows, HEAD_DIM), bf16),
+            pltpu.VMEM((SEQ, rows, HEAD_DIM), bf16),
+            pltpu.VMEM((rows, width), bf16),
+            pltpu.VMEM((half, width), bf16),
+            pltpu.VMEM((quarter, width), bf16),
+            pltpu.VMEM((quarter, width), bf16),
+            pltpu.VMEM((rows, width), bf16),
+            pltpu.VMEM((1, rows), f32),
+            pltpu.VMEM((1, rows), f32),
+            pltpu.VMEM((HEAD_DIM, rows), f32),
+            pltpu.SemaphoreType.DMA((copies,)),
+            pltpu.SemaphoreType.DMA((copies,)),
+            pltpu.SemaphoreType.DMA((16,)),
+        ],
+        compiler_params=pltpu.CompilerParams(collective_id=0, has_side_effects=True, vmem_limit_bytes=56 * 2**20),
+        cost_estimate=pl.CostEstimate(flops=8 * 10**9, bytes_accessed=50 * 10**6, transcendentals=5 * 10**6),
+    )(f0, w_three, w_out, w_up, w_down, own, bias)
+
+
+def attend_back_kernel(place_ref, valid_ref, qkv_ref, out_ref, lse_ref, do_ref, grad_ref, delta, dq, dk, dv):
     place = place_ref[0]
     scale = HEAD_DIM ** (-0.5)
     dq[...] = jnp.zeros_like(dq)
@@ -377,7 +606,8 @@
         def _():
             def query_frame(i, inner):
                 at = lax.rem(place - i + SEQ, SEQ)
-                query, key, value, d_out = q_ref[at], k_ref[here], v_ref[here], do_ref[at]
+                query, key, value = qkv_ref[at, :, :HEAD_DIM], qkv_ref[here, :, HEAD_DIM : 2 * HEAD_DIM], qkv_ref[here, :, 2 * HEAD_DIM :]
+                d_out = do_ref[at]
                 scores = lax.dot_general(key, query, (((1,), (1,)), ((), ())), preferred_element_type=jnp.float32) * scale
                 prob = jnp.exp(scores - lse_ref[at])
                 d_prob = lax.dot_general(value, d_out, (((1,), (1,)), ((), ())), preferred_element_type=jnp.float32)
@@ -398,14 +628,14 @@
         grad_ref[f, :, :HEAD_DIM] = (dq[f] * scale).T.astype(jnp.bfloat16)
 
 
-def attend_back(place, valid, query, key, value, out, lse, d_out):
-    rows = query.shape[1]
+def attend_back(place, valid, qkv, out, lse, d_out):
+    rows = qkv.shape[1]
     smem = pl.BlockSpec(memory_space=pltpu.SMEM)
     vmem = pl.BlockSpec(memory_space=pltpu.VMEM)
     return pl.pallas_call(
         attend_back_kernel,
         out_shape=jax.ShapeDtypeStruct((SEQ, rows, 3 * HEAD_DIM), jnp.bfloat16),
-        in_specs=[smem, smem] + [vmem] * 6,
+        in_specs=[smem, smem] + [vmem] * 4,
         out_specs=vmem,
         scratch_shapes=[
             pltpu.VMEM((SEQ, 1, rows), jnp.float32),
@@ -414,8 +644,8 @@
             pltpu.VMEM((rows, HEAD_DIM), jnp.float32),
         ],
         compiler_params=pltpu.CompilerParams(vmem_limit_bytes=48 * 2**20),
-        cost_estimate=pl.CostEstimate(flops=10 * 10 * rows * rows * HEAD_DIM * 2, bytes_accessed=12 * query.size, transcendentals=10 * rows * rows),
-    )(place, valid, query, key, value, out, lse, d_out)
+        cost_estimate=pl.CostEstimate(flops=10 * 10 * rows * rows * HEAD_DIM * 2, bytes_accessed=5 * qkv.size, transcendentals=10 * rows * rows),
+    )(place, valid, qkv, out, lse, d_out)
 
 
 def norm_parts(values):
@@ -468,40 +698,17 @@
     own_in = inputs[0]
     normed_one_all = norm_parts(own_in.astype(f32))[0].astype(bf16)
     frame0 = rel_rows(normed_one_all)
-    first = [frame0[:quarter]]
-    for _ in range(SEQ - 1):
-        first.append(shift(first[-1], 1))
-    frames = [frame0] + [gather_tensor(first[k]) for k in range(1, SEQ)]
-
     w_three = jnp.stack([w_query, w_key, w_value], axis=1).reshape(part, 3, heads, HEAD_DIM)
     w_three = (w_three.astype(f32) * first_gain.astype(f32)[:, None, None, None]).astype(bf16)
     w_three = w_three.transpose(2, 0, 1, 3).reshape(heads, part, 3 * HEAD_DIM)
-    mine = [dyn(w_three, z)] + [shift(dyn(w_three, lax.rem(z + k, SEQ)), k) for k in range(1, SEQ)]
-    mine = jnp.stack(mine)
-    both = jnp.concatenate([mine, swap_dp(mine)], axis=0)
-    w_head = jnp.concatenate([dyn(both, (dp ^ (c // SEQ)) * SEQ + lax.rem(z - c % SEQ + SEQ, SEQ)) for c in range(2 * SEQ)], axis=0)
-
-    out_mine, out_other = gather_blocks(w_out)
-    out_rel = jnp.concatenate(out_mine + out_other, axis=1)
     w_up_scaled = (w_up.astype(f32) * second_gain.astype(f32)[:, None]).astype(bf16)
-    up_mine, up_other = gather_blocks(w_up_scaled)
-    up_rel = jnp.concatenate(up_mine + up_other, axis=0)
-    down_mine, down_other = gather_blocks(w_down)
-    down_rel = jnp.concatenate(down_mine + down_other, axis=1)
-
-    qkv = [mm(frame, w_head) for frame in frames]
-    query, key, value = (jnp.stack([one[:, n * HEAD_DIM : (n + 1) * HEAD_DIM] for one in qkv]) for n in range(3))
+    own_rel = rel_cols(lax.dynamic_slice_in_dim(own_in, t * quarter, quarter, 0)).astype(f32)
     place = z.reshape(1)
     valid = frame_mask[0]
-    attended_f, lse = attend(place, valid, query, key, value)
-    attended_low = attended_f.astype(bf16)
-    came = jnp.stack([attended_low[0]] + [shift(attended_low[k], -k) for k in range(1, SEQ)])
-    attended = jnp.concatenate([dyn(came, lax.rem(h - z + SEQ, SEQ)) for h in range(heads)], axis=1)
-
-    own_rel = rel_cols(lax.dynamic_slice_in_dim(own_in, t * quarter, quarter, 0)).astype(f32)
-    resid_mid = own_rel + scatter_tensor(mm(attended, out_rel))
-    normed_two, rate_two = norm_parts(resid_mid)
-    second_in = gather_tensor(normed_two.astype(bf16))
+    bias = jnp.broadcast_to(jnp.where(valid == 1, 0.0, MASK_FILL).astype(f32)[:, None, None], (SEQ, 1, rows))
+    whole, w_head, qkv, attended_f, lse, attended, out_rel, resid_mid, normed_two, rate_two, second_in, up_rel, down_rel = front(
+        frame0, w_three, w_out, w_up_scaled, w_down, own_rel, bias
+    )
 
     cot_rel = rel_cols(rel_rows(cotangent[0]))
     up_pre = mm(second_in, up_rel, out=f32)
@@ -522,9 +729,8 @@
     d_heads = jnp.stack([d_attended[:, h * HEAD_DIM : (h + 1) * HEAD_DIM] for h in range(heads)])
     d_out = jnp.stack([dyn(d_heads, z)] + [shift(dyn(d_heads, lax.rem(z + k, SEQ)), k) for k in range(1, SEQ)])
 
-    d_three = attend_back(place, valid, query, key, value, attended_f, lse, d_out)
-    whole = jnp.concatenate(frames, axis=0)
-    grad_head = mm(whole, d_three.reshape(SEQ * rows, 3 * HEAD_DIM), ((0,), (0,)))
+    d_three = attend_back(place, valid, qkv, attended_f, lse, d_out)
+    grad_head = mm(whole.reshape(SEQ * rows, width), d_three.reshape(SEQ * rows, 3 * HEAD_DIM), ((0,), (0,)))
     grad_head = grad_head.reshape(2, SEQ * part, 3 * HEAD_DIM)
     grad_rows = dyn(grad_head, dp).astype(f32) + swap_dp(dyn(grad_head, 1 - dp)).astype(f32)
     grad_rows = grad_rows.astype(bf16).reshape(SEQ, part, 3 * HEAD_DIM)

time: 868 us -> 820 us (0.945)
  Pallas kernels: 26.3 us -> 338 us
  waiting for transfers between devices: 572 us -> 287 us
  local copies, waits for them, and re-layouts: 61 us -> 26.9 us
  starting transfers between devices: 73.8 us -> 43.1 us
  matrix products: 80.7 us -> 66.7 us
    pallas_call x1, Pallas kernels: 12.6 us -> 324 us  [front(): pl.pallas_call(front_kernel, out_shape=[o[0] for o in outs], in_specs=[an...]
    ppermute x26 -> x13, waiting for transfers between devices: 223 us -> 78.4 us  [swap_dp(): return lax.ppermute(values, 'dp', [(0, 1), (1, 0)])]
    ppermute x36 -> x18, waiting for transfers between devices: 258 us -> 128 us  [shift(): return lax.ppermute(values, 'seq', [(i, (i + k) % SEQ) for i in range(SEQ)])]
    unnamed x171 -> x99, local copies, waits for them, and re-layouts: 47.1 us -> 11 us
    ppermute x26 -> x13, starting transfers between devices: 28.8 us -> 12.8 us  [swap_dp(): return lax.ppermute(values, 'dp', [(0, 1), (1, 0)])]
    dot_general x18 -> x13, matrix products: 80.7 us -> 66.7 us  [mm(): lax.dot_general(left, right, (dims, ((), ())), preferred_element_type=jnp...]
    ppermute x36 -> x18, starting transfers between devices: 30.7 us -> 17.6 us  [shift(): return lax.ppermute(values, 'seq', [(i, (i + k) % SEQ) for i in range(SEQ)])]
    ppermute x15 -> x10, waiting for transfers between devices: 90.6 us -> 80.4 us  [swap_chip(): return lax.ppermute(values, 'tensor', [(i, i ^ 2) for i in range(4)])]
  transfers between devices with their start and end apart: 92 -> 51, of which waited for: 38 -> 24; matrix products, arithmetic and copies ran while one was open for 16% -> 12% of each run, Pallas kernels for 3% -> 2%
where the time goes in v2:
time: 820 us; the launch traced here: 816 us
  Pallas kernels  338 us (41%)
  waiting for transfers between devices  287 us (35%)
  matrix products  66.7 us (8%)
  other arithmetic  52.4 us (6%)
  starting transfers between devices  43.1 us (5%)
  local copies, waits for them, and re-layouts  26.9 us (3%)
    pallas_call x1, Pallas kernels, front(): pl.pallas_call(front_kernel, out_shape=[o[0] for o in outs], in_specs=[an...  324 us
    ppermute x18, waiting for transfers between devices, shift(): return lax.ppermute(values, 'seq', [(i, (i + k) % SEQ) for i in range(SEQ)])  128 us
    ppermute x10, waiting for transfers between devices, swap_chip(): return lax.ppermute(values, 'tensor', [(i, i ^ 2) for i in range(4)])  80.4 us
    ppermute x13, waiting for transfers between devices, swap_dp(): return lax.ppermute(values, 'dp', [(0, 1), (1, 0)])  78.4 us
    dot_general x13, matrix products, mm(): lax.dot_general(left, right, (dims, ((), ())), preferred_element_type=jnp...  66.7 us
    ppermute x18, starting transfers between devices, shift(): return lax.ppermute(values, 'seq', [(i, (i + k) % SEQ) for i in range(SEQ)])  17.6 us
  transfers between devices with their start and end apart: 51, of which 24 were waited for; matrix products, arithmetic and copies ran while one was open for 12% of the time, Pallas kernels for 2%

profile of v2, /device:TPU:0, one launch (start us, length us, event | category | flops | bytes accessed | tf_op | source)
XLA Modules:
  0.0 815.6 jit_solution(14739063522536830528)
XLA Ops:
  22.0 324.0 %shard_map.186 = (bf16[4,640,2048]{2,1,0:T(8,128)(2,1)}, bf16[2048,384]{1,0:T(8,128)(2,1)}, bf16[4,640,384]{2,1,0:T(8,128)(2,1)}, f32[4,640,128]{2,1,0:T(8,128)}...) custom-call(bf16[640,2048]{1,0:T(8,128)(2,1)} %pad_maximum_fusion.f0, ...), custom_call_target="tpu_custom_call" | custom-call | flops 8000000000 | bytes 50000000 | tf_op jit(solution)/shard_map/pallas_call | solution.py:565
  346.0 9.2 %multiply_convert_fusion = (bf16[640,2048]{1,0:T(8,128)(2,1)S(1)}, f32[640,2048]{1,0:T(8,128)S(1)}) fusion(bf16[640,2048]{1,0:T(8,128)(2,1)} %get-tuple-element.24, bf16[2048,2048]{1,0:T(8,128)(2,1)} %get-tuple-element.25), kind=kOutput, calls=%fused_computation.16 | convolution fusion | flops 5375262720 | bytes 18874368 | tf_op jit(solution)/shard_map/dot_general | solution.py:662
  355.3 6.2 convolution_convert_fusion.3
  365.9 7.4 fusion.10
  373.3 8.0 convolution_convert_fusion.2
  384.6 7.0 convolution_convert_fusion.1
  398.5 9.3 %convolution_convert_fusion = bf16[2048,2048]{1,0:T(8,128)(2,1)} fusion(bf16[640,2048]{1,0:T(8,128)(2,1)S(1)} %get-tuple-element.110, bf16[640,2048]{1,0:T(8,128)(2,1)S(1)} %dynamic-slice_dynamic-update-slice_fusion), kind=kOutput, calls=%fused_computation.1 | convolution fusion | flops 5372903424 | bytes 13631488 | tf_op jit(solution)/shard_map/dot_general | solution.py:662
  411.7 10.8 %collective-permute-done.31 = bf16[256,2048]{1,0:T(8,128)(2,1)} collective-permute-done((bf16[256,2048]{1,0:T(8,128)(2,1)}, bf16[256,2048]{1,0:T(8,128)(2,1)}, u32[]{:S(2)}, u32[]{:S(2)}) %collective-permute-start.31) | collective-permute-done | bytes 1048608 | tf_op jit(solution)/shard_map/ppermute | solution.py:266
  428.5 61.4 %collective-permute-done.47 = bf16[2048,256]{1,0:T(8,128)(2,1)S(1)} collective-permute-done((bf16[2048,256]{1,0:T(8,128)(2,1)S(1)}, bf16[2048,256]{1,0:T(8,128)(2,1)S(1)}, u32[]{:S(2)}, u32[]{:S(2)}) %collective-permute-start.47) | collective-permute-done | bytes 1048608 | tf_op jit(solution)/shard_map/ppermute | solution.py:266
  497.7 7.5 collective-permute-done.1
  507.3 12.2 %collective-permute-done.5 = bf16[160,2048]{1,0:T(8,128)(2,1)S(1)} collective-permute-done((bf16[160,2048]{1,0:T(8,128)(2,1)S(1)}, bf16[160,2048]{1,0:T(8,128)(2,1)S(1)}, u32[]{:S(2)}, u32[]{:S(2)}) %collective-permute-start.5) | collective-permute-done | bytes 655392 | tf_op jit(solution)/shard_map/ppermute | solution.py:270
  529.6 13.5 %collective-permute-done.48 = bf16[2048,256]{1,0:T(8,128)(2,1)S(1)} collective-permute-done((bf16[2048,256]{1,0:T(8,128)(2,1)S(1)}, bf16[2048,256]{1,0:T(8,128)(2,1)S(1)}, u32[]{:S(2)}, u32[]{:S(2)}) %collective-permute-start.48) | collective-permute-done | bytes 1048608 | tf_op jit(solution)/shard_map/ppermute | solution.py:262
  553.5 17.5 %collective-permute-done.33 = bf16[256,2048]{1,0:T(8,128)(2,1)S(1)} collective-permute-done((bf16[256,2048]{1,0:T(8,128)(2,1)S(1)}, bf16[256,2048]{1,0:T(8,128)(2,1)S(1)}, u32[]{:S(2)}, u32[]{:S(2)}) %collective-permute-start.33) | collective-permute-done | bytes 1048608 | tf_op jit(solution)/shard_map/ppermute | solution.py:262
  575.6 12.7 %collective-permute-done.49 = bf16[2048,256]{1,0:T(8,128)(2,1)S(1)} collective-permute-done((bf16[2048,256]{1,0:T(8,128)(2,1)S(1)}, bf16[2048,256]{1,0:T(8,128)(2,1)S(1)}, u32[]{:S(2)}, u32[]{:S(2)}) %collective-permute-start.49) | collective-permute-done | bytes 1048608 | tf_op jit(solution)/shard_map/ppermute | solution.py:262
  599.8 26.0 %collective-permute-done.9 = bf16[640,128]{1,0:T(8,128)(2,1)S(1)} collective-permute-done((bf16[640,128]{1,0:T(8,128)(2,1)S(1)}, bf16[640,128]{1,0:T(8,128)(2,1)S(1)}, u32[]{:S(2)}, u32[]{:S(2)}) %collective-permute-start.9) | collective-permute-done | bytes 163872 | tf_op jit(solution)/shard_map/ppermute | solution.py:262
  627.7 13.6 %shard_map.187 = bf16[4,640,384]{2,1,0:T(8,128)(2,1)S(1)} custom-call(s32[1]{0:T(128)} %bitcast.21.place_ref, s32[4]{0:T(128)S(1)} %bitcast.156, bf16[4,640,384]{2,1,0:T(8,128)(2,1)S(1)} %copy-done.1, f32[4,640,128]{2,1,0:T(8,128)S(1)} %copy-done.2, f32[4,1,640]{2,1,0:T(1,128)S(1)} %copy-done.3, bf16[4,640,128]{2,1,0:T(8,128)(2,1)S(1)} %pad_maximum_fusion.12.do_ref), custom_call_target="tpu_custom_call" | custom-call | flops 10485760000 | bytes 4915200 | tf_op jit(solution)/shard_map/pallas_call | solution.py:635
  646.0 8.3 %bitcast_convert_fusion = bf16[2048,384]{1,0:T(8,128)(2,1)S(1)} fusion(bf16[4,640,2048]{2,1,0:T(8,128)(2,1)} %get-tuple-element.34, bf16[4,640,384]{2,1,0:T(8,128)(2,1)S(1)} %shard_map.187), kind=kOutput, calls=%fused_computation.24 | convolution fusion | flops 4027318272 | bytes 14024704 | tf_op jit(solution)/shard_map/dot_general | solution.py:662
  676.8 5.4 collective-permute-done.42
  683.9 13.3 %collective-permute-done.18 = bf16[160,2048]{1,0:T(8,128)(2,1)S(1)} collective-permute-done((bf16[160,2048]{1,0:T(8,128)(2,1)S(1)}, bf16[160,2048]{1,0:T(8,128)(2,1)S(1)}, u32[]{:S(2)}, u32[]{:S(2)}) %collective-permute-start.18) | collective-permute-done | bytes 655392 | tf_op jit(solution)/shard_map/ppermute | solution.py:270
  699.1 12.9 %collective-permute-done.16 = bf16[160,2048]{1,0:T(8,128)(2,1)S(1)} collective-permute-done((bf16[160,2048]{1,0:T(8,128)(2,1)S(1)}, bf16[160,2048]{1,0:T(8,128)(2,1)S(1)}, u32[]{:S(2)}, u32[]{:S(2)}) %collective-permute-start.16) | collective-permute-done | bytes 655392 | tf_op jit(solution)/shard_map/ppermute | solution.py:270
  725.2 29.1 %collective-permute-done.20 = bf16[160,2048]{1,0:T(8,128)(2,1)S(1)} collective-permute-done((bf16[160,2048]{1,0:T(8,128)(2,1)S(1)}, bf16[160,2048]{1,0:T(8,128)(2,1)S(1)}, u32[]{:S(2)}, u32[]{:S(2)}) %collective-permute-start.20) | collective-permute-done | bytes 655392 | tf_op jit(solution)/shard_map/ppermute | solution.py:262
  755.3 11.8 %collective-permute-done.26 = bf16[256,384]{1,0:T(8,128)(2,1)S(1)} collective-permute-done((bf16[256,384]{1,0:T(8,128)(2,1)S(1)}, bf16[256,384]{1,0:T(8,128)(2,1)S(1)}, u32[]{:S(2)}, u32[]{:S(2)}) %collective-permute-start.26) | collective-permute-done | bytes 196640 | tf_op jit(solution)/shard_map/ppermute | solution.py:262
  768.7 15.1 %collective-permute-done.12 = bf16[160,2048]{1,0:T(8,128)(2,1)S(1)} collective-permute-done((bf16[160,2048]{1,0:T(8,128)(2,1)S(1)}, bf16[160,2048]{1,0:T(8,128)(2,1)S(1)}, u32[]{:S(2)}, u32[]{:S(2)}) %collective-permute-start.12) | collective-permute-done | bytes 655392 | tf_op jit(solution)/shard_map/ppermute | solution.py:270
  790.8 12.5 %collective-permute-done.22 = bf16[160,2048]{1,0:T(8,128)(2,1)S(1)} collective-permute-done((bf16[160,2048]{1,0:T(8,128)(2,1)S(1)}, bf16[160,2048]{1,0:T(8,128)(2,1)S(1)}, u32[]{:S(2)}, u32[]{:S(2)}) %collective-permute-start.22) | collective-permute-done | bytes 655392 | tf_op jit(solution)/shard_map/ppermute | solution.py:270
  (289 shorter events, 158.4 us)
Async XLA Ops:
  362.7 61.8 %collective-permute-start = (bf16[320,2048]{1,0:T(8,128)(2,1)}, bf16[320,2048]{1,0:T(8,128)(2,1)}, u32[]{:S(2)}, u32[]{:S(2)}) collective-permute-start(bf16[320,2048]{1,0:T(8,128)(2,1)} %slice.291), channel_id=1, source_target_pairs={{0,1},{1,0},{2,3},{3,2},{4,5},{5,4},{6,7},{7,6},{8,9},{9,8},{10,11... | collective-permute-start | bytes 3932168 | tf_op jit(solution)/shard_map/ppermute | solution.py:274
  382.5 110.8 %collective-permute-start.4 = (bf16[320,2048]{1,0:T(8,128)(2,1)}, bf16[320,2048]{1,0:T(8,128)(2,1)}, u32[]{:S(2)}, u32[]{:S(2)}) collective-permute-start(bf16[320,2048]{1,0:T(8,128)(2,1)} %slice.296), channel_id=1, source_target_pairs={{0,1},{1,0},{2,3},{3,2},{4,5},{5,4},{6,7},{7,6},{8,9},{9,8},{10,11... | collective-permute-start | bytes 3932168 | tf_op jit(solution)/shard_map/ppermute | solution.py:274
  396.2 128.1 %collective-permute-start.30 = (bf16[256,2048]{1,0:T(8,128)(2,1)}, bf16[256,2048]{1,0:T(8,128)(2,1)}, u32[]{:S(2)}, u32[]{:S(2)}) collective-permute-start(bf16[256,2048]{1,0:T(8,128)(2,1)} %get-tuple-element.50), channel_id=1, source_target_pairs={{0,16},{16,0},{1,17},{17,1},{2,18},{18,2},{3,19},{19,3},{4,20},{20... | collective-permute-start | bytes 3145736 | tf_op jit(solution)/shard_map/ppermute | solution.py:266
  398.3 153.9 %collective-permute-start.29 = (bf16[256,2048]{1,0:T(8,128)(2,1)}, bf16[256,2048]{1,0:T(8,128)(2,1)}, u32[]{:S(2)}, u32[]{:S(2)}) collective-permute-start(bf16[256,2048]{1,0:T(8,128)(2,1)} %get-tuple-element.51), channel_id=1, source_target_pairs={{0,16},{16,0},{1,17},{17,1},{2,18},{18,2},{3,19},{19,3},{4,20},{20... | collective-permute-start | bytes 3145736 | tf_op jit(solution)/shard_map/ppermute | solution.py:266
  422.6 67.3 %collective-permute-start.47 = (bf16[2048,256]{1,0:T(8,128)(2,1)S(1)}, bf16[2048,256]{1,0:T(8,128)(2,1)S(1)}, u32[]{:S(2)}, u32[]{:S(2)}) collective-permute-start(bf16[2048,256]{1,0:T(8,128)(2,1)S(1)} %get-tuple-element.45), channel_id=1, source_target_pairs={{0,16},{16,0},{1,17},{17,1},{2,18},{18,2},{3,19},{19,3},{4,20},{20... | collective-permute-start | bytes 3145736 | tf_op jit(solution)/shard_map/ppermute | solution.py:266
  424.5 104.8 %collective-permute-start.46 = (bf16[2048,256]{1,0:T(8,128)(2,1)S(1)}, bf16[2048,256]{1,0:T(8,128)(2,1)S(1)}, u32[]{:S(2)}, u32[]{:S(2)}) collective-permute-start(bf16[2048,256]{1,0:T(8,128)(2,1)S(1)} %get-tuple-element.46), channel_id=1, source_target_pairs={{0,16},{16,0},{1,17},{17,1},{2,18},{18,2},{3,19},{19,3},{4,20},{20... | collective-permute-start | bytes 3145736 | tf_op jit(solution)/shard_map/ppermute | solution.py:266
  493.3 32.1 %collective-permute-start.32 = (bf16[256,2048]{1,0:T(8,128)(2,1)S(1)}, bf16[256,2048]{1,0:T(8,128)(2,1)S(1)}, u32[]{:S(2)}, u32[]{:S(2)}) collective-permute-start(bf16[256,2048]{1,0:T(8,128)(2,1)S(1)} %add_convert_fusion.5), channel_id=1, source_target_pairs={{0,4},{4,8},{8,12},{12,0},{1,5},{5,9},{9,13},{13,1},{2,6},{6,10},{... | collective-permute-start | bytes 3145736 | tf_op jit(solution)/shard_map/ppermute | solution.py:262
  524.3 51.2 %collective-permute-start.45 = (bf16[2048,256]{1,0:T(8,128)(2,1)S(1)}, bf16[2048,256]{1,0:T(8,128)(2,1)S(1)}, u32[]{:S(2)}, u32[]{:S(2)}) collective-permute-start(bf16[2048,256]{1,0:T(8,128)(2,1)S(1)} %get-tuple-element.47), channel_id=1, source_target_pairs={{0,16},{16,0},{1,17},{17,1},{2,18},{18,2},{3,19},{19,3},{4,20},{20... | collective-permute-start | bytes 3145736 | tf_op jit(solution)/shard_map/ppermute | solution.py:266
  543.1 27.9 %collective-permute-start.33 = (bf16[256,2048]{1,0:T(8,128)(2,1)S(1)}, bf16[256,2048]{1,0:T(8,128)(2,1)S(1)}, u32[]{:S(2)}, u32[]{:S(2)}) collective-permute-start(bf16[256,2048]{1,0:T(8,128)(2,1)S(1)} %add_convert_fusion.4), channel_id=1, source_target_pairs={{0,4},{4,8},{8,12},{12,0},{1,5},{5,9},{9,13},{13,1},{2,6},{6,10},{... | collective-permute-start | bytes 3145736 | tf_op jit(solution)/shard_map/ppermute | solution.py:262
  547.2 41.1 %collective-permute-start.49 = (bf16[2048,256]{1,0:T(8,128)(2,1)S(1)}, bf16[2048,256]{1,0:T(8,128)(2,1)S(1)}, u32[]{:S(2)}, u32[]{:S(2)}) collective-permute-start(bf16[2048,256]{1,0:T(8,128)(2,1)S(1)} %add_convert_fusion.1), channel_id=1, source_target_pairs={{0,4},{4,8},{8,12},{12,0},{1,5},{5,9},{9,13},{13,1},{2,6},{6,10},{... | collective-permute-start | bytes 3145736 | tf_op jit(solution)/shard_map/ppermute | solution.py:262
  552.0 38.0 %collective-permute-start.7 = (bf16[320,2048]{1,0:T(8,128)(2,1)S(1)}, bf16[320,2048]{1,0:T(8,128)(2,1)S(1)}, u32[]{:S(2)}, u32[]{:S(2)}) collective-permute-start(bf16[320,2048]{1,0:T(8,128)(2,1)S(1)} %pad_maximum_fusion.6), channel_id=1, source_target_pairs={{0,1},{1,0},{2,3},{3,2},{4,5},{5,4},{6,7},{7,6},{8,9},{9,8},{10,11... | collective-permute-start | bytes 3932168 | tf_op jit(solution)/shard_map/ppermute | solution.py:274
  552.1 107.8 %collective-permute-start.28 = (bf16[256,2048]{1,0:T(8,128)(2,1)}, bf16[256,2048]{1,0:T(8,128)(2,1)}, u32[]{:S(2)}, u32[]{:S(2)}) collective-permute-start(bf16[256,2048]{1,0:T(8,128)(2,1)} %get-tuple-element.48), channel_id=1, source_target_pairs={{0,16},{16,0},{1,17},{17,1},{2,18},{18,2},{3,19},{19,3},{4,20},{20... | collective-permute-start | bytes 3145736 | tf_op jit(solution)/shard_map/ppermute | solution.py:266
  571.0 232.4 %collective-permute-start.44 = (bf16[2048,256]{1,0:T(8,128)(2,1)}, bf16[2048,256]{1,0:T(8,128)(2,1)S(1)}, u32[]{:S(2)}, u32[]{:S(2)}) collective-permute-start(bf16[2048,256]{1,0:T(8,128)(2,1)} %get-tuple-element.44), channel_id=1, source_target_pairs={{0,16},{16,0},{1,17},{17,1},{2,18},{18,2},{3,19},{19,3},{4,20},{20... | collective-permute-start | bytes 3145736 | tf_op jit(solution)/shard_map/ppermute | solution.py:266
  593.2 32.6 %collective-permute-start.9 = (bf16[640,128]{1,0:T(8,128)(2,1)S(1)}, bf16[640,128]{1,0:T(8,128)(2,1)S(1)}, u32[]{:S(2)}, u32[]{:S(2)}) collective-permute-start(bf16[640,128]{1,0:T(8,128)(2,1)S(1)} %get-tuple-element.82), channel_id=1, source_target_pairs={{0,8},{4,12},{8,0},{12,4},{1,9},{5,13},{9,1},{13,5},{2,10},{6,14},... | collective-permute-start | bytes 491528 | tf_op jit(solution)/shard_map/ppermute | solution.py:262
  594.0 33.6 %collective-permute-start.8 = (bf16[640,128]{1,0:T(8,128)(2,1)S(1)}, bf16[640,128]{1,0:T(8,128)(2,1)S(1)}, u32[]{:S(2)}, u32[]{:S(2)}) collective-permute-start(bf16[640,128]{1,0:T(8,128)(2,1)S(1)} %get-tuple-element.83), channel_id=1, source_target_pairs={{0,4},{4,8},{8,12},{12,0},{1,5},{5,9},{9,13},{13,1},{2,6},{6,10},{... | collective-permute-start | bytes 491528 | tf_op jit(solution)/shard_map/ppermute | solution.py:262
  599.6 60.9 %collective-permute-start.34 = (bf16[256,2048]{1,0:T(8,128)(2,1)}, bf16[256,2048]{1,0:T(8,128)(2,1)}, u32[]{:S(2)}, u32[]{:S(2)}) collective-permute-start(bf16[256,2048]{1,0:T(8,128)(2,1)} %add_convert_fusion.3), channel_id=1, source_target_pairs={{0,4},{4,8},{8,12},{12,0},{1,5},{5,9},{9,13},{13,1},{2,6},{6,10},{... | collective-permute-start | bytes 3145736 | tf_op jit(solution)/shard_map/ppermute | solution.py:262
  625.8 32.4 %collective-permute-start.40 = (bf16[512,256]{1,0:T(8,128)(2,1)}, bf16[512,256]{1,0:T(8,128)(2,1)}, u32[]{:S(2)}, u32[]{:S(2)}) collective-permute-start(bf16[512,256]{1,0:T(8,128)(2,1)} %get-tuple-element.69), channel_id=1, source_target_pairs={{0,16},{16,0},{1,17},{17,1},{2,18},{18,2},{3,19},{19,3},{4,20},{20... | collective-permute-start | bytes 786440 | tf_op jit(solution)/shard_map/ppermute | solution.py:266
  670.9 27.3 %collective-permute-start.24 = (bf16[1024,384]{1,0:T(8,128)(2,1)S(1)}, bf16[1024,384]{1,0:T(8,128)(2,1)S(1)}, u32[]{:S(2)}, u32[]{:S(2)}) collective-permute-start(bf16[1024,384]{1,0:T(8,128)(2,1)S(1)} %dynamic-slice_bitcast_fusion), channel_id=1, source_target_pairs={{0,16},{16,0},{1,17},{17,1},{2,18},{18,2},{3,19},{19,3},{4,20},{20... | collective-permute-start | bytes 2359304 | tf_op jit(solution)/shard_map/ppermute | solution.py:266
  683.2 35.1 %collective-permute-start.11 = (bf16[320,2048]{1,0:T(8,128)(2,1)S(1)}, bf16[320,2048]{1,0:T(8,128)(2,1)S(1)}, u32[]{:S(2)}, u32[]{:S(2)}) collective-permute-start(bf16[320,2048]{1,0:T(8,128)(2,1)S(1)} %slice.305), channel_id=1, source_target_pairs={{0,1},{1,0},{2,3},{3,2},{4,5},{5,4},{6,7},{7,6},{8,9},{9,8},{10,11... | collective-permute-start | bytes 3932168 | tf_op jit(solution)/shard_map/ppermute | solution.py:274
  698.5 105.5 %collective-permute-start.50 = (bf16[2048,256]{1,0:T(8,128)(2,1)S(1)}, bf16[2048,256]{1,0:T(8,128)(2,1)S(1)}, u32[]{:S(2)}, u32[]{:S(2)}) collective-permute-start(bf16[2048,256]{1,0:T(8,128)(2,1)S(1)} %add_convert_fusion), channel_id=1, source_target_pairs={{0,4},{4,8},{8,12},{12,0},{1,5},{5,9},{9,13},{13,1},{2,6},{6,10},{... | collective-permute-start | bytes 3145736 | tf_op jit(solution)/shard_map/ppermute | solution.py:262
  718.2 36.2 %collective-permute-start.20 = (bf16[160,2048]{1,0:T(8,128)(2,1)S(1)}, bf16[160,2048]{1,0:T(8,128)(2,1)S(1)}, u32[]{:S(2)}, u32[]{:S(2)}) collective-permute-start(bf16[160,2048]{1,0:T(8,128)(2,1)S(1)} %fusion.28), channel_id=1, source_target_pairs={{0,4},{4,8},{8,12},{12,0},{1,5},{5,9},{9,13},{13,1},{2,6},{6,10},{... | collective-permute-start | bytes 1966088 | tf_op jit(solution)/shard_map/ppermute | solution.py:262
  718.3 36.3 %collective-permute-start.27 = (bf16[256,384]{1,0:T(8,128)(2,1)S(1)}, bf16[256,384]{1,0:T(8,128)(2,1)S(1)}, u32[]{:S(2)}, u32[]{:S(2)}) collective-permute-start(bf16[256,384]{1,0:T(8,128)(2,1)S(1)} %get-tuple-element.77), channel_id=1, source_target_pairs={{0,12},{4,0},{8,4},{12,8},{1,13},{5,1},{9,5},{13,9},{2,14},{6,2},{... | collective-permute-start | bytes 589832 | tf_op jit(solution)/shard_map/ppermute | solution.py:262
  725.2 41.9 %collective-permute-start.26 = (bf16[256,384]{1,0:T(8,128)(2,1)S(1)}, bf16[256,384]{1,0:T(8,128)(2,1)S(1)}, u32[]{:S(2)}, u32[]{:S(2)}) collective-permute-start(bf16[256,384]{1,0:T(8,128)(2,1)S(1)} %get-tuple-element.78), channel_id=1, source_target_pairs={{0,8},{4,12},{8,0},{12,4},{1,9},{5,13},{9,1},{13,5},{2,10},{6,14},... | collective-permute-start | bytes 589832 | tf_op jit(solution)/shard_map/ppermute | solution.py:262
  754.6 53.3 %collective-permute-start.37 = (bf16[512,256]{1,0:T(8,128)(2,1)S(1)}, bf16[512,256]{1,0:T(8,128)(2,1)S(1)}, u32[]{:S(2)}, u32[]{:S(2)}) collective-permute-start(bf16[512,256]{1,0:T(8,128)(2,1)S(1)} %copy-done.21), channel_id=1, source_target_pairs={{0,16},{16,0},{1,17},{17,1},{2,18},{18,2},{3,19},{19,3},{4,20},{20... | collective-permute-start | bytes 786440 | tf_op jit(solution)/shard_map/ppermute | solution.py:266
  (61 other events, 843.4 us)

commit v3 on v2

--- a/solution.py
+++ b/solution.py
@@ -289,24 +289,6 @@
     half = part[: 2 * n].astype(jnp.float32) + swap_core(low[2 * n :]).astype(jnp.float32)
     other = swap_chip(half[n:].astype(jnp.bfloat16))
     return half[:n] + other.astype(jnp.float32)
-
-
-def gather_blocks(own):
-    mine = [own]
-    for _ in range(SEQ - 1):
-        mine.append(shift(mine[-1], 1))
-    return mine, [swap_dp(block) for block in mine]
-
-
-def scatter_blocks(parts):
-    running = None
-    for k in (1, 2, 3, 0):
-        total = parts[k].astype(jnp.float32) + swap_dp(parts[SEQ + k]).astype(jnp.float32)
-        if running is not None:
-            total = total + running.astype(jnp.float32)
-        if k:
-            running = shift(total.astype(jnp.bfloat16), 1)
-    return total
 
 
 def dyn(stack, index):
@@ -590,62 +572,375 @@
     )(f0, w_three, w_out, w_up, w_down, own, bias)
 
 
-def attend_back_kernel(place_ref, valid_ref, qkv_ref, out_ref, lse_ref, do_ref, grad_ref, delta, dq, dk, dv):
-    place = place_ref[0]
+def back_kernel(
+    gd_ref, gd_came_ref, gu_ref, dn_ref, cot_ref, normed_two_ref, rate_two_ref, attended_ref, out_ref, qkv_ref, att_ref, lse_ref, bias_ref, w_head_ref, whole_ref,
+    normed_one_ref, rate_one_ref,
+    down_sum_ref, up_sum_ref, out_sum_ref, arrived_ref, grad_in_ref, cross_down_ref, cross_up_ref, ring_down_ref, ring_up_ref, first_core_ref, first_chip_ref, first_ring_ref,
+    frames, t_cross, t_own, t_ring, outbox, mix, d_head, d_out, dq, dk, dv, delta, d_three, out_send, out_cross, out_ring, out_box,
+    head_acc, head_low, head_cross, head_sum, dn_own, dn_core, half_low, dn_chip, mid, quart_box, in_box,
+    send, recv, keep_sem, load_sem,
+):
+    dp, z, t = lax.axis_index("dp"), lax.axis_index("seq"), lax.axis_index("tensor")
+    other_dp, chip, core = {"dp": 1 - dp}, {"tensor": lax.rem(t + 2, 4)}, {"tensor": t + 1 - 2 * lax.rem(t, 2)}
+    f32, bf16 = jnp.float32, jnp.bfloat16
+
+    def along(k):
+        return {"seq": lax.rem(z + k + SEQ, SEQ)}
+
+    rows, width = dn_ref.shape
+    quarter, half = rows // 4, rows // 2
+    part, hidden = gd_came_ref.shape
+    inner = attended_ref.shape[1]
+    half_inner = inner // 2
+    ring = along(1)
     scale = HEAD_DIM ** (-0.5)
+    used, sent = [], []
+
+    def remote(src, dst, device):
+        i = len(used)
+        copy = pltpu.make_async_remote_copy(src_ref=src, dst_ref=dst, send_sem=send.at[i], recv_sem=recv.at[i], device_id=device, device_id_type=MESH)
+        used.append(copy)
+        return copy
+
+    def flush(copy):
+        if not any(copy is done for done in sent):
+            copy.wait_send()
+            sent.append(copy)
+
+    def load(*pairs):
+        copies = [pltpu.make_async_copy(src, dst, load_sem.at[i]) for i, (src, dst) in enumerate(pairs)]
+        for copy in copies:
+            copy.start()
+        for copy in copies:
+            copy.wait()
+
+    barrier = pltpu.get_barrier_semaphore()
+    peers = [other_dp, chip, core] + [along(k) for k in range(1, SEQ)]
+    for peer in peers:
+        pl.semaphore_signal(barrier, inc=1, device_id=peer, device_id_type=MESH)
+    pl.semaphore_wait(barrier, len(peers))
+
+    def block(ref, b):
+        return ref.at[pl.ds(b * part, part), :]
+
+    dn_core_copy = remote(dn_ref.at[pl.ds(half, half), :], dn_core, core)
+    dn_chip_copy = remote(half_low, dn_chip, chip)
+    mix_chip = remote(mix.at[pl.ds(0, quarter), :], mix.at[pl.ds(quarter, quarter), :], chip)
+    mix_core = remote(mix.at[pl.ds(0, half), :], mix.at[pl.ds(half, half), :], core)
+    spread = [None] + [remote(d_head.at[lax.rem(z + k, SEQ)], d_out.at[k], along(k)) for k in range(1, SEQ)]
+    cross_down = {k: remote(block(gd_ref, SEQ + k), cross_down_ref.at[k], other_dp) for k in (2, 3, 0)}
+    cross_up = {k: remote(block(gu_ref, SEQ + k), cross_up_ref.at[k], other_dp) for k in (1, 2, 3, 0)}
+    cross_out = {k: remote(out_send.at[k], out_cross.at[k], other_dp) for k in (1, 2, 3, 0)}
+    ring_down = {k: remote(outbox.at[k - 1], ring_down_ref.at[k - 1], ring) for k in (1, 2, 3)}
+    ring_up = {k: remote(outbox.at[k - 1], ring_up_ref.at[k - 1], ring) for k in (1, 2, 3)}
+    ring_out = {k: remote(out_box.at[k - 1], out_ring.at[k - 1], ring) for k in (1, 2, 3)}
+    first_core = {k: remote(frames.at[k, pl.ds(half, half), :], first_core_ref.at[k], core) for k in (1, 2, 3, 0)}
+    first_chip = {k: remote(quart_box.at[k], first_chip_ref.at[k], chip) for k in (1, 2, 3, 0)}
+    first_ring = {k: remote(in_box.at[k - 1], first_ring_ref.at[k - 1], ring) for k in (1, 2, 3)}
+    head_dp = remote(head_low.at[1 - dp], head_cross, other_dp)
+    head_out = [None] + [remote(head_sum.at[lax.rem(z + k, SEQ)], arrived_ref.at[k], along(k)) for k in range(1, SEQ)]
+    mine = grad_in_ref.at[pl.ds(t * quarter, quarter), :]
+    mate = grad_in_ref.at[pl.ds(lax.rem(t + 2, 4) * quarter, quarter), :]
+    in_chip = remote(in_box.at[3], mine, chip)
+    in_core = [remote(in_box.at[3], mine, core), remote(mate, mate, core)]
+
+    def scatter(k, own_ref, cross_at, crossing, ring_ref, rings, out, turned):
+        pairs = [(cross_at, t_cross), (block(own_ref, k), t_own)]
+        if crossing is not None and k != 2:
+            crossing.wait_recv()
+        if k != 1:
+            came = (k - 1) % SEQ
+            rings[came].wait_recv()
+            pairs.append((ring_ref.at[came - 1], t_ring))
+        load(*pairs)
+        if k:
+            for copies in (ring_down, ring_up):
+                if copies is not rings and any(copies[k] is one for one in busy):
+                    flush(copies[k])
+            busy.append(rings[k])
+
+        def piece(n, carry):
+            at = pl.ds(pl.multiple_of(n * 256, 256), 256)
+            sum_ = t_cross[:, at].astype(f32) + t_own[:, at].astype(f32)
+            if k != 1:
+                sum_ = sum_ + t_ring[:, at].astype(f32)
+            if k:
+                outbox[k - 1, :, at] = sum_.astype(bf16)
+            elif turned:
+                out[at, :] = sum_.T
+            else:
+                out[:, at] = sum_
+            return carry
+
+        lax.fori_loop(0, hidden // 256, piece, 0)
+        if k:
+            rings[k].start()
+
+    busy = []
+
+    def scatter_down(k):
+        scatter(k, gd_ref, gd_came_ref if k == 1 else cross_down_ref.at[k], cross_down.get(k), ring_down_ref, ring_down, down_sum_ref, True)
+
+    def scatter_up(k):
+        if k == 2:
+            cross_up[k].wait_recv()
+        scatter(k, gu_ref, cross_up_ref.at[k], cross_up[k], ring_up_ref, ring_up, up_sum_ref, False)
+
+    def out_block(b):
+        return lax.dot_general(attended_ref[...], mix[:, b * part : (b + 1) * part], (((0,), (0,)), ((), ())), preferred_element_type=f32)
+
+    def scatter_out(k):
+        cross_out[k].wait_recv()
+        sum_ = out_block(k) + out_cross[k].astype(f32)
+        if k != 1:
+            came = (k - 1) % SEQ
+            ring_out[came].wait_recv()
+            sum_ = sum_ + out_ring[came - 1].astype(f32)
+        if k:
+            out_box[k - 1] = sum_.astype(bf16)
+            ring_out[k].start()
+        else:
+            out_sum_ref[...] = sum_
+
+    dn_core_copy.start()
+    cross_down[2].start()
+    cross_down[3].start()
+    fetch = [pltpu.make_async_copy(whole_ref.at[k], frames.at[k], keep_sem.at[k]) for k in range(SEQ)]
+    spare = head_acc.at[pl.ds(0, quarter), :]
+    load((dn_ref.at[pl.ds(0, half), :], dn_own), (normed_two_ref, spare), (out_ref.at[pl.ds(0, half_inner), :], outbox.at[1]), (out_ref.at[pl.ds(half_inner, half_inner), :], outbox.at[2]))
+    for copy in fetch:
+        copy.start()
+    dn_core_copy.wait_recv()
+    half_low[...] = (dn_own[quarter:half, :].astype(f32) + dn_core[quarter:half, :].astype(f32)).astype(bf16)
+    dn_chip_copy.start()
+    scatter_down(1)
+    dn_chip_copy.wait_recv()
+    grad = (dn_own[0:quarter, :].astype(f32) + dn_core[0:quarter, :].astype(f32)) + dn_chip[...].astype(f32)
+    normed = spare[...]
+    grad = rate_two_ref[...] * (grad - jnp.mean(grad, axis=1, keepdims=True) - normed * jnp.mean(grad * normed, axis=1, keepdims=True))
+    grad = cot_ref[...].astype(f32) + grad
+    mid[...] = grad
+    mix[0:quarter, :] = grad.astype(bf16)
+    mix_chip.start()
+    cross_down[2].wait_recv()
+    cross_down[0].start()
+    mix_chip.wait_recv()
+    mix_core.start()
+    mix_core.wait_recv()
+
+    for n in range(4):
+        at = slice(n * quarter, (n + 1) * quarter)
+        for side in range(2):
+            piece = lax.dot_general(mix[at, :], outbox[side + 1], (((1,), (1,)), ((), ())), preferred_element_type=f32).astype(bf16)
+            for h in range(SEQ // 2):
+                d_head[side * (SEQ // 2) + h, at, :] = piece[:, h * HEAD_DIM : (h + 1) * HEAD_DIM]
+    for k in range(1, SEQ):
+        spread[k].start()
+    d_out[0] = d_head[z]
+    for k in (1, 2, 3, 0):
+        out_send[k] = out_block(SEQ + k).astype(bf16)
+        cross_out[k].start()
+    scatter_down(2)
+    cross_up[1].start()
+    for k in range(1, SEQ):
+        spread[k].wait_recv()
     dq[...] = jnp.zeros_like(dq)
     for f in range(SEQ):
-        delta[f] = jnp.sum((do_ref[f].astype(jnp.float32) * out_ref[f]).T, axis=0, keepdims=True)
-
-    def key_frame(j, carry):
-        here = lax.rem(place - j + SEQ, SEQ)
+        delta[f] = jnp.sum((d_out[f].astype(f32) * att_ref[f]).T, axis=0, keepdims=True)
+
+    def key_frame(j):
+        here = lax.rem(z - j + SEQ, SEQ)
         dk[...] = jnp.zeros_like(dk)
         dv[...] = jnp.zeros_like(dv)
 
-        @pl.when(valid_ref[j] == 1)
-        def _():
-            def query_frame(i, inner):
-                at = lax.rem(place - i + SEQ, SEQ)
-                query, key, value = qkv_ref[at, :, :HEAD_DIM], qkv_ref[here, :, HEAD_DIM : 2 * HEAD_DIM], qkv_ref[here, :, 2 * HEAD_DIM :]
-                d_out = do_ref[at]
-                scores = lax.dot_general(key, query, (((1,), (1,)), ((), ())), preferred_element_type=jnp.float32) * scale
-                prob = jnp.exp(scores - lse_ref[at])
-                d_prob = lax.dot_general(value, d_out, (((1,), (1,)), ((), ())), preferred_element_type=jnp.float32)
-                d_scores = (prob * (d_prob - delta[at])).astype(jnp.bfloat16)
-                dv[...] += jnp.dot(prob.astype(jnp.bfloat16), d_out, preferred_element_type=jnp.float32)
-                dk[...] += jnp.dot(d_scores, query, preferred_element_type=jnp.float32)
-                dq[at] += lax.dot_general(key, d_scores, (((0,), (0,)), ((), ())), preferred_element_type=jnp.float32)
-                return inner
-
-            lax.fori_loop(j, SEQ, query_frame, 0)
-
-        grad_ref[here, :, HEAD_DIM : 2 * HEAD_DIM] = (dk[...] * scale).astype(jnp.bfloat16)
-        grad_ref[here, :, 2 * HEAD_DIM :] = dv[...].astype(jnp.bfloat16)
-        return carry
-
-    lax.fori_loop(0, SEQ, key_frame, 0)
+        def query_frame(i, inner_):
+            at = lax.rem(z - i + SEQ, SEQ)
+            query, key, value = qkv_ref[at, :, :HEAD_DIM], qkv_ref[here, :, HEAD_DIM : 2 * HEAD_DIM], qkv_ref[here, :, 2 * HEAD_DIM :]
+            grad_out = d_out[at]
+            scores = lax.dot_general(key, query, (((1,), (1,)), ((), ())), preferred_element_type=f32) * scale + bias_ref[j]
+            prob = jnp.exp(scores - lse_ref[at])
+            d_prob = lax.dot_general(value, grad_out, (((1,), (1,)), ((), ())), preferred_element_type=f32)
+            d_scores = (prob * (d_prob - delta[at])).astype(bf16)
+            dv[...] += jnp.dot(prob.astype(bf16), grad_out, preferred_element_type=f32)
+            dk[...] += jnp.dot(d_scores, query, preferred_element_type=f32)
+            dq[at] += lax.dot_general(key, d_scores, (((0,), (0,)), ((), ())), preferred_element_type=f32)
+            return inner_
+
+        lax.fori_loop(j, SEQ, query_frame, 0)
+        d_three[here, :, HEAD_DIM : 2 * HEAD_DIM] = (dk[...] * scale).astype(bf16)
+        d_three[here, :, 2 * HEAD_DIM :] = dv[...].astype(bf16)
+
+    key_frame(0)
+    scatter_out(1)
+    key_frame(1)
+    scatter_down(3)
+    cross_up[2].start()
+    key_frame(2)
+    scatter_out(2)
+    key_frame(3)
     for f in range(SEQ):
-        grad_ref[f, :, :HEAD_DIM] = (dq[f] * scale).T.astype(jnp.bfloat16)
-
-
-def attend_back(place, valid, qkv, out, lse, d_out):
-    rows = qkv.shape[1]
-    smem = pl.BlockSpec(memory_space=pltpu.SMEM)
-    vmem = pl.BlockSpec(memory_space=pltpu.VMEM)
+        d_three[f, :, :HEAD_DIM] = (dq[f] * scale).T.astype(bf16)
+
+    def project_back(k):
+        fetch[k].wait()
+
+        def piece(n, carry):
+            at = pl.ds(pl.multiple_of(n * 512, 512), 512)
+            term = lax.dot_general(d_three[k], frames[k, :, at], (((0,), (0,)), ((), ())), preferred_element_type=f32)
+            head_acc[:, at] = term if k == 1 else head_acc[:, at] + term
+            return carry
+
+        lax.fori_loop(0, width // 512, piece, 0)
+
+        def back_piece(n, carry):
+            at = pl.ds(pl.multiple_of(n * 512, 512), 512)
+            frames[k, :, at] = lax.dot_general(d_three[k], w_head_ref[at, :], (((1,), (1,)), ((), ())), preferred_element_type=f32).astype(bf16)
+            return carry
+
+        lax.fori_loop(0, width // 512, back_piece, 0)
+        first_core[k].start()
+
+    def half_sum(k):
+        first_core[k].wait_recv()
+        load((first_core_ref.at[k], dn_own))
+        quart_box[k] = (frames[k, quarter:half, :].astype(f32) + dn_own[quarter:half, :].astype(f32)).astype(bf16)
+        first_chip[k].start()
+        frames[k, 0:quarter, :] = (frames[k, 0:quarter, :].astype(f32) + dn_own[0:quarter, :].astype(f32)).astype(bf16)
+
+    def quarter_sum(k):
+        first_chip[k].wait_recv()
+        pairs = [(first_chip_ref.at[k], dn_own.at[pl.ds(0, quarter), :])]
+        if k != 1:
+            came = (k - 1) % SEQ
+            first_ring[came].wait_recv()
+            pairs.append((first_ring_ref.at[came - 1], dn_own.at[pl.ds(quarter, quarter), :]))
+        load(*pairs)
+        sum_ = frames[k, 0:quarter, :].astype(f32) + dn_own[0:quarter, :].astype(f32)
+        if k != 1:
+            sum_ = sum_ + dn_own[quarter:half, :].astype(f32)
+        return sum_
+
+    project_back(1)
+    project_back(2)
+    half_sum(1)
+    project_back(3)
+    half_sum(2)
+    project_back(0)
+    half_sum(3)
+    half_sum(0)
+    for side in range(2):
+        head_low[side] = head_acc[:, side * (width // 2) : (side + 1) * (width // 2)].astype(bf16)
+    head_dp.start()
+    scatter_out(3)
+    in_box[0] = quarter_sum(1).astype(bf16)
+    first_ring[1].start()
+    scatter_down(0)
+    cross_up[3].start()
+    in_box[1] = quarter_sum(2).astype(bf16)
+    first_ring[2].start()
+    scatter_up(1)
+    in_box[2] = quarter_sum(3).astype(bf16)
+    first_ring[3].start()
+    head_dp.wait_recv()
+    cross_up[0].start()
+    for j in range(SEQ):
+        at = slice(j * part, (j + 1) * part)
+        head_sum[j] = (head_low[dp, :, at].astype(f32) + head_cross[:, at].astype(f32)).astype(bf16)
+    for k in range(1, SEQ):
+        head_out[k].start()
+    own_head = pltpu.make_async_copy(head_sum.at[z], arrived_ref.at[0], keep_sem.at[0])
+    own_head.start()
+    scatter_out(0)
+    scatter_up(2)
+    grad = quarter_sum(0)
+    load((normed_one_ref, spare))
+    normed = spare[...]
+    grad = rate_one_ref[...] * (grad - jnp.mean(grad, axis=1, keepdims=True) - normed * jnp.mean(grad * normed, axis=1, keepdims=True))
+    for c in range(2 * SEQ):
+        b = lax.rem(dp + c // SEQ, 2) * SEQ + lax.rem(z - c % SEQ + SEQ, SEQ)
+        at = slice(c * part, (c + 1) * part)
+        in_box[3, :, at] = (mid[:, pl.ds(pl.multiple_of(b * part, part), part)] + grad[:, at]).astype(bf16)
+    in_chip.start()
+    in_core[0].start()
+    own_in = pltpu.make_async_copy(in_box.at[3], mine, keep_sem.at[1])
+    own_in.start()
+    in_chip.wait_recv()
+    in_core[1].start()
+    scatter_up(3)
+    scatter_up(0)
+    for copy in in_core + head_out[1:]:
+        copy.wait_recv()
+    for copy in used:
+        flush(copy)
+    own_head.wait()
+    own_in.wait()
+
+
+def back(gd, gd_came, gu, dn, cot, normed_two, rate_two, attended, out_rel, qkv, att, lse, bias, w_head, whole, normed_one, rate_one):
+    rows, width = dn.shape
+    quarter, half = rows // 4, rows // 2
+    part = gd_came.shape[0]
+    inner = attended.shape[1]
+    hidden = gd.shape[1]
+    three = 3 * HEAD_DIM
+    f32, bf16 = jnp.float32, jnp.bfloat16
+    any_, vmem = pl.BlockSpec(memory_space=pl.ANY), pl.BlockSpec(memory_space=pltpu.VMEM)
+    shape = jax.ShapeDtypeStruct
+    outs = [
+        (shape((hidden, part), f32), vmem),
+        (shape((part, hidden), f32), vmem),
+        (shape((inner, part), f32), vmem),
+        (shape((SEQ, three, part), bf16), any_),
+        (shape((rows, width), bf16), any_),
+        (shape((SEQ, part, hidden), bf16), any_),
+        (shape((SEQ, part, hidden), bf16), any_),
+        (shape((SEQ - 1, part, hidden), bf16), any_),
+        (shape((SEQ - 1, part, hidden), bf16), any_),
+        (shape((SEQ, half, width), bf16), any_),
+        (shape((SEQ, quarter, width), bf16), any_),
+        (shape((SEQ - 1, quarter, width), bf16), any_),
+    ]
+    copies = 4 + 3 + 3 + 4 + 4 + 9 + 4 + 4 + 3 + 1 + 3 + 3
+    scratch = [
+        ((SEQ, rows, width), bf16),
+        ((part, hidden), bf16),
+        ((part, hidden), bf16),
+        ((part, hidden), bf16),
+        ((SEQ - 1, part, hidden), bf16),
+        ((rows, width), bf16),
+        ((SEQ, rows, HEAD_DIM), bf16),
+        ((SEQ, rows, HEAD_DIM), bf16),
+        ((SEQ, HEAD_DIM, rows), f32),
+        ((rows, HEAD_DIM), f32),
+        ((rows, HEAD_DIM), f32),
+        ((SEQ, 1, rows), f32),
+        ((SEQ, rows, three), bf16),
+        ((SEQ, inner, part), bf16),
+        ((SEQ, inner, part), bf16),
+        ((SEQ - 1, inner, part), bf16),
+        ((SEQ - 1, inner, part), bf16),
+        ((three, width), f32),
+        ((2, three, width // 2), bf16),
+        ((three, width // 2), bf16),
+        ((SEQ, three, part), bf16),
+        ((half, width), bf16),
+        ((half, width), bf16),
+        ((quarter, width), bf16),
+        ((quarter, width), bf16),
+        ((quarter, width), f32),
+        ((SEQ, quarter, width), bf16),
+        ((SEQ, quarter, width), bf16),
+    ]
     return pl.pallas_call(
-        attend_back_kernel,
-        out_shape=jax.ShapeDtypeStruct((SEQ, rows, 3 * HEAD_DIM), jnp.bfloat16),
-        in_specs=[smem, smem] + [vmem] * 4,
-        out_specs=vmem,
-        scratch_shapes=[
-            pltpu.VMEM((SEQ, 1, rows), jnp.float32),
-            pltpu.VMEM((SEQ, HEAD_DIM, rows), jnp.float32),
-            pltpu.VMEM((rows, HEAD_DIM), jnp.float32),
-            pltpu.VMEM((rows, HEAD_DIM), jnp.float32),
-        ],
-        compiler_params=pltpu.CompilerParams(vmem_limit_bytes=48 * 2**20),
-        cost_estimate=pl.CostEstimate(flops=10 * 10 * rows * rows * HEAD_DIM * 2, bytes_accessed=5 * qkv.size, transcendentals=10 * rows * rows),
-    )(place, valid, qkv, out, lse, d_out)
+        back_kernel,
+        out_shape=[o[0] for o in outs],
+        in_specs=[any_] * 4 + [vmem, any_, vmem, vmem, any_] + [vmem] * 5 + [any_] * 2 + [vmem],
+        out_specs=[o[1] for o in outs],
+        scratch_shapes=[pltpu.VMEM(*one) for one in scratch]
+        + [pltpu.SemaphoreType.DMA((copies,)), pltpu.SemaphoreType.DMA((copies,)), pltpu.SemaphoreType.DMA((SEQ,)), pltpu.SemaphoreType.DMA((4,))],
+        compiler_params=pltpu.CompilerParams(collective_id=1, has_side_effects=True, vmem_limit_bytes=62 * 2**20),
+        cost_estimate=pl.CostEstimate(flops=20 * 10**9, bytes_accessed=60 * 10**6, transcendentals=5 * 10**6),
+    )(gd, gd_came, gu, dn, cot, normed_two, rate_two, attended, out_rel, qkv, att, lse, bias, w_head, whole, normed_one, rate_one)[:5]
 
 
 def norm_parts(values):
@@ -715,46 +1010,24 @@
     cdf = 0.5 * (1.0 + lax.erf(up_pre * (0.5**0.5)))
     up_act = (up_pre * cdf).astype(bf16)
     slope = cdf + up_pre * jnp.exp(-0.5 * up_pre * up_pre) * ((2.0 * jnp.pi) ** -0.5)
-    grad_down = mm(up_act, cot_rel, ((0,), (0,)))
-    d_up = (mm(cot_rel, down_rel, ((1,), (1,)), f32) * slope).astype(bf16)
+    grad_down = mm(cot_rel, up_act, ((0,), (0,)))
+    down_came = swap_dp(grad_down[(SEQ + 1) * part : (SEQ + 2) * part])
     result = resid_mid + scatter_tensor(mm(up_act, down_rel))
     result = can_rows(gather_tensor(can_cols(result.astype(bf16))))[None]
+    d_up = (mm(cot_rel, down_rel, ((1,), (1,)), f32) * slope).astype(bf16)
     grad_up = mm(second_in, d_up, ((0,), (0,)))
-    d_normed_two = scatter_tensor(mm(d_up, up_rel, ((1,), (1,))))
-    cot_own = cot_rel[:quarter].astype(f32)
-    d_mid = cot_own + norm_back(normed_two, rate_two, d_normed_two)
-    d_mix = gather_tensor(d_mid.astype(bf16))
-    grad_out = mm(attended, d_mix, ((0,), (0,)))
-    d_attended = mm(d_mix, out_rel, ((1,), (1,)))
-    d_heads = jnp.stack([d_attended[:, h * HEAD_DIM : (h + 1) * HEAD_DIM] for h in range(heads)])
-    d_out = jnp.stack([dyn(d_heads, z)] + [shift(dyn(d_heads, lax.rem(z + k, SEQ)), k) for k in range(1, SEQ)])
-
-    d_three = attend_back(place, valid, qkv, attended_f, lse, d_out)
-    grad_head = mm(whole.reshape(SEQ * rows, width), d_three.reshape(SEQ * rows, 3 * HEAD_DIM), ((0,), (0,)))
-    grad_head = grad_head.reshape(2, SEQ * part, 3 * HEAD_DIM)
-    grad_rows = dyn(grad_head, dp).astype(f32) + swap_dp(dyn(grad_head, 1 - dp)).astype(f32)
-    grad_rows = grad_rows.astype(bf16).reshape(SEQ, part, 3 * HEAD_DIM)
-    arrived = jnp.stack([dyn(grad_rows, z)] + [shift(dyn(grad_rows, lax.rem(z + k, SEQ)), k) for k in range(1, SEQ)])
-    by_head = [dyn(arrived, lax.rem(z - h + SEQ, SEQ)).astype(f32) for h in range(heads)]
+    d_normed_two = mm(d_up, up_rel, ((1,), (1,)))
+
+    own_quarter = lax.dynamic_slice_in_dim(own_in, t * quarter, quarter, 0).astype(f32)
+    normed_one, rate_one = norm_parts(own_quarter)
+    down_sum, up_raw, out_sum, arrived, grad_in = back(
+        grad_down, down_came, grad_up, d_normed_two, cot_rel[:quarter], normed_two, rate_two, attended, out_rel, qkv, attended_f, lse, bias, w_head, whole, normed_one, rate_one
+    )
+    grad_inputs = grad_in[None]
+    by_head = [dyn(arrived, lax.rem(z - h + SEQ, SEQ)).astype(f32).T for h in range(heads)]
     gain_one = first_gain.astype(f32)[:, None]
     raw = [jnp.concatenate([one[:, n * HEAD_DIM : (n + 1) * HEAD_DIM] for one in by_head], axis=1) for n in range(3)]
     d_gain_one = sum(jnp.sum(weight.astype(f32) * one, axis=1) for weight, one in zip((w_query, w_key, w_value), raw))
-
-    running = None
-    for k in (1, 2, 3, 0):
-        total = scatter_tensor(mm(d_three[k], w_head, ((1,), (1,))))
-        if running is not None:
-            total = total + running.astype(f32)
-        if k:
-            running = shift(total.astype(bf16), 1)
-    own_quarter = lax.dynamic_slice_in_dim(own_in, t * quarter, quarter, 0).astype(f32)
-    normed_one, rate_one = norm_parts(own_quarter)
-    d_in = can_cols(d_mid) + norm_back(normed_one, rate_one, total)
-    grad_inputs = can_rows(gather_tensor(d_in.astype(bf16)))[None]
-
-    down_sum = scatter_blocks([grad_down[:, b * part : (b + 1) * part] for b in range(2 * SEQ)])
-    up_raw = scatter_blocks([grad_up[b * part : (b + 1) * part] for b in range(2 * SEQ)])
-    out_sum = scatter_blocks([grad_out[:, b * part : (b + 1) * part] for b in range(2 * SEQ)])
     d_gain_two = jnp.sum(w_up.astype(f32) * up_raw, axis=1)
     gains = jnp.stack([d_gain_one, d_gain_two])
     gains = gains + swap_core(gains)

time: 820 us -> 767 us (0.935)
  the two profiles are of different devices: /device:TPU:0 before, /device:TPU:27 now
where the time goes in v3:
time: 767 us; the launch traced here: 763 us
  Pallas kernels  628 us (82%)
  matrix products  56.3 us (7%)
  local copies, waits for them, and re-layouts  30.6 us (4%)
  other arithmetic  25.4 us (3%)
  waiting for transfers between devices  14.6 us (2%)
    pallas_call x1, Pallas kernels, front(): pl.pallas_call(front_kernel, out_shape=[o[0] for o in outs], in_specs=[an...  317 us
    pallas_call x1, Pallas kernels, back(): pl.pallas_call(back_kernel, out_shape=[o[0] for o in outs], in_specs=[any...  310 us
    dot_general x6, matrix products, mm(): lax.dot_general(left, right, (dims, ((), ())), preferred_element_type=jnp...  56.3 us
    unnamed x80, local copies, waits for them, and re-layouts  20.3 us
  transfers between devices with their start and end apart: 7, of which 2 were waited for; matrix products, arithmetic and copies ran while one was open for 7% of the time, Pallas kernels for 41%

profile of v3, /device:TPU:27, one launch (start us, length us, event | category | flops | bytes accessed | tf_op | source)
XLA Modules:
  0.0 762.9 jit_solution(15356464794997459173)
XLA Ops:
  2.9 2.2 convert_reduce_fusion
  12.0 2.2 fusion.4
  14.1 2.4 fusion.11.w_up_ref
  16.6 1.9 constant_dynamic-slice_fusion.7
  18.4 2.1 pad_maximum_fusion.f0_ref
  21.2 317.3 %shard_map.186 = (bf16[4,640,2048]{2,1,0:T(8,128)(2,1)}, bf16[2048,384]{1,0:T(8,128)(2,1)}, bf16[4,640,384]{2,1,0:T(8,128)(2,1)}, f32[4,640,128]{2,1,0:T(8,128)}...) custom-call(bf16[640,2048]{1,0:T(8,128)(2,1)} %pad_maximum_fusion.f0, ...), custom_call_target="tpu_custom_call" | custom-call | flops 8000000000 | bytes 50000000 | tf_op jit(solution)/shard_map/pallas_call | solution.py:547
  338.5 10.6 %multiply_convert_fusion = (bf16[640,2048]{1,0:T(8,128)(2,1)S(1)}, f32[640,2048]{1,0:T(8,128)}) fusion(bf16[640,2048]{1,0:T(8,128)(2,1)} %get-tuple-element.29, bf16[2048,2048]{1,0:T(8,128)(2,1)} %get-tuple-element.30), kind=kOutput, calls=%fused_computation.16 | convolution fusion | flops 5375262720 | bytes 18874368 | tf_op jit(solution)/shard_map/dot_general | solution.py:957
  349.2 6.0 convolution_convert_fusion.3
  356.8 1.6 copy-done.6
  359.5 7.0 convolution_convert_fusion.1.gd_ref
  367.7 2.6 copy-done.22
  371.2 2.0 slice.86.cot_ref
  374.3 10.8 %fusion.10 = bf16[640,2048]{1,0:T(8,128)(2,1)S(1)} fusion(f32[640,2048]{1,0:T(8,128)} %get-tuple-element.107, bf16[640,2048]{1,0:T(8,128)(2,1)} %copy-done.18, bf16[2048,2048]{1,0:T(8,128)(2,1)} %get-tuple-element.31), kind=kOutput, calls=%fused_computation.15 | convolution fusion | flops 5381816320 | bytes 18874368 | tf_op jit(solution)/shard_map/dot_general | solution.py:957
  386.6 10.5 %convolution_convert_fusion.2.dn_ref = bf16[640,2048]{1,0:T(8,128)(2,1)} fusion(bf16[640,2048]{1,0:T(8,128)(2,1)S(1)} %fusion.10, bf16[2048,2048]{1,0:T(8,128)(2,1)} %get-tuple-element.30), kind=kOutput, calls=%fused_computation.18 | convolution fusion | flops 5370019840 | bytes 13631488 | tf_op jit(solution)/shard_map/dot_general | solution.py:957
  397.1 11.3 %convolution_convert_fusion.gu_ref = bf16[2048,2048]{1,0:T(8,128)(2,1)} fusion(bf16[640,2048]{1,0:T(8,128)(2,1)} %get-tuple-element.29, bf16[640,2048]{1,0:T(8,128)(2,1)} %copy-done.24), kind=kOutput, calls=%fused_computation.1 | convolution fusion | flops 5372903424 | bytes 13631488 | tf_op jit(solution)/shard_map/dot_general | solution.py:957
  409.9 1.8 convert_add_fusion
  413.3 2.0 collective-permute-start.1
  415.3 310.4 %shard_map.187 = (f32[2048,256]{1,0:T(8,128)}, f32[256,2048]{1,0:T(8,128)}, f32[512,256]{1,0:T(8,128)}, bf16[4,384,256]{2,1,0:T(8,128)(2,1)}, bf16[640,2048]{1,0...) custom-call(bf16[2048,2048]{1,0:T(8,128)(2,1)} %copy-done.22, ...), custom_call_target="tpu_custom_call" | custom-call | flops 20000000000 | bytes 60000000 | tf_op jit(solution)/shard_map/pallas_call | solution.py:934
  725.7 1.5 convert_bitcast_fusion.5
  729.7 13.5 %collective-permute-done.2 = bf16[160,2048]{1,0:T(8,128)(2,1)S(1)} collective-permute-done((bf16[160,2048]{1,0:T(8,128)(2,1)S(1)}, bf16[160,2048]{1,0:T(8,128)(2,1)S(1)}, u32[]{:S(2)}, u32[]{:S(2)}) %collective-permute-start.2) | collective-permute-done | bytes 655392 | tf_op jit(solution)/shard_map/ppermute | solution.py:270
  744.3 2.7 collective-permute-start.3
  747.1 1.6 broadcast_multiply_fusion
  754.0 1.5 pad_maximum_fusion.1
  755.9 1.6 maximum_bitcast_fusion
  (125 shorter events, 34.3 us)
Async XLA Ops:
  0.6 4.5 copy-start
  2.9 3.1 copy-start.19
  2.9 3.9 copy-start.20
  2.9 4.8 copy-start.21
  8.5 2.2 copy-start.10
  8.5 2.2 copy-start.12
  338.5 10.6 %copy-start.23 = (bf16[2048,2048]{1,0:T(8,128)(2,1)S(1)}, bf16[2048,2048]{1,0:T(8,128)(2,1)}, u32[]{:S(2)}) copy-start(bf16[2048,2048]{1,0:T(8,128)(2,1)} %get-tuple-element.31) | copy-start | bytes 25165828
  355.1 3.5 copy-start.4
  355.2 3.2 copy-start.6
  356.4 53.6 %collective-permute-start = (bf16[320,2048]{1,0:T(8,128)(2,1)}, bf16[320,2048]{1,0:T(8,128)(2,1)}, u32[]{:S(2)}, u32[]{:S(2)}) collective-permute-start(bf16[320,2048]{1,0:T(8,128)(2,1)} %slice.82), channel_id=1, source_target_pairs={{0,1},{1,0},{2,3},{3,2},{4,5},{5,4},{6,7},{7,6},{8,9},{9,8},{10,11... | collective-permute-start | bytes 3932168 | tf_op jit(solution)/shard_map/ppermute | solution.py:274
  359.5 7.1 copy-start.18
  366.6 3.7 copy-start.22
  370.3 45.0 %collective-permute-start.4 = (bf16[256,2048]{1,0:T(8,128)(2,1)}, bf16[256,2048]{1,0:T(8,128)(2,1)}, u32[]{:S(2)}, u32[]{:S(2)}) collective-permute-start(bf16[256,2048]{1,0:T(8,128)(2,1)} %slice.85), channel_id=1, source_target_pairs={{0,16},{16,0},{1,17},{17,1},{2,18},{18,2},{3,19},{19,3},{4,20},{20... | collective-permute-start | bytes 3145736 | tf_op jit(solution)/shard_map/ppermute | solution.py:266
  397.1 12.8 %copy-start.5 = (bf16[640,2048]{1,0:T(8,128)(2,1)S(1)}, bf16[640,2048]{1,0:T(8,128)(2,1)}, u32[]{:S(2)}) copy-start(bf16[640,2048]{1,0:T(8,128)(2,1)} %copy-done.4) | copy-start | bytes 7864324
  413.3 314.0 %collective-permute-start.1 = (bf16[160,2048]{1,0:T(8,128)(2,1)S(1)}, bf16[160,2048]{1,0:T(8,128)(2,1)S(1)}, u32[]{:S(2)}, u32[]{:S(2)}) collective-permute-start(bf16[160,2048]{1,0:T(8,128)(2,1)S(1)} %slice.108), channel_id=1, source_target_pairs={{0,2},{1,3},{2,0},{3,1},{4,6},{5,7},{6,4},{7,5},{8,10},{9,11},{10,... | collective-permute-start | bytes 1966088 | tf_op jit(solution)/shard_map/ppermute | solution.py:270
  725.7 2.4 copy-start.16
  728.7 14.5 %collective-permute-start.2 = (bf16[160,2048]{1,0:T(8,128)(2,1)S(1)}, bf16[160,2048]{1,0:T(8,128)(2,1)S(1)}, u32[]{:S(2)}, u32[]{:S(2)}) collective-permute-start(bf16[160,2048]{1,0:T(8,128)(2,1)S(1)} %dynamic-slice_dynamic-update-slice_fusion.8), channel_id=1, source_target_pairs={{0,2},{1,3},{2,0},{3,1},{4,6},{5,7},{6,4},{7,5},{8,10},{9,11},{10,... | collective-permute-start | bytes 1966088 | tf_op jit(solution)/shard_map/ppermute | solution.py:270
  729.5 17.6 %copy-start.3 = (bf16[256,2048]{1,0:T(8,128)(2,1)S(1)}, bf16[256,2048]{1,0:T(8,128)(2,1)}, u32[]{:S(2)}) copy-start(bf16[256,2048]{1,0:T(8,128)(2,1)} %param.18) | copy-start | bytes 3145732
  729.5 17.6 %copy-start.14 = (f32[256,2048]{1,0:T(8,128)S(1)}, f32[256,2048]{1,0:T(8,128)}, u32[]{:S(2)}) copy-start(f32[256,2048]{1,0:T(8,128)} %get-tuple-element.43) | copy-start | bytes 6291460
  744.3 9.7 %collective-permute-start.3 = (bf16[320,2048]{1,0:T(8,128)(2,1)}, bf16[320,2048]{1,0:T(8,128)(2,1)}, u32[]{:S(2)}, u32[]{:S(2)}) collective-permute-start(bf16[320,2048]{1,0:T(8,128)(2,1)} %pad_maximum_fusion.3), channel_id=1, source_target_pairs={{0,1},{1,0},{2,3},{3,2},{4,5},{5,4},{6,7},{7,6},{8,9},{9,8},{10,11... | collective-permute-start | bytes 3932168 | tf_op jit(solution)/shard_map/ppermute | solution.py:274
  748.7 1.2 collective-permute-start.5
  750.0 3.5 collective-permute-start.6
  755.8 2.7 copy-start.7
  758.5 2.9 copy-start.15
  (8 other events, 11.8 us)

commit v4 on v0

--- a/solution.py
+++ b/solution.py
@@ -1,6 +1,10 @@
+import functools
+
 import jax
 import jax.numpy as jnp
 from jax import lax
+from jax.experimental import pallas as pl
+from jax.experimental.pallas import tpu as pltpu
 from jax.sharding import PartitionSpec as P
 
 HEAD_DIM = 128
@@ -9,6 +13,7 @@
 
 NORM_EPS = 1e-05
 MASK_FILL = -1e30
+MESH = pl.DeviceIdType.MESH
 
 
 def norm_rows(values):
@@ -253,6 +258,767 @@
     )
 
 
+def axes_of():
+    dp, z, t = lax.axis_index("dp"), lax.axis_index("seq"), lax.axis_index("tensor")
+    other_dp, chip, core = {"dp": 1 - dp}, {"tensor": lax.rem(t + 2, 4)}, {"tensor": t + 1 - 2 * lax.rem(t, 2)}
+    pair = {"seq": z + 1 - 2 * lax.rem(z, 2)}
+    return dp, z, t, other_dp, chip, core, pair
+
+
+class Copies:
+    def __init__(self, send, recv):
+        self.send, self.recv, self.all, self.came, self.left = send, recv, [], [], []
+
+    def make(self, src, dst, device):
+        i = len(self.all)
+        copy = pltpu.make_async_remote_copy(src_ref=src, dst_ref=dst, send_sem=self.send.at[i], recv_sem=self.recv.at[i], device_id=device, device_id_type=MESH)
+        self.all.append(copy)
+        return copy
+
+    def wait(self, *copies):
+        for copy in copies:
+            if not any(copy is done for done in self.came):
+                copy.wait_recv()
+                self.came.append(copy)
+
+    def finish(self):
+        self.wait(*self.all)
+        for copy in self.all:
+            copy.wait_send()
+
+
+def greet(peers):
+    barrier = pltpu.get_barrier_semaphore()
+    for peer in peers:
+        pl.semaphore_signal(barrier, inc=1, device_id=peer, device_id_type=MESH)
+    pl.semaphore_wait(barrier, len(peers))
+
+
+def front_kernel(
+    x_ref, w_query_ref, w_key_ref, w_value_ref, w_out_ref, w_up_ref, w_down_ref, gain_one_ref, gain_two_ref, cot_ref, bias_ref,
+    whole_ref, w_head_ref, qkv_ref, att_ref, lse_ref, attended_ref, out_ref, resid_ref, normed_ref, rate_ref, second_ref, up_ref, down_ref, cots_ref,
+    tokens, frames, w_own, w_head, up_own, out_all, att_low, came, part_low, core_in, half_low, chip_in, second, peak, total, acc, send, recv, local_sem,
+):
+    f32, bf16 = jnp.float32, jnp.bfloat16
+    dp, z, t, other_dp, chip, core, pair = axes_of()
+    rows, width = x_ref.shape
+    quarter, half = rows // 4, rows // 2
+    part, hidden = w_up_ref.shape
+    side = hidden // 2
+    copies = Copies(send, recv)
+    kept = []
+
+    def keep(src, dst):
+        copy = pltpu.make_async_copy(src, dst, local_sem.at[len(kept)])
+        kept.append(copy)
+        copy.start()
+        return copy
+
+    def along(k):
+        return {"seq": lax.rem(z + k + SEQ, SEQ)}
+
+    def owner(k):
+        return (dp * SEQ + lax.rem(z - k + SEQ, SEQ)) * part
+
+    mate = t + 1 - 2 * lax.rem(t, 2)
+    quarters = [t, lax.rem(t + 2, 4), mate, lax.rem(mate + 2, 4)]
+    load_tokens = [keep(x_ref.at[pl.ds(quarters[n] * quarter, quarter), :], tokens.at[pl.ds(n * quarter, quarter), :]) for n in range(4)]
+    keep_cots = [keep(cot_ref.at[pl.ds(quarters[n] * quarter, quarter), :], cots_ref.at[pl.ds(n * quarter, quarter), :]) for n in range(4)]
+    own_out = keep(w_out_ref, out_all.at[:, pl.ds(owner(0), part)])
+    keep(w_down_ref.at[pl.ds(lax.rem(z, 2) * side, side), :], down_ref.at[:, pl.ds(owner(0), part)])
+    greet([other_dp, chip, core] + [along(k) for k in range(1, SEQ)])
+
+    first = slice(0, quarter)
+
+    def rows_at(n, count=1):
+        return pl.ds(n * quarter, count * quarter)
+
+    token = [None] + [copies.make(frames.at[k - 1, rows_at(0), :], frames.at[k, rows_at(0), :], along(1)) for k in range(1, SEQ)]
+    token_chip = [None] + [copies.make(frames.at[k, rows_at(0), :], frames.at[k, rows_at(1), :], chip) for k in range(1, SEQ)]
+    token_core = [None] + [copies.make(frames.at[k, rows_at(0, 2), :], frames.at[k, rows_at(2, 2), :], core) for k in range(1, SEQ)]
+    head = [None] + [copies.make(w_own.at[lax.rem(z + k, SEQ)], w_head.at[pl.ds(owner(0), part), :], along(k)) for k in range(1, SEQ)]
+    mine = pl.ds(dp * SEQ * part, SEQ * part)
+    head_dp = copies.make(w_head.at[mine, :], w_head.at[mine, :], other_dp)
+
+    def gather(source, at):
+        step = [None] + [copies.make(source(lax.rem(z + k, 2)), at(owner(0)), along(k)) for k in range(1, SEQ)]
+        cross = [copies.make(at(owner(k)) if k else source(lax.rem(z, 2)), at(owner(k)), other_dp) for k in range(SEQ)]
+        return step, cross
+
+    out_step, out_dp = gather(lambda h: w_out_ref, lambda c: out_all.at[:, pl.ds(c, part)])
+    up_step, up_dp = gather(lambda h: up_own.at[h], lambda c: up_ref.at[pl.ds(c, part), :])
+    down_step, down_dp = gather(lambda h: w_down_ref.at[pl.ds(h * side, side), :], lambda c: down_ref.at[:, pl.ds(c, part)])
+    first_back = len(copies.all) - 1
+    back_home = [None] + [copies.make(att_low.at[k], came.at[k], along(-k)) for k in range(1, SEQ)]
+    sum_core = copies.make(part_low.at[rows_at(2, 2), :], core_in, core)
+    sum_chip = copies.make(half_low, chip_in, chip)
+    second_pair = copies.make(second.at[rows_at(0), :], second.at[rows_at(4), :], pair)
+    second_chip = [copies.make(second.at[rows_at(4 * n), :], second.at[rows_at(4 * n + 1), :], chip) for n in range(2)]
+    second_core = [copies.make(second.at[rows_at(4 * n, 2), :], second.at[rows_at(4 * n + 2, 2), :], core) for n in range(2)]
+    cot_pair = copies.make(cot_ref.at[pl.ds(t * quarter, quarter), :], cots_ref.at[rows_at(4), :], pair)
+    cot_chip = copies.make(cots_ref.at[rows_at(4), :], cots_ref.at[rows_at(5), :], chip)
+    cot_core = copies.make(cots_ref.at[rows_at(4, 2), :], cots_ref.at[rows_at(6, 2), :], core)
+
+    def norm_piece(n, carry):
+        values = tokens[rows_at(n), :].astype(f32)
+        center = values - jnp.mean(values, axis=1, keepdims=True)
+        frames[0, rows_at(n), :] = (center * lax.rsqrt(jnp.mean(center * center, axis=1, keepdims=True) + NORM_EPS)).astype(bf16)
+        return carry
+
+    out_dp[0].start()
+    out_step[1].start()
+    down_dp[0].start()
+    load_tokens[0].wait()
+    lax.fori_loop(0, 1, norm_piece, 0)
+    token[1].start()
+    gain = gain_one_ref[...]
+    for h in range(SEQ):
+        at = slice(h * HEAD_DIM, (h + 1) * HEAD_DIM)
+        for n, ref in enumerate((w_query_ref, w_key_ref, w_value_ref)):
+            w_own[h, :, n * HEAD_DIM : (n + 1) * HEAD_DIM] = (ref[:, at].astype(f32) * gain).astype(bf16)
+    for k in range(1, SEQ):
+        head[k].start()
+    w_head[pl.ds(owner(0), part), :] = w_own[z]
+    gain = gain_two_ref[...]
+    for h in range(2):
+        up_own[h] = (w_up_ref[:, h * side : (h + 1) * side].astype(f32) * gain).astype(bf16)
+    keep(up_own.at[lax.rem(z, 2)], up_ref.at[pl.ds(owner(0), part), :])
+    for copy in load_tokens[1:]:
+        copy.wait()
+    lax.fori_loop(1, 4, norm_piece, 0)
+    keep(frames.at[0], whole_ref.at[0])
+
+    def arrive(copy, *then):
+        copies.wait(copy)
+        for one in then:
+            one.start()
+
+    def project(k):
+        def piece(n, carry):
+            qkv_ref[k, rows_at(n), :] = jnp.dot(frames[k, rows_at(n), :], w_head[...], preferred_element_type=f32).astype(bf16)
+            return carry
+
+        lax.fori_loop(0, 4, piece, 0)
+
+    scale = HEAD_DIM ** (-0.5)
+
+    def query_frame(i):
+        at = lax.rem(z - i + SEQ, SEQ)
+        query = qkv_ref[at, :, 0:HEAD_DIM]
+        peak[...] = jnp.full_like(peak, MASK_FILL)
+        total[...] = jnp.zeros_like(total)
+        acc[...] = jnp.zeros_like(acc)
+
+        def key_frame(j, inner):
+            here = lax.rem(z - j + SEQ, SEQ)
+            scores = lax.dot_general(qkv_ref[here, :, HEAD_DIM : 2 * HEAD_DIM], query, (((1,), (1,)), ((), ())), preferred_element_type=f32) * scale + bias_ref[j]
+            before = peak[...]
+            after = jnp.maximum(before, jnp.max(scores, axis=0, keepdims=True))
+            terms = jnp.exp(scores - after)
+            fix = jnp.exp(before - after)
+            peak[...] = after
+            total[...] = total[...] * fix + jnp.sum(terms, axis=0, keepdims=True)
+            acc[...] = acc[...] * fix + lax.dot_general(qkv_ref[here, :, 2 * HEAD_DIM :], terms.astype(bf16), (((0,), (0,)), ((), ())), preferred_element_type=f32)
+            return inner
+
+        lax.fori_loop(0, i + 1, key_frame, 0)
+        outcome = (acc[...] / total[...]).T
+        att_ref[at] = outcome
+        att_low[at] = outcome.astype(bf16)
+        lse_ref[at] = peak[...] + jnp.log(total[...])
+
+        @pl.when(at != 0)
+        def _():
+            pltpu.make_async_remote_copy(
+                src_ref=att_low.at[at], dst_ref=came.at[at], send_sem=send.at[first_back + at], recv_sem=recv.at[first_back + at],
+                device_id={"seq": i}, device_id_type=MESH,
+            ).start()
+
+    def mix(start):
+        def piece(n, carry):
+            at = pl.ds(pl.multiple_of(n * 512, 512), 512)
+            part_low[pl.ds(start, half), at] = jnp.dot(attended_ref[pl.ds(start, half), :], out_all[:, at], preferred_element_type=f32).astype(bf16)
+            return carry
+
+        lax.fori_loop(0, width // 512, piece, 0)
+
+    arrive(out_step[1], out_step[2])
+    for k in range(1, SEQ):
+        copies.wait(head[k])
+    head_dp.start()
+    arrive(token[1], token[2], token_chip[1])
+    arrive(out_step[2], out_step[3])
+    out_dp[1].start()
+    out_dp[2].start()
+    arrive(token_chip[1], token_core[1])
+    copies.wait(head_dp)
+    keep(w_head, w_head_ref)
+    project(0)
+    arrive(out_step[3], out_dp[3], up_step[1])
+    up_dp[0].start()
+    arrive(token_core[1])
+    keep(frames.at[1], whole_ref.at[1])
+    project(1)
+    arrive(token[2], token[3], token_chip[2])
+    arrive(token_chip[2], token_core[2])
+    arrive(token_core[2])
+    keep(frames.at[2], whole_ref.at[2])
+    project(2)
+    arrive(up_step[1], up_step[2], up_dp[1])
+    arrive(token[3], token_chip[3])
+    arrive(up_step[2], up_step[3], up_dp[2])
+    arrive(token_chip[3], token_core[3])
+    arrive(token_core[3])
+    keep(frames.at[3], whole_ref.at[3])
+    project(3)
+    query_frame(0)
+    query_frame(1)
+    query_frame(2)
+    query_frame(3)
+    came[0] = att_low[0]
+    arrive(up_step[3], up_dp[3], cot_pair)
+    copies.wait(*back_home[1:])
+    for h in range(SEQ):
+        attended_ref[:, h * HEAD_DIM : (h + 1) * HEAD_DIM] = came[lax.rem(h - z + SEQ, SEQ)]
+    own_out.wait()
+    copies.wait(*out_dp)
+    keep(out_all, out_ref)
+
+    mix(half)
+    sum_core.start()
+    mix(0)
+    arrive(cot_pair, cot_chip, down_step[1])
+    copies.wait(sum_core)
+    half_low[...] = (part_low[quarter:half, :].astype(f32) + core_in[quarter:half, :].astype(f32)).astype(bf16)
+    sum_chip.start()
+    arrive(down_step[1], down_step[2], down_dp[1])
+    arrive(cot_chip, cot_core)
+    copies.wait(sum_chip)
+    resid = tokens[first, :].astype(f32) + (part_low[first, :].astype(f32) + core_in[first, :].astype(f32)) + chip_in[...].astype(f32)
+    center = resid - jnp.mean(resid, axis=1, keepdims=True)
+    rate = lax.rsqrt(jnp.mean(center * center, axis=1, keepdims=True) + NORM_EPS)
+    normed = center * rate
+    second[first, :] = normed.astype(bf16)
+    second_pair.start()
+    second_chip[0].start()
+    resid_ref[...] = resid
+    rate_ref[...] = rate
+    normed_ref[...] = normed
+    arrive(down_step[2], down_step[3], down_dp[2])
+    arrive(second_chip[0], second_core[0])
+    arrive(second_pair, second_chip[1])
+    arrive(down_step[3], down_dp[3])
+    arrive(second_chip[1], second_core[1])
+    copies.wait(*second_core)
+    keep(second, second_ref)
+    copies.finish()
+    for copy in kept:
+        if not any(copy is done for done in [own_out] + load_tokens):
+            copy.wait()
+
+
+def front(x, w_query, w_key, w_value, w_out, w_up, w_down, gain_one, gain_two, cot, bias):
+    rows, width = x.shape
+    quarter, half = rows // 4, rows // 2
+    part, hidden = w_up.shape
+    inner = w_out.shape[0]
+    three = 3 * HEAD_DIM
+    f32, bf16 = jnp.float32, jnp.bfloat16
+    any_, vmem = pl.BlockSpec(memory_space=pl.ANY), pl.BlockSpec(memory_space=pltpu.VMEM)
+    shape = jax.ShapeDtypeStruct
+    outs = [
+        (shape((SEQ, rows, width), bf16), any_),
+        (shape((width, three), bf16), any_),
+        (shape((SEQ, rows, three), bf16), vmem),
+        (shape((SEQ, rows, HEAD_DIM), f32), vmem),
+        (shape((SEQ, 1, rows), f32), vmem),
+        (shape((rows, inner), bf16), vmem),
+        (shape((inner, width), bf16), any_),
+        (shape((quarter, width), f32), vmem),
+        (shape((quarter, width), f32), vmem),
+        (shape((quarter, 1), f32), vmem),
+        (shape((2 * rows, width), bf16), any_),
+        (shape((width, hidden // 2), bf16), any_),
+        (shape((hidden // 2, width), bf16), any_),
+        (shape((2 * rows, width), bf16), any_),
+    ]
+    scratch = [
+        ((rows, width), bf16),
+        ((SEQ, rows, width), bf16),
+        ((SEQ, part, three), bf16),
+        ((width, three), bf16),
+        ((2, part, hidden // 2), bf16),
+        ((inner, width), bf16),
+        ((SEQ, rows, HEAD_DIM), bf16),
+        ((SEQ, rows, HEAD_DIM), bf16),
+        ((rows, width), bf16),
+        ((half, width), bf16),
+        ((quarter, width), bf16),
+        ((quarter, width), bf16),
+        ((2 * rows, width), bf16),
+        ((1, rows), f32),
+        ((1, rows), f32),
+        ((HEAD_DIM, rows), f32),
+    ]
+    count = 3 * 3 + 4 + 3 * 7 + 3 + 2 + 5 + 3
+    return pl.pallas_call(
+        front_kernel,
+        out_shape=[o[0] for o in outs],
+        in_specs=[any_] + [vmem] * 3 + [any_, vmem, any_, vmem, vmem, any_, vmem],
+        out_specs=[o[1] for o in outs],
+        scratch_shapes=[pltpu.VMEM(*one) for one in scratch] + [pltpu.SemaphoreType.DMA((count,)), pltpu.SemaphoreType.DMA((count,)), pltpu.SemaphoreType.DMA((24,))],
+        compiler_params=pltpu.CompilerParams(collective_id=0, has_side_effects=True, vmem_limit_bytes=58 * 2**20),
+        cost_estimate=pl.CostEstimate(flops=8 * 10**9, bytes_accessed=50 * 10**6, transcendentals=5 * 10**6),
+    )(x, w_query, w_key, w_value, w_out, w_up, w_down, gain_one, gain_two, cot, bias)
+
+
+def back_kernel(
+    gd_ref, gd_came_ref, gu_ref, dn_ref, ff_ref, resid_ref, cots_ref, normed_two_ref, rate_two_ref, attended_ref, out_ref, qkv_ref, att_ref, lse_ref, bias_ref, w_head_ref, whole_ref, x_ref,
+    down_sum_ref, up_sum_ref, out_sum_ref, arrived_ref, grad_in_ref, result_ref, cross_up_ref, far_down_ref, far_up_ref, dn_core_ref, dn_chip_ref, ff_core_ref, ff_chip_ref, pair_ref, first_core_ref, first_chip_ref, first_ring_ref,
+    frames, temp, box_down, box_up, mix, d_head, d_out, dq, dk, dv, delta, d_three, out_send, out_cross, out_far, out_box,
+    head_acc, head_low, head_cross, head_sum, held_a, held_b, half_box, pair_box, mid, quart_box, in_box, own_box,
+    send, recv, keep_sem, load_sem,
+):
+    f32, bf16 = jnp.float32, jnp.bfloat16
+    dp, z, t, other_dp, chip, core, pair = axes_of()
+    rows, width = whole_ref.shape[1:]
+    quarter, half = rows // 4, rows // 2
+    part = width // (2 * SEQ)
+    side = gd_ref.shape[1]
+    copies = Copies(send, recv)
+    scale = HEAD_DIM ** (-0.5)
+    first, later = slice(0, quarter), slice(quarter, half)
+
+    def along(k):
+        return {"seq": lax.rem(z + k + SEQ, SEQ)}
+
+    def load(*pairs):
+        moves = [pltpu.make_async_copy(src, dst, load_sem.at[i]) for i, (src, dst) in enumerate(pairs)]
+        for move in moves:
+            move.start()
+        for move in moves:
+            move.wait()
+
+    def block(side_dp, k):
+        return pl.multiple_of((side_dp * SEQ + lax.rem(z - k + SEQ, SEQ)) * part, part)
+
+    def rows_at(n, count=1):
+        return pl.ds(n * quarter, count * quarter)
+
+    greet([other_dp, chip, core] + [along(k) for k in range(1, SEQ)])
+
+    def sums(part_ref, core_ref, chip_ref, n):
+        to_core = [copies.make(part_ref.at[rows_at(4 * i + 2, 2), :], core_ref.at[i], core) for i in range(2)]
+        to_chip = [copies.make(half_box.at[2 * n + i], chip_ref.at[i], chip) for i in range(2)]
+        to_pair = copies.make(pair_box.at[n], pair_ref.at[n], pair)
+        return to_core, to_chip, to_pair
+
+    dn_core, dn_chip, dn_pair = sums(dn_ref, dn_core_ref, dn_chip_ref, 0)
+    ff_core, ff_chip, ff_pair = sums(ff_ref, ff_core_ref, ff_chip_ref, 1)
+    mix_chip = copies.make(mix.at[rows_at(0), :], mix.at[rows_at(1), :], chip)
+    mix_core = copies.make(mix.at[rows_at(0, 2), :], mix.at[rows_at(2, 2), :], core)
+    spread = [None] + [copies.make(d_head.at[lax.rem(z + k, SEQ)], d_out.at[k], along(k)) for k in range(1, SEQ)]
+    cross_up = [copies.make(gu_ref.at[pl.ds(block(1 - dp, k), part), :], cross_up_ref.at[k], other_dp) for k in range(SEQ)]
+    cross_out = [copies.make(out_send.at[k], out_cross.at[k], other_dp) for k in range(SEQ)]
+    far_down = [None] + [copies.make(box_down.at[k - 1], far_down_ref.at[k - 1], along(-k)) for k in range(1, SEQ)]
+    far_up = [None] + [copies.make(box_up.at[k - 1], far_up_ref.at[k - 1], along(-k)) for k in range(1, SEQ)]
+    far_out = [None] + [copies.make(out_box.at[k - 1], out_far.at[k - 1], along(-k)) for k in range(1, SEQ)]
+    first_core = [copies.make(frames.at[k, rows_at(2, 2), :], first_core_ref.at[k], core) for k in range(SEQ)]
+    first_chip = [copies.make(quart_box.at[k], first_chip_ref.at[k], chip) for k in range(SEQ)]
+    first_ring = [None] + [copies.make(in_box.at[k - 1], first_ring_ref.at[k - 1], along(1)) for k in range(1, SEQ)]
+    head_dp = copies.make(head_low.at[1 - dp], head_cross, other_dp)
+    head_out = [None] + [copies.make(head_sum.at[lax.rem(z + k, SEQ)], arrived_ref.at[k], along(k)) for k in range(1, SEQ)]
+    kept = []
+
+    def publish(n, ref):
+        mine = ref.at[pl.ds(t * quarter, quarter), :]
+        mate = ref.at[pl.ds(lax.rem(t + 2, 4) * quarter, quarter), :]
+        return [copies.make(own_box.at[n], mine, chip), copies.make(own_box.at[n], mine, core), copies.make(mate, mate, core)], (own_box.at[n], mine)
+
+    result_out, result_own = publish(0, result_ref)
+    grad_out_copies, grad_own = publish(1, grad_in_ref)
+
+    def keep(src, dst):
+        move = pltpu.make_async_copy(src, dst, keep_sem.at[SEQ + len(kept)])
+        kept.append(move)
+        move.start()
+
+    def half_of(part_ref, core_ref, to_core, to_chip, i, n):
+        copies.wait(to_core[i])
+        load((part_ref.at[rows_at(4 * i + 1), :], held_a.at[rows_at(0), :]), (core_ref.at[i, rows_at(1), :], held_a.at[rows_at(1), :]))
+        half_box[2 * n + i] = (held_a[first, :].astype(f32) + held_a[later, :].astype(f32)).astype(bf16)
+        to_chip[i].start()
+
+    def quarter_of(part_ref, core_ref, chip_ref, to_chip, i, *more):
+        copies.wait(to_chip[i])
+        load(
+            (part_ref.at[rows_at(4 * i), :], held_a.at[rows_at(0), :]), (core_ref.at[i, rows_at(0), :], held_a.at[rows_at(1), :]), (chip_ref.at[i], held_b.at[rows_at(0), :]),
+            *more,
+        )
+        return (held_a[first, :].astype(f32) + held_a[later, :].astype(f32)) + held_b[first, :].astype(f32)
+
+    def pair_sum(part_ref, core_ref, chip_ref, to_chip, to_pair, n):
+        pair_box[n] = quarter_of(part_ref, core_ref, chip_ref, to_chip, 1).astype(bf16)
+        to_pair.start()
+
+    def own_sum(part_ref, core_ref, chip_ref, to_chip, to_pair, n, extra):
+        copies.wait(to_pair)
+        total = quarter_of(part_ref, core_ref, chip_ref, to_chip, 0, (pair_ref.at[n], held_b.at[rows_at(1), :]), (extra, spare))
+        return total + held_b[later, :].astype(f32)
+
+    def scatter(k, own_ref, cross_at, crossing, box, far):
+        if crossing is not None:
+            copies.wait(crossing)
+        load((cross_at, temp.at[0]), (own_ref.at[pl.ds(block(dp, k), part), :], temp.at[1]))
+        box[k - 1] = (temp[0].astype(f32) + temp[1].astype(f32)).astype(bf16)
+        far[k].start()
+
+    def down_block(k):
+        return gd_came_ref.at[pl.ds(pl.multiple_of(lax.rem(z - k + SEQ, SEQ) * part, part), part), :]
+
+    def scatter_down(k):
+        scatter(k, gd_ref, down_block(k), None, box_down, far_down)
+
+    def scatter_up(k):
+        scatter(k, gu_ref, cross_up_ref.at[k], cross_up[k], box_up, far_up)
+
+    same = pl.multiple_of(lax.rem(z, 2) * side, side)
+    unlike = pl.multiple_of((1 - lax.rem(z, 2)) * side, side)
+
+    def total_of(own_ref, cross_at, far_ref, far, crossing, store):
+        copies.wait(*far[1:])
+        if crossing is not None:
+            copies.wait(crossing)
+        load((cross_at, temp.at[0]), (own_ref.at[pl.ds(block(dp, 0), part), :], temp.at[1]), (far_ref.at[1], temp.at[2]))
+        store(same, lambda at: (temp[0, :, at].astype(f32) + temp[1, :, at].astype(f32)) + temp[2, :, at].astype(f32))
+        load((far_ref.at[0], temp.at[0]), (far_ref.at[2], temp.at[1]))
+        store(unlike, lambda at: temp[0, :, at].astype(f32) + temp[1, :, at].astype(f32))
+
+    def store_turned(base, value):
+        for n in range(side // 256):
+            down_sum_ref[pl.ds(base + n * 256, 256), :] = value(slice(n * 256, (n + 1) * 256)).T
+
+    def store_plain(base, value):
+        up_sum_ref[:, pl.ds(base, side)] = value(slice(0, side))
+
+    def out_block(start):
+        return lax.dot_general(attended_ref[...], mix[:, pl.ds(start, part)], (((0,), (0,)), ((), ())), preferred_element_type=f32)
+
+    def scatter_out(k):
+        copies.wait(cross_out[k])
+        out_box[k - 1] = (out_block(block(dp, k)) + out_cross[k].astype(f32)).astype(bf16)
+        far_out[k].start()
+
+    for copy in (dn_core[1], dn_core[0], cross_up[1], cross_up[2]):
+        copy.start()
+    spare = head_acc.at[pl.ds(0, quarter), :]
+    scatter_down(1)
+    half_of(dn_ref, dn_core_ref, dn_core, dn_chip, 1, 0)
+    load(*[(out_ref.at[pl.ds(h * HEAD_DIM, HEAD_DIM), :], quart_box.at[h, pl.ds(0, HEAD_DIM), :]) for h in range(SEQ)])
+    scatter_down(2)
+    fetch = [pltpu.make_async_copy(whole_ref.at[k], frames.at[k], keep_sem.at[k]) for k in range(SEQ)]
+    for move in fetch:
+        move.start()
+    copies.wait(dn_chip[1])
+    half_of(dn_ref, dn_core_ref, dn_core, dn_chip, 0, 0)
+    pair_sum(dn_ref, dn_core_ref, dn_chip_ref, dn_chip, dn_pair, 0)
+    grad = own_sum(dn_ref, dn_core_ref, dn_chip_ref, dn_chip, dn_pair, 0, normed_two_ref)
+    normed = spare[...]
+    grad = rate_two_ref[...] * (grad - jnp.mean(grad, axis=1, keepdims=True) - normed * jnp.mean(grad * normed, axis=1, keepdims=True))
+    load((cots_ref.at[rows_at(0), :], held_a.at[rows_at(0), :]))
+    grad = held_a[first, :].astype(f32) + grad
+    mid[...] = grad
+    mix[first, :] = grad.astype(bf16)
+    mix_chip.start()
+    scatter_down(3)
+    copies.wait(cross_up[1], cross_up[2])
+    cross_up[3].start()
+    cross_up[0].start()
+    copies.wait(mix_chip)
+    mix_core.start()
+    copies.wait(mix_core)
+
+    for n in range(4):
+        at = slice(n * quarter, (n + 1) * quarter)
+        for h in range(SEQ):
+            d_head[h, at, :] = lax.dot_general(mix[at, :], quart_box[h, 0:HEAD_DIM, :], (((1,), (1,)), ((), ())), preferred_element_type=f32).astype(bf16)
+    for k in range(1, SEQ):
+        spread[k].start()
+    ff_core[1].start()
+    ff_core[0].start()
+    d_out[0] = d_head[z]
+    for k in (1, 2, 3, 0):
+        out_send[k] = out_block(block(1 - dp, k)).astype(bf16)
+        cross_out[k].start()
+    half_of(ff_ref, ff_core_ref, ff_core, ff_chip, 1, 1)
+    copies.wait(*spread[1:])
+    dq[...] = jnp.zeros_like(dq)
+    for f in range(SEQ):
+        delta[f] = jnp.sum((d_out[f].astype(f32) * att_ref[f]).T, axis=0, keepdims=True)
+
+    def key_frame(j):
+        here = lax.rem(z - j + SEQ, SEQ)
+        dk[...] = jnp.zeros_like(dk)
+        dv[...] = jnp.zeros_like(dv)
+
+        def query_frame(i, inner_):
+            at = lax.rem(z - i + SEQ, SEQ)
+            query, key, value = qkv_ref[at, :, :HEAD_DIM], qkv_ref[here, :, HEAD_DIM : 2 * HEAD_DIM], qkv_ref[here, :, 2 * HEAD_DIM :]
+            grad_out = d_out[at]
+            scores = lax.dot_general(key, query, (((1,), (1,)), ((), ())), preferred_element_type=f32) * scale + bias_ref[j]
+            prob = jnp.exp(scores - lse_ref[at])
+            d_prob = lax.dot_general(value, grad_out, (((1,), (1,)), ((), ())), preferred_element_type=f32)
+            d_scores = (prob * (d_prob - delta[at])).astype(bf16)
+            dv[...] += jnp.dot(prob.astype(bf16), grad_out, preferred_element_type=f32)
+            dk[...] += jnp.dot(d_scores, query, preferred_element_type=f32)
+            dq[at] += lax.dot_general(key, d_scores, (((0,), (0,)), ((), ())), preferred_element_type=f32)
+            return inner_
+
+        lax.fori_loop(j, SEQ, query_frame, 0)
+        d_three[here, :, HEAD_DIM : 2 * HEAD_DIM] = (dk[...] * scale).astype(bf16)
+        d_three[here, :, 2 * HEAD_DIM :] = dv[...].astype(bf16)
+
+    key_frame(0)
+    scatter_up(1)
+    key_frame(1)
+    half_of(ff_ref, ff_core_ref, ff_core, ff_chip, 0, 1)
+    scatter_up(2)
+    key_frame(2)
+    key_frame(3)
+    for f in range(SEQ):
+        d_three[f, :, :HEAD_DIM] = (dq[f] * scale).T.astype(bf16)
+
+    def project_back(k):
+        fetch[k].wait()
+
+        def piece(n, carry):
+            at = pl.ds(pl.multiple_of(n * 512, 512), 512)
+            term = lax.dot_general(d_three[k], frames[k, :, at], (((0,), (0,)), ((), ())), preferred_element_type=f32)
+            head_acc[:, at] = term if k == 1 else head_acc[:, at] + term
+            return carry
+
+        lax.fori_loop(0, width // 512, piece, 0)
+
+        def back_piece(n, carry):
+            at = pl.ds(pl.multiple_of(n * 512, 512), 512)
+            frames[k, :, at] = lax.dot_general(d_three[k], w_head_ref[at, :], (((1,), (1,)), ((), ())), preferred_element_type=f32).astype(bf16)
+            return carry
+
+        lax.fori_loop(0, width // 512, back_piece, 0)
+        first_core[k].start()
+
+    def half_sum(k):
+        copies.wait(first_core[k])
+        load((first_core_ref.at[k], held_a))
+        quart_box[k] = (frames[k, later, :].astype(f32) + held_a[later, :].astype(f32)).astype(bf16)
+        first_chip[k].start()
+        frames[k, first, :] = (frames[k, first, :].astype(f32) + held_a[first, :].astype(f32)).astype(bf16)
+
+    def quarter_sum(k):
+        copies.wait(first_chip[k])
+        pairs = [(first_chip_ref.at[k], held_a.at[rows_at(0), :])]
+        if k != 1:
+            before = (k - 1) % SEQ
+            copies.wait(first_ring[before])
+            pairs.append((first_ring_ref.at[before - 1], held_a.at[rows_at(1), :]))
+        load(*pairs)
+        sum_ = frames[k, first, :].astype(f32) + held_a[first, :].astype(f32)
+        if k != 1:
+            sum_ = sum_ + held_a[later, :].astype(f32)
+        return sum_
+
+    project_back(1)
+    project_back(2)
+    half_sum(1)
+    project_back(3)
+    project_back(0)
+    for n in range(2):
+        head_low[n] = head_acc[:, n * (width // 2) : (n + 1) * (width // 2)].astype(bf16)
+    head_dp.start()
+    scatter_up(3)
+    copies.wait(first_chip[1])
+    half_sum(2)
+    in_box[0] = quarter_sum(1).astype(bf16)
+    first_ring[1].start()
+    total_of(gd_ref, down_block(0), far_down_ref, far_down, None, store_turned)
+    scatter_out(1)
+    copies.wait(first_chip[2])
+    half_sum(3)
+    in_box[1] = quarter_sum(2).astype(bf16)
+    first_ring[2].start()
+    copies.wait(head_dp)
+    for j in range(SEQ):
+        at = slice(j * part, (j + 1) * part)
+        head_sum[j] = (head_low[dp, :, at].astype(f32) + head_cross[:, at].astype(f32)).astype(bf16)
+    for k in range(1, SEQ):
+        head_out[k].start()
+    keep(head_sum.at[z], arrived_ref.at[0])
+    scatter_out(2)
+    copies.wait(first_chip[3])
+    half_sum(0)
+    in_box[2] = quarter_sum(3).astype(bf16)
+    first_ring[3].start()
+    scatter_out(3)
+    pair_sum(ff_ref, ff_core_ref, ff_chip_ref, ff_chip, ff_pair, 1)
+    total_of(gu_ref, cross_up_ref.at[0], far_up_ref, far_up, cross_up[0], store_plain)
+    grad = quarter_sum(0)
+    load((x_ref.at[pl.ds(t * quarter, quarter), :], held_a.at[rows_at(0), :]))
+    center = held_a[first, :].astype(f32)
+    center = center - jnp.mean(center, axis=1, keepdims=True)
+    rate = lax.rsqrt(jnp.mean(center * center, axis=1, keepdims=True) + NORM_EPS)
+    normed = center * rate
+    grad = rate * (grad - jnp.mean(grad, axis=1, keepdims=True) - normed * jnp.mean(grad * normed, axis=1, keepdims=True))
+    own_box[1] = (mid[...] + grad).astype(bf16)
+    grad_out_copies[0].start()
+    grad_out_copies[1].start()
+    keep(*grad_own)
+    total = own_sum(ff_ref, ff_core_ref, ff_chip_ref, ff_chip, ff_pair, 1, resid_ref)
+    own_box[0] = (spare[...] + total).astype(bf16)
+    result_out[0].start()
+    result_out[1].start()
+    keep(*result_own)
+    copies.wait(cross_out[0], *far_out[1:])
+    sum_ = out_block(block(dp, 0)) + out_cross[0].astype(f32)
+    for k in range(1, SEQ):
+        sum_ = sum_ + out_far[k - 1].astype(f32)
+    out_sum_ref[...] = sum_
+    copies.wait(grad_out_copies[0])
+    grad_out_copies[2].start()
+    copies.wait(result_out[0])
+    result_out[2].start()
+    copies.finish()
+    for move in kept:
+        move.wait()
+
+
+def back(gd, gd_came, gu, dn, ff, resid, cots, normed_two, rate_two, attended, out_rel, qkv, att, lse, bias, w_head, whole, x):
+    rows, width = x.shape
+    quarter, half = rows // 4, rows // 2
+    part = width // (2 * SEQ)
+    inner = attended.shape[1]
+    side = gd.shape[1]
+    three = 3 * HEAD_DIM
+    f32, bf16 = jnp.float32, jnp.bfloat16
+    any_, vmem = pl.BlockSpec(memory_space=pl.ANY), pl.BlockSpec(memory_space=pltpu.VMEM)
+    shape = jax.ShapeDtypeStruct
+    outs = [
+        (shape((2 * side, part), f32), vmem),
+        (shape((part, 2 * side), f32), vmem),
+        (shape((inner, part), f32), vmem),
+        (shape((SEQ, three, part), bf16), any_),
+        (shape((rows, width), bf16), any_),
+        (shape((rows, width), bf16), any_),
+        (shape((SEQ, part, side), bf16), any_),
+        (shape((SEQ - 1, part, side), bf16), any_),
+        (shape((SEQ - 1, part, side), bf16), any_),
+        (shape((2, half, width), bf16), any_),
+        (shape((2, quarter, width), bf16), any_),
+        (shape((2, half, width), bf16), any_),
+        (shape((2, quarter, width), bf16), any_),
+        (shape((2, quarter, width), bf16), any_),
+        (shape((SEQ, half, width), bf16), any_),
+        (shape((SEQ, quarter, width), bf16), any_),
+        (shape((SEQ - 1, quarter, width), bf16), any_),
+    ]
+    count = 10 + 2 + 3 + 4 + 4 + 9 + 8 + 3 + 4 + 6
+    scratch = [
+        ((SEQ, rows, width), bf16),
+        ((3, part, side), bf16),
+        ((SEQ - 1, part, side), bf16),
+        ((SEQ - 1, part, side), bf16),
+        ((rows, width), bf16),
+        ((SEQ, rows, HEAD_DIM), bf16),
+        ((SEQ, rows, HEAD_DIM), bf16),
+        ((SEQ, HEAD_DIM, rows), f32),
+        ((rows, HEAD_DIM), f32),
+        ((rows, HEAD_DIM), f32),
+        ((SEQ, 1, rows), f32),
+        ((SEQ, rows, three), bf16),
+        ((SEQ, inner, part), bf16),
+        ((SEQ, inner, part), bf16),
+        ((SEQ - 1, inner, part), bf16),
+        ((SEQ - 1, inner, part), bf16),
+        ((three, width), f32),
+        ((2, three, width // 2), bf16),
+        ((three, width // 2), bf16),
+        ((SEQ, three, part), bf16),
+        ((half, width), bf16),
+        ((half, width), bf16),
+        ((4, quarter, width), bf16),
+        ((2, quarter, width), bf16),
+        ((quarter, width), f32),
+        ((SEQ, quarter, width), bf16),
+        ((SEQ - 1, quarter, width), bf16),
+        ((2, quarter, width), bf16),
+    ]
+    return pl.pallas_call(
+        back_kernel,
+        out_shape=[o[0] for o in outs],
+        in_specs=[any_] * 8 + [vmem, vmem, any_] + [vmem] * 5 + [any_] * 2,
+        out_specs=[o[1] for o in outs],
+        scratch_shapes=[pltpu.VMEM(*one) for one in scratch]
+        + [pltpu.SemaphoreType.DMA((count,)), pltpu.SemaphoreType.DMA((count,)), pltpu.SemaphoreType.DMA((SEQ + 3,)), pltpu.SemaphoreType.DMA((6,))],
+        compiler_params=pltpu.CompilerParams(collective_id=1, has_side_effects=True, vmem_limit_bytes=62 * 2**20),
+        cost_estimate=pl.CostEstimate(flops=20 * 10**9, bytes_accessed=60 * 10**6, transcendentals=5 * 10**6),
+    )(gd, gd_came, gu, dn, ff, resid, cots, normed_two, rate_two, attended, out_rel, qkv, att, lse, bias, w_head, whole, x)[:6]
+
+
+def swap_dp(values):
+    return lax.ppermute(values, "dp", [(0, 1), (1, 0)])
+
+
+def swap_chip(values):
+    return lax.ppermute(values, "tensor", [(i, i ^ 2) for i in range(4)])
+
+
+def swap_core(values):
+    return lax.ppermute(values, "tensor", [(i, i ^ 1) for i in range(4)])
+
+
+def dyn(stack, index):
+    return lax.dynamic_index_in_dim(stack, index, 0, keepdims=False)
+
+
+def mm(left, right, dims=((1,), (0,)), out=jnp.bfloat16):
+    return lax.dot_general(left, right, (dims, ((), ())), preferred_element_type=jnp.float32).astype(out)
+
+
+def local_fast(inputs, first_gain, w_query, w_key, w_value, w_out, second_gain, w_up, w_down, frame_mask, cotangent):
+    dp, z = lax.axis_index("dp"), lax.axis_index("seq")
+    rows, width = inputs.shape[1:]
+    heads = w_query.shape[1] // HEAD_DIM
+    f32, bf16 = jnp.float32, jnp.bfloat16
+    gain_one, gain_two = first_gain.astype(f32)[:, None], second_gain.astype(f32)[:, None]
+    bias = jnp.broadcast_to(jnp.where(frame_mask[0] == 1, 0.0, MASK_FILL).astype(f32)[:, None, None], (SEQ, 1, rows))
+    whole, w_head, qkv, attended_f, lse, attended, out_all, resid_mid, normed_two, rate_two, second_in, up_side, down_side, cots = front(
+        inputs[0], w_query, w_key, w_value, w_out, w_up, w_down, gain_one, gain_two, cotangent[0], bias
+    )
+    up_pre = mm(second_in, up_side, out=f32)
+    cdf = 0.5 * (1.0 + lax.erf(up_pre * (0.5**0.5)))
+    up_act = (up_pre * cdf).astype(bf16)
+    slope = cdf + up_pre * jnp.exp(-0.5 * up_pre * up_pre) * ((2.0 * jnp.pi) ** -0.5)
+    grad_down = mm(cots, up_act, ((0,), (0,)))
+    down_came = swap_dp(lax.dynamic_slice_in_dim(grad_down, (1 - dp) * (width // 2), width // 2, 0))
+    d_up = (mm(cots, down_side, ((1,), (1,)), f32) * slope).astype(bf16)
+    grad_up = mm(second_in, d_up, ((0,), (0,)))
+    d_normed_two = mm(d_up, up_side, ((1,), (1,)))
+    ff_part = mm(up_act, down_side)
+    down_sum, up_raw, out_sum, arrived, grad_in, result = back(
+        grad_down, down_came, grad_up, d_normed_two, ff_part, resid_mid, cots, normed_two, rate_two, attended, out_all, qkv, attended_f, lse, bias, w_head, whole, inputs[0]
+    )
+    by_head = [dyn(arrived, lax.rem(z - h + SEQ, SEQ)).astype(f32).T for h in range(heads)]
+    raw = [jnp.concatenate([one[:, n * HEAD_DIM : (n + 1) * HEAD_DIM] for one in by_head], axis=1) for n in range(3)]
+    d_gain_one = sum(jnp.sum(weight.astype(f32) * one, axis=1) for weight, one in zip((w_query, w_key, w_value), raw))
+    d_gain_two = jnp.sum(w_up.astype(f32) * up_raw, axis=1)
+    gains = jnp.stack([d_gain_one, d_gain_two])
+    gains = gains + swap_core(gains)
+    gains = gains + swap_chip(gains)
+    return (result[None], grad_in[None], gains[0], raw[0] * gain_one, raw[1] * gain_one, raw[2] * gain_one, out_sum, gains[1], up_raw * gain_two, down_sum)
+
+
+SEQ = 4
+
+
 def solution(mesh):
     placed = (
         P("dp", "seq", None),
@@ -267,8 +1033,10 @@
         P("dp", None),
         P("dp", "seq", None),
     )
+    sizes = dict(mesh.shape)
+    spread = sizes == {"dp": 2, "seq": SEQ, "tensor": 4}
     return jax.shard_map(
-        local,
+        local_fast if spread else local,
         mesh=mesh,
         in_specs=placed,
         out_specs=(

time: 1620 us -> 609 us (0.38)
  waiting for transfers between devices: 1220 us -> 3.81 us
  Pallas kernels: 0 us -> 504 us
  matrix products: 209 us -> 59.6 us
  blocking collectives: 62.5 us -> 0 us
  other arithmetic: 53.4 us -> 6.66 us
  local copies, waits for them, and re-layouts: 47.7 us -> 20.4 us
    reduce_scatter x7 -> x0, waiting for transfers between devices: 553 us -> none  [the longest x1 150 us: local(): lax.psum_scatter(grad_up.astype(jnp.bfloat16), ('dp', 'seq'), scatter_dim...]
    pallas_call x0 -> x2, Pallas kernels: none -> 504 us  [the longest x1 260 us: back(): pl.pallas_call(back_kernel, out_shape=[o[0] for o in outs], in_specs=[any...]
    all_gather x8 -> x0, waiting for transfers between devices: 462 us -> none  [the longest x1 123 us: local(): lax.all_gather(w_up, ('dp', 'seq'), axis=0, tiled=True)]
    psum x3 -> x0, waiting for transfers between devices: 196 us -> none  [heads_total(): return lax.psum(values.astype(jnp.bfloat16), 'tensor').astype(jnp.float32)]
    dot_general x34 -> x6, matrix products: 209 us -> 59.6 us  [mm(): lax.dot_general(left, right, (dims, ((), ())), preferred_element_type=jnp...]
    all_gather x2 -> x0, blocking collectives: 40 us -> none  [the longest x1 22.3 us: local(): lax.all_gather(first_gain, ('dp', 'seq'), axis=0, tiled=True)]
    unnamed x1 -> x0, blocking collectives: 22.5 us -> none
    reduce_sum x9 -> x0, other arithmetic: 21.2 us -> none  [the longest x3 6.8 us: norm_rows(): center = values - jnp.mean(values, axis=-1, keepdims=True)]
  transfers between devices with their start and end apart: 18 -> 3, of which waited for: 18 -> 2; matrix products, arithmetic and copies ran while one was open for 12% -> 8% of each run, Pallas kernels for 0% -> 0%
where the time goes in v4:
time: 609 us; the launch traced here: 599 us
  Pallas kernels  504 us (83%)
  matrix products  59.6 us (10%)
  local copies, waits for them, and re-layouts  20.4 us (3%)
  other arithmetic  6.66 us (1%)
    pallas_call x1, Pallas kernels, back(): pl.pallas_call(back_kernel, out_shape=[o[0] for o in outs], in_specs=[any...  260 us
    pallas_call x1, Pallas kernels, front(): pl.pallas_call(front_kernel, out_shape=[o[0] for o in outs], in_specs=[an...  245 us
    dot_general x6, matrix products, mm(): lax.dot_general(left, right, (dims, ((), ())), preferred_element_type=jnp...  59.6 us
    unnamed x32, local copies, waits for them, and re-layouts  15.6 us
  transfers between devices with their start and end apart: 3, of which 2 were waited for; matrix products, arithmetic and copies ran while one was open for 8% of the time, Pallas kernels for 0%

profile of v4, /device:TPU:0, one launch (start us, length us, event | category | flops | bytes accessed | tf_op | source)
XLA Modules:
  0.0 599.1 jit_solution(7625682854985704860)
XLA Ops:
  2.8 0.8 copy.28.gain_two_ref
  4.9 244.7 %shard_map.186 = (bf16[4,640,2048]{2,1,0:T(8,128)(2,1)}, bf16[2048,384]{1,0:T(8,128)(2,1)}, bf16[4,640,384]{2,1,0:T(8,128)(2,1)}, f32[4,640,128]{2,1,0:T(8,128)}...) custom-call(bf16[640,2048]{1,0:T(8,128)(2,1)} %bitcast.57, ...), custom_call_target="tpu_custom_call" | custom-call | flops 8000000000 | bytes 50000000 | tf_op jit(solution)/shard_map/pallas_call | solution.py:564
  249.6 10.7 %multiply_convert_fusion = (bf16[1280,1024]{1,0:T(8,128)(2,1)S(1)}, f32[1280,1024]{1,0:T(8,128)}) fusion(bf16[1280,2048]{1,0:T(8,128)(2,1)} %get-tuple-element.31, bf16[2048,1024]{1,0:T(8,128)(2,1)} %get-tuple-element.32), kind=kOutput, calls=%fused_computation.9 | convolution fusion | flops 5375262720 | bytes 17301504 | tf_op jit(solution)/shard_map/dot_general | solution.py:983
  260.3 1.5 copy-done.9
  261.8 7.4 %convolution_convert_fusion.3.gd_ref = bf16[2048,1024]{1,0:T(8,128)(2,1)} fusion(bf16[1280,2048]{1,0:T(8,128)(2,1)S(1)} %copy-done.7, bf16[1280,1024]{1,0:T(8,128)(2,1)S(1)} %get-tuple-element.98), kind=kOutput, calls=%fused_computation.12 | convolution fusion | flops 5370806272 | bytes 12058624 | tf_op jit(solution)/shard_map/dot_general | solution.py:983
  269.2 1.8 constant_dynamic-slice_fusion
  271.0 1.3 collective-permute-start
  272.6 1.1 copy.31
  273.7 10.0 %convolution_convert_fusion.ff_ref = bf16[1280,2048]{1,0:T(8,128)(2,1)} fusion(bf16[1280,1024]{1,0:T(8,128)(2,1)} %copy-done.9, bf16[1024,2048]{1,0:T(8,128)(2,1)} %get-tuple-element.33), kind=kOutput, calls=%fused_computation.1 | convolution fusion | flops 5371330560 | bytes 12058624 | tf_op jit(solution)/shard_map/dot_general | solution.py:983
  283.7 11.2 %fusion.5 = bf16[1280,1024]{1,0:T(8,128)(2,1)} fusion(f32[1280,1024]{1,0:T(8,128)} %get-tuple-element.99, bf16[1280,2048]{1,0:T(8,128)(2,1)} %get-tuple-element.30.cots_ref, bf16[1024,2048]{1,0:T(8,128)(2,1)S(1)} %copy-done.8), kind=kOutput, calls=%fused_computation.8 | convolution fusion | flops 5381816320 | bytes 17301504 | tf_op jit(solution)/shard_map/dot_general | solution.py:983
  294.9 10.1 %convolution_convert_fusion.1.dn_ref = bf16[1280,2048]{1,0:T(8,128)(2,1)} fusion(bf16[1280,1024]{1,0:T(8,128)(2,1)} %fusion.5, bf16[2048,1024]{1,0:T(8,128)(2,1)} %get-tuple-element.32), kind=kOutput, calls=%fused_computation.2 | convolution fusion | flops 5371330560 | bytes 12058624 | tf_op jit(solution)/shard_map/dot_general | solution.py:983
  305.0 10.2 %convolution_convert_fusion.2.gu_ref = bf16[2048,1024]{1,0:T(8,128)(2,1)} fusion(bf16[1280,2048]{1,0:T(8,128)(2,1)} %get-tuple-element.31, bf16[1280,1024]{1,0:T(8,128)(2,1)S(1)} %copy-done.10), kind=kOutput, calls=%fused_computation.11 | convolution fusion | flops 5370806272 | bytes 12058624 | tf_op jit(solution)/shard_map/dot_general | solution.py:983
  315.2 3.0 collective-permute-done.gd_came_ref
  318.2 259.6 %shard_map.187 = (f32[2048,256]{1,0:T(8,128)}, f32[256,2048]{1,0:T(8,128)}, f32[512,256]{1,0:T(8,128)}, bf16[4,384,256]{2,1,0:T(8,128)(2,1)}, bf16[640,2048]{1,0...) custom-call(bf16[2048,1024]{1,0:T(8,128)(2,1)} %convolution_convert_, ...), custom_call_target="tpu_custom_call" | custom-call | flops 20000000000 | bytes 60000000 | tf_op jit(solution)/shard_map/pallas_call | solution.py:954
  577.8 3.3 broadcast_multiply_fusion
  581.5 1.1 fusion.6
  583.1 0.8 collective-permute-done.1
  584.0 1.6 collective-permute-start.2
  585.6 1.0 copy.32
  586.6 2.0 copy.33
  588.6 2.0 copy.34
  591.2 3.6 copy.39
  594.9 1.5 copy.40
  597.6 1.3 copy.42
  (40 shorter events, 6.4 us)
Async XLA Ops:
  249.6 12.2 %copy-start.7 = (bf16[1280,2048]{1,0:T(8,128)(2,1)S(1)}, bf16[1280,2048]{1,0:T(8,128)(2,1)}, u32[]{:S(2)}) copy-start(bf16[1280,2048]{1,0:T(8,128)(2,1)} %get-tuple-element.30.cots_ref) | copy-start | bytes 15728644
  260.3 1.5 copy-start.9
  269.2 3.1 copy-start.5
  269.2 3.3 copy-start.6
  271.0 47.2 %collective-permute-start = (bf16[1024,1024]{1,0:T(8,128)(2,1)S(1)}, bf16[1024,1024]{1,0:T(8,128)(2,1)}, u32[]{:S(2)}, u32[]{:S(2)}) collective-permute-start(bf16[1024,1024]{1,0:T(8,128)(2,1)S(1)} %constant_dynamic-slice_fusion), channel_id=1, source_target_pairs={{0,16},{16,0},{1,17},{17,1},{2,18},{18,2},{3,19},{19,3},{4,20},{20... | collective-permute-start | bytes 6291464 | tf_op jit(solution)/shard_map/ppermute | solution.py:967
  273.7 10.0 %copy-start.8 = (bf16[1024,2048]{1,0:T(8,128)(2,1)S(1)}, bf16[1024,2048]{1,0:T(8,128)(2,1)}, u32[]{:S(2)}) copy-start(bf16[1024,2048]{1,0:T(8,128)(2,1)} %get-tuple-element.33) | copy-start | bytes 12582916
  294.9 10.1 %copy-start.10 = (bf16[1280,1024]{1,0:T(8,128)(2,1)S(1)}, bf16[1280,1024]{1,0:T(8,128)(2,1)}, u32[]{:S(2)}) copy-start(bf16[1280,1024]{1,0:T(8,128)(2,1)} %fusion.5) | copy-start | bytes 7864324
  318.2 259.6 %copy-start.2 = (bf16[256,2048]{1,0:T(8,128)(2,1)S(1)}, bf16[256,2048]{1,0:T(8,128)(2,1)}, u32[]{:S(2)}) copy-start(bf16[256,2048]{1,0:T(8,128)(2,1)} %w_up_ref.1) | copy-start | bytes 3145732
  577.8 3.3 copy-start.3
  582.6 1.3 collective-permute-start.1
  584.0 6.7 %collective-permute-start.2 = (f32[2,256]{1,0:T(2,128)S(1)}, f32[2,256]{1,0:T(2,128)S(1)}, u32[]{:S(2)}, u32[]{:S(2)}) collective-permute-start(f32[2,256]{1,0:T(2,128)S(1)} %fusion.10), channel_id=1, source_target_pairs={{0,2},{1,3},{2,0},{3,1},{4,6},{5,7},{6,4},{7,5},{8,10},{9,11},{10,... | collective-permute-start | bytes 6152 | tf_op jit(solution)/shard_map/ppermute | solution.py:971
  585.6 9.3 %copy-start = (bf16[640,2048]{1,0:T(8,128)(2,1)S(1)}, bf16[640,2048]{1,0:T(8,128)(2,1)}, u32[]{:S(2)}) copy-start(bf16[640,2048]{1,0:T(8,128)(2,1)} %get-tuple-element.45) | copy-start | bytes 7864324
  591.2 5.1 copy-start.4
  594.9 2.7 copy-start.1

commit v5 on v4

--- a/solution.py
+++ b/solution.py
@@ -281,10 +281,15 @@
                 copy.wait_recv()
                 self.came.append(copy)
 
+    def flush(self, *copies):
+        for copy in copies:
+            if not any(copy is done for done in self.left):
+                copy.wait_send()
+                self.left.append(copy)
+
     def finish(self):
         self.wait(*self.all)
-        for copy in self.all:
-            copy.wait_send()
+        self.flush(*self.all)
 
 
 def greet(peers):
@@ -366,7 +371,6 @@
         return carry
 
     out_dp[0].start()
-    out_step[1].start()
     down_dp[0].start()
     load_tokens[0].wait()
     lax.fori_loop(0, 1, norm_piece, 0)
@@ -442,41 +446,37 @@
 
         lax.fori_loop(0, width // 512, piece, 0)
 
-    arrive(out_step[1], out_step[2])
     for k in range(1, SEQ):
         copies.wait(head[k])
     head_dp.start()
     arrive(token[1], token[2], token_chip[1])
-    arrive(out_step[2], out_step[3])
-    out_dp[1].start()
-    out_dp[2].start()
+    up_dp[0].start()
+    arrive(token[2], token[3], token_chip[2])
     arrive(token_chip[1], token_core[1])
     copies.wait(head_dp)
     keep(w_head, w_head_ref)
     project(0)
-    arrive(out_step[3], out_dp[3], up_step[1])
-    up_dp[0].start()
     arrive(token_core[1])
     keep(frames.at[1], whole_ref.at[1])
     project(1)
-    arrive(token[2], token[3], token_chip[2])
     arrive(token_chip[2], token_core[2])
+    arrive(token[3], token_chip[3], out_step[1], out_step[2], cot_pair)
     arrive(token_core[2])
     keep(frames.at[2], whole_ref.at[2])
     project(2)
-    arrive(up_step[1], up_step[2], up_dp[1])
-    arrive(token[3], token_chip[3])
-    arrive(up_step[2], up_step[3], up_dp[2])
     arrive(token_chip[3], token_core[3])
     arrive(token_core[3])
     keep(frames.at[3], whole_ref.at[3])
     project(3)
     query_frame(0)
+    arrive(out_step[1], out_step[3], out_dp[1])
     query_frame(1)
+    arrive(out_step[2], up_step[1], out_dp[2])
+    arrive(cot_pair, cot_chip)
     query_frame(2)
     query_frame(3)
     came[0] = att_low[0]
-    arrive(up_step[3], up_dp[3], cot_pair)
+    arrive(out_step[3], out_dp[3], up_step[2])
     copies.wait(*back_home[1:])
     for h in range(SEQ):
         attended_ref[:, h * HEAD_DIM : (h + 1) * HEAD_DIM] = came[lax.rem(h - z + SEQ, SEQ)]
@@ -487,11 +487,10 @@
     mix(half)
     sum_core.start()
     mix(0)
-    arrive(cot_pair, cot_chip, down_step[1])
     copies.wait(sum_core)
     half_low[...] = (part_low[quarter:half, :].astype(f32) + core_in[quarter:half, :].astype(f32)).astype(bf16)
     sum_chip.start()
-    arrive(down_step[1], down_step[2], down_dp[1])
+    arrive(up_step[1], up_step[3], up_dp[1])
     arrive(cot_chip, cot_core)
     copies.wait(sum_chip)
     resid = tokens[first, :].astype(f32) + (part_low[first, :].astype(f32) + core_in[first, :].astype(f32)) + chip_in[...].astype(f32)
@@ -504,11 +503,14 @@
     resid_ref[...] = resid
     rate_ref[...] = rate
     normed_ref[...] = normed
-    arrive(down_step[2], down_step[3], down_dp[2])
+    arrive(up_step[2], down_step[1], up_dp[2])
     arrive(second_chip[0], second_core[0])
-    arrive(second_pair, second_chip[1])
+    arrive(second_pair, second_chip[1], down_step[2])
+    arrive(up_step[3], up_dp[3], down_step[3])
+    arrive(down_step[1], down_dp[1])
+    arrive(second_chip[1], second_core[1])
+    arrive(down_step[2], down_dp[2])
     arrive(down_step[3], down_dp[3])
-    arrive(second_chip[1], second_core[1])
     copies.wait(*second_core)
     keep(second, second_ref)
     copies.finish()
@@ -573,11 +575,13 @@
 
 
 def back_kernel(
-    gd_ref, gd_came_ref, gu_ref, dn_ref, ff_ref, resid_ref, cots_ref, normed_two_ref, rate_two_ref, attended_ref, out_ref, qkv_ref, att_ref, lse_ref, bias_ref, w_head_ref, whole_ref, x_ref,
-    down_sum_ref, up_sum_ref, out_sum_ref, arrived_ref, grad_in_ref, result_ref, cross_up_ref, far_down_ref, far_up_ref, dn_core_ref, dn_chip_ref, ff_core_ref, ff_chip_ref, pair_ref, first_core_ref, first_chip_ref, first_ring_ref,
+    gd_ref, d_up_ref, second_ref, act_ref, down_ref, dn_ref, resid_ref, cots_ref, normed_two_ref, rate_two_ref, attended_ref, out_ref, qkv_ref, att_ref, lse_ref, bias_ref, w_head_ref, whole_ref, x_ref,
+    w_query_ref, w_key_ref, w_value_ref, w_up_ref, gain_one_ref, gain_two_ref,
+    down_sum_ref, up_sum_ref, out_sum_ref, grad_query_ref, grad_key_ref, grad_value_ref, gains_ref, grad_in_ref, result_ref,
+    gu_ref, ff_ref, arrived_ref, cross_down_ref, cross_up_ref, far_down_ref, far_up_ref, dn_core_ref, dn_chip_ref, ff_core_ref, ff_chip_ref, pair_ref, first_core_ref, first_chip_ref, first_ring_ref,
     frames, temp, box_down, box_up, mix, d_head, d_out, dq, dk, dv, delta, d_three, out_send, out_cross, out_far, out_box,
-    head_acc, head_low, head_cross, head_sum, held_a, held_b, half_box, pair_box, mid, quart_box, in_box, own_box,
-    send, recv, keep_sem, load_sem,
+    head_acc, head_low, head_cross, head_sum, held_a, held_b, half_box, pair_box, mid, quart_box, in_box, gain_box, gain_came,
+    send, recv, keep_sem, load_sem, arena_sem, stage_sem,
 ):
     f32, bf16 = jnp.float32, jnp.bfloat16
     dp, z, t, other_dp, chip, core, pair = axes_of()
@@ -585,6 +589,7 @@
     quarter, half = rows // 4, rows // 2
     part = width // (2 * SEQ)
     side = gd_ref.shape[1]
+    inner = attended_ref.shape[1]
     copies = Copies(send, recv)
     scale = HEAD_DIM ** (-0.5)
     first, later = slice(0, quarter), slice(quarter, half)
@@ -618,6 +623,7 @@
     mix_chip = copies.make(mix.at[rows_at(0), :], mix.at[rows_at(1), :], chip)
     mix_core = copies.make(mix.at[rows_at(0, 2), :], mix.at[rows_at(2, 2), :], core)
     spread = [None] + [copies.make(d_head.at[lax.rem(z + k, SEQ)], d_out.at[k], along(k)) for k in range(1, SEQ)]
+    cross_down = [copies.make(gd_ref.at[pl.ds(block(1 - dp, k), part), :], cross_down_ref.at[k], other_dp) for k in range(SEQ)]
     cross_up = [copies.make(gu_ref.at[pl.ds(block(1 - dp, k), part), :], cross_up_ref.at[k], other_dp) for k in range(SEQ)]
     cross_out = [copies.make(out_send.at[k], out_cross.at[k], other_dp) for k in range(SEQ)]
     far_down = [None] + [copies.make(box_down.at[k - 1], far_down_ref.at[k - 1], along(-k)) for k in range(1, SEQ)]
@@ -628,18 +634,21 @@
     first_ring = [None] + [copies.make(in_box.at[k - 1], first_ring_ref.at[k - 1], along(1)) for k in range(1, SEQ)]
     head_dp = copies.make(head_low.at[1 - dp], head_cross, other_dp)
     head_out = [None] + [copies.make(head_sum.at[lax.rem(z + k, SEQ)], arrived_ref.at[k], along(k)) for k in range(1, SEQ)]
-    kept = []
+    kept, numbered = [], []
 
     def publish(n, ref):
         mine = ref.at[pl.ds(t * quarter, quarter), :]
         mate = ref.at[pl.ds(lax.rem(t + 2, 4) * quarter, quarter), :]
-        return [copies.make(own_box.at[n], mine, chip), copies.make(own_box.at[n], mine, core), copies.make(mate, mate, core)], (own_box.at[n], mine)
-
+        return [copies.make(half_box.at[n], mine, chip), copies.make(half_box.at[n], mine, core), copies.make(mate, mate, core)], (half_box.at[n], mine)
+
+    gain_core = copies.make(gain_box.at[0], gain_came.at[0], core)
+    gain_chip = copies.make(gain_box.at[1], gain_came.at[1], chip)
     result_out, result_own = publish(0, result_ref)
     grad_out_copies, grad_own = publish(1, grad_in_ref)
 
     def keep(src, dst):
-        move = pltpu.make_async_copy(src, dst, keep_sem.at[SEQ + len(kept)])
+        move = pltpu.make_async_copy(src, dst, keep_sem.at[SEQ + len(numbered)])
+        numbered.append(move)
         kept.append(move)
         move.start()
 
@@ -667,17 +676,13 @@
         return total + held_b[later, :].astype(f32)
 
     def scatter(k, own_ref, cross_at, crossing, box, far):
-        if crossing is not None:
-            copies.wait(crossing)
+        copies.wait(crossing)
         load((cross_at, temp.at[0]), (own_ref.at[pl.ds(block(dp, k), part), :], temp.at[1]))
         box[k - 1] = (temp[0].astype(f32) + temp[1].astype(f32)).astype(bf16)
         far[k].start()
 
-    def down_block(k):
-        return gd_came_ref.at[pl.ds(pl.multiple_of(lax.rem(z - k + SEQ, SEQ) * part, part), part), :]
-
     def scatter_down(k):
-        scatter(k, gd_ref, down_block(k), None, box_down, far_down)
+        scatter(k, gd_ref, cross_down_ref.at[k], cross_down[k], box_down, far_down)
 
     def scatter_up(k):
         scatter(k, gu_ref, cross_up_ref.at[k], cross_up[k], box_up, far_up)
@@ -686,9 +691,7 @@
     unlike = pl.multiple_of((1 - lax.rem(z, 2)) * side, side)
 
     def total_of(own_ref, cross_at, far_ref, far, crossing, store):
-        copies.wait(*far[1:])
-        if crossing is not None:
-            copies.wait(crossing)
+        copies.wait(crossing, *far[1:])
         load((cross_at, temp.at[0]), (own_ref.at[pl.ds(block(dp, 0), part), :], temp.at[1]), (far_ref.at[1], temp.at[2]))
         store(same, lambda at: (temp[0, :, at].astype(f32) + temp[1, :, at].astype(f32)) + temp[2, :, at].astype(f32))
         load((far_ref.at[0], temp.at[0]), (far_ref.at[2], temp.at[1]))
@@ -698,8 +701,12 @@
         for n in range(side // 256):
             down_sum_ref[pl.ds(base + n * 256, 256), :] = value(slice(n * 256, (n + 1) * 256)).T
 
+    gain_sums = []
+
     def store_plain(base, value):
-        up_sum_ref[:, pl.ds(base, side)] = value(slice(0, side))
+        raw = value(slice(0, side))
+        gain_sums.append(jnp.sum(held_a[0:part, pl.ds(base, side)].astype(f32) * raw, axis=1, keepdims=True))
+        up_sum_ref[:, pl.ds(base, side)] = raw * gain_two_ref[...]
 
     def out_block(start):
         return lax.dot_general(attended_ref[...], mix[:, pl.ds(start, part)], (((0,), (0,)), ((), ())), preferred_element_type=f32)
@@ -709,19 +716,52 @@
         out_box[k - 1] = (out_block(block(dp, k)) + out_cross[k].astype(f32)).astype(bf16)
         far_out[k].start()
 
-    for copy in (dn_core[1], dn_core[0], cross_up[1], cross_up[2]):
+    for copy in (dn_core[1], dn_core[0], cross_down[1], cross_down[2]):
         copy.start()
+
+    def place(*pairs):
+        moves = [pltpu.make_async_copy(src, dst, arena_sem.at[i]) for i, (src, dst) in enumerate(pairs)]
+        for move in moves:
+            move.start()
+        return moves
+
+    def sides(ref, at):
+        return [(ref.at[pl.ds(n * rows, rows), :], frames.at[at, :, pl.ds(n * side, side)]) for n in range(2)]
+
+    arena = place(*sides(d_up_ref, 0), *sides(act_ref, 3), *[(second_ref.at[pl.ds(n * rows, rows), :], frames.at[1 + n]) for n in range(2)])
     spare = head_acc.at[pl.ds(0, quarter), :]
-    scatter_down(1)
     half_of(dn_ref, dn_core_ref, dn_core, dn_chip, 1, 0)
     load(*[(out_ref.at[pl.ds(h * HEAD_DIM, HEAD_DIM), :], quart_box.at[h, pl.ds(0, HEAD_DIM), :]) for h in range(SEQ)])
-    scatter_down(2)
-    fetch = [pltpu.make_async_copy(whole_ref.at[k], frames.at[k], keep_sem.at[k]) for k in range(SEQ)]
-    for move in fetch:
+    for move in arena:
+        move.wait()
+
+    def up_piece(b, carry):
+        at = pl.ds(pl.multiple_of(b * part, part), part)
+        slot = lax.rem(b, 2)
+        move = pltpu.make_async_copy(temp.at[slot], gu_ref.at[at, :], stage_sem.at[slot])
+
+        @pl.when(b >= 2)
+        def _():
+            move.wait()
+
+        turned = (((0,), (0,)), ((), ()))
+        value = lax.dot_general(frames[1, :, at], frames[0, :, 0:side], turned, preferred_element_type=f32)
+        value = value + lax.dot_general(frames[2, :, at], frames[0, :, side:], turned, preferred_element_type=f32)
+        temp[slot] = value.astype(bf16)
         move.start()
+        return carry
+
+    lax.fori_loop(0, 2 * SEQ, up_piece, 0)
+    for slot in range(2):
+        pltpu.make_async_copy(temp.at[slot], gu_ref.at[pl.ds(0, part), :], stage_sem.at[slot]).wait()
+    arena = place((down_ref.at[pl.ds(0, rows), :], frames.at[1]), (down_ref.at[pl.ds(rows, side - rows), :], frames.at[2, pl.ds(0, side - rows), :]))
+    scatter_down(1)
     copies.wait(dn_chip[1])
     half_of(dn_ref, dn_core_ref, dn_core, dn_chip, 0, 0)
     pair_sum(dn_ref, dn_core_ref, dn_chip_ref, dn_chip, dn_pair, 0)
+    cross_down[3].start()
+    cross_up[1].start()
+    scatter_down(2)
     grad = own_sum(dn_ref, dn_core_ref, dn_chip_ref, dn_chip, dn_pair, 0, normed_two_ref)
     normed = spare[...]
     grad = rate_two_ref[...] * (grad - jnp.mean(grad, axis=1, keepdims=True) - normed * jnp.mean(grad * normed, axis=1, keepdims=True))
@@ -731,9 +771,9 @@
     mix[first, :] = grad.astype(bf16)
     mix_chip.start()
     scatter_down(3)
-    copies.wait(cross_up[1], cross_up[2])
-    cross_up[3].start()
-    cross_up[0].start()
+    for copy in (cross_up[2], cross_up[3], cross_up[0], cross_down[0]):
+        copy.start()
+    scatter_up(1)
     copies.wait(mix_chip)
     mix_core.start()
     copies.wait(mix_core)
@@ -744,17 +784,46 @@
             d_head[h, at, :] = lax.dot_general(mix[at, :], quart_box[h, 0:HEAD_DIM, :], (((1,), (1,)), ((), ())), preferred_element_type=f32).astype(bf16)
     for k in range(1, SEQ):
         spread[k].start()
+    d_out[0] = d_head[z]
+    for move in arena:
+        move.wait()
+
+    def ff_piece(n, carry):
+        at = pl.ds(n * quarter, quarter)
+        slot = lax.rem(n, 2)
+        stage = held_b.at[pl.ds(slot * quarter, quarter), :]
+        move = pltpu.make_async_copy(stage, ff_ref.at[at, :], stage_sem.at[slot])
+
+        @pl.when(n >= 2)
+        def _():
+            move.wait()
+
+        left = frames[3, pl.ds(lax.rem(n, 4) * quarter, quarter), pl.ds(pl.multiple_of(n // 4 * side, side), side)]
+        value = jnp.dot(left[:, 0:rows], frames[1], preferred_element_type=f32)
+        value = value + jnp.dot(left[:, rows:], frames[2, 0 : side - rows, :], preferred_element_type=f32)
+        held_b[pl.ds(slot * quarter, quarter), :] = value.astype(bf16)
+        move.start()
+        return carry
+
+    lax.fori_loop(0, 8, ff_piece, 0)
+    for slot in range(2):
+        pltpu.make_async_copy(held_b.at[pl.ds(slot * quarter, quarter), :], ff_ref.at[pl.ds(0, quarter), :], stage_sem.at[slot]).wait()
     ff_core[1].start()
     ff_core[0].start()
-    d_out[0] = d_head[z]
+    fetch = [pltpu.make_async_copy(whole_ref.at[k], frames.at[k], keep_sem.at[k]) for k in range(SEQ)]
+    for move in fetch:
+        move.start()
     for k in (1, 2, 3, 0):
         out_send[k] = out_block(block(1 - dp, k)).astype(bf16)
         cross_out[k].start()
     half_of(ff_ref, ff_core_ref, ff_core, ff_chip, 1, 1)
+    high = head_acc.shape[0]
+    pieces = [(f, slice(0, high) if n == 0 else slice(high, rows), slice((2 * f + n) * HEAD_DIM, (2 * f + n + 1) * HEAD_DIM)) for f in range(SEQ) for n in range(2)]
+    load(*[(att_ref.at[f, pl.ds(at.start, at.stop - at.start), :], head_acc.at[pl.ds(0, at.stop - at.start), pl.ds(lanes.start, HEAD_DIM)]) for f, at, lanes in pieces])
     copies.wait(*spread[1:])
     dq[...] = jnp.zeros_like(dq)
-    for f in range(SEQ):
-        delta[f] = jnp.sum((d_out[f].astype(f32) * att_ref[f]).T, axis=0, keepdims=True)
+    for f, at, lanes in pieces:
+        delta[f, :, at] = jnp.sum((d_out[f, at, :].astype(f32) * head_acc[0 : at.stop - at.start, lanes]).T, axis=0, keepdims=True)
 
     def key_frame(j):
         here = lax.rem(z - j + SEQ, SEQ)
@@ -779,12 +848,14 @@
         d_three[here, :, 2 * HEAD_DIM :] = dv[...].astype(bf16)
 
     key_frame(0)
-    scatter_up(1)
+    scatter_up(2)
     key_frame(1)
     half_of(ff_ref, ff_core_ref, ff_core, ff_chip, 0, 1)
-    scatter_up(2)
+    scatter_up(3)
     key_frame(2)
+    scatter_out(1)
     key_frame(3)
+    pair_sum(ff_ref, ff_core_ref, ff_chip_ref, ff_chip, ff_pair, 1)
     for f in range(SEQ):
         d_three[f, :, :HEAD_DIM] = (dq[f] * scale).T.astype(bf16)
 
@@ -828,20 +899,20 @@
         return sum_
 
     project_back(1)
+    scatter_out(2)
     project_back(2)
     half_sum(1)
+    scatter_out(3)
     project_back(3)
     project_back(0)
     for n in range(2):
         head_low[n] = head_acc[:, n * (width // 2) : (n + 1) * (width // 2)].astype(bf16)
     head_dp.start()
-    scatter_up(3)
     copies.wait(first_chip[1])
     half_sum(2)
     in_box[0] = quarter_sum(1).astype(bf16)
     first_ring[1].start()
-    total_of(gd_ref, down_block(0), far_down_ref, far_down, None, store_turned)
-    scatter_out(1)
+    total_of(gd_ref, cross_down_ref.at[0], far_down_ref, far_down, cross_down[0], store_turned)
     copies.wait(first_chip[2])
     half_sum(3)
     in_box[1] = quarter_sum(2).astype(bf16)
@@ -853,14 +924,43 @@
     for k in range(1, SEQ):
         head_out[k].start()
     keep(head_sum.at[z], arrived_ref.at[0])
-    scatter_out(2)
     copies.wait(first_chip[3])
     half_sum(0)
     in_box[2] = quarter_sum(3).astype(bf16)
     first_ring[3].start()
-    scatter_out(3)
-    pair_sum(ff_ref, ff_core_ref, ff_chip_ref, ff_chip, ff_pair, 1)
+    total = own_sum(ff_ref, ff_core_ref, ff_chip_ref, ff_chip, ff_pair, 1, resid_ref)
+    copies.flush(*dn_chip)
+    half_box[0] = (spare[...] + total).astype(bf16)
+    result_out[0].start()
+    result_out[1].start()
+    keep(*result_own)
+    load((w_up_ref, held_a.at[pl.ds(0, part), :]))
     total_of(gu_ref, cross_up_ref.at[0], far_up_ref, far_up, cross_up[0], store_plain)
+    copies.wait(cross_out[0], *far_out[1:])
+    sum_ = out_block(block(dp, 0)) + out_cross[0].astype(f32)
+    for k in range(1, SEQ):
+        sum_ = sum_ + out_far[k - 1].astype(f32)
+    out_sum_ref[...] = sum_
+    copies.wait(*head_out[1:])
+    kept.pop(0).wait()
+    load(
+        *[(arrived_ref.at[k], head_cross.at[:, pl.ds(k * part, part)]) for k in range(SEQ)],
+        *[(ref, held_a.at[pl.ds(0, part), pl.ds(n * inner, inner)]) for n, ref in enumerate((w_query_ref, w_key_ref, w_value_ref))],
+    )
+    gain_first = jnp.zeros((part, 1), f32)
+    for h in range(SEQ):
+        raw = head_cross[:, pl.ds(pl.multiple_of(lax.rem(z - h + SEQ, SEQ) * part, part), part)].astype(f32).T
+        for n, ref in enumerate((grad_query_ref, grad_key_ref, grad_value_ref)):
+            one = raw[:, n * HEAD_DIM : (n + 1) * HEAD_DIM]
+            weight = held_a[0:part, n * inner + h * HEAD_DIM : n * inner + (h + 1) * HEAD_DIM].astype(f32)
+            gain_first = gain_first + jnp.sum(weight * one, axis=1, keepdims=True)
+            ref[:, h * HEAD_DIM : (h + 1) * HEAD_DIM] = one * gain_one_ref[...]
+    lane = lax.broadcasted_iota(jnp.int32, (part, HEAD_DIM), 1)
+    gain_box[0] = jnp.where(lane == 0, gain_first, gain_sums[0] + gain_sums[1])
+    gain_core.start()
+    copies.wait(gain_core)
+    gain_box[1] = gain_box[0] + gain_came[0]
+    gain_chip.start()
     grad = quarter_sum(0)
     load((x_ref.at[pl.ds(t * quarter, quarter), :], held_a.at[rows_at(0), :]))
     center = held_a[first, :].astype(f32)
@@ -868,30 +968,21 @@
     rate = lax.rsqrt(jnp.mean(center * center, axis=1, keepdims=True) + NORM_EPS)
     normed = center * rate
     grad = rate * (grad - jnp.mean(grad, axis=1, keepdims=True) - normed * jnp.mean(grad * normed, axis=1, keepdims=True))
-    own_box[1] = (mid[...] + grad).astype(bf16)
+    half_box[1] = (mid[...] + grad).astype(bf16)
     grad_out_copies[0].start()
     grad_out_copies[1].start()
     keep(*grad_own)
-    total = own_sum(ff_ref, ff_core_ref, ff_chip_ref, ff_chip, ff_pair, 1, resid_ref)
-    own_box[0] = (spare[...] + total).astype(bf16)
-    result_out[0].start()
-    result_out[1].start()
-    keep(*result_own)
-    copies.wait(cross_out[0], *far_out[1:])
-    sum_ = out_block(block(dp, 0)) + out_cross[0].astype(f32)
-    for k in range(1, SEQ):
-        sum_ = sum_ + out_far[k - 1].astype(f32)
-    out_sum_ref[...] = sum_
+    copies.wait(result_out[0], gain_chip)
+    result_out[2].start()
+    gains_ref[...] = gain_box[1] + gain_came[1]
     copies.wait(grad_out_copies[0])
     grad_out_copies[2].start()
-    copies.wait(result_out[0])
-    result_out[2].start()
     copies.finish()
     for move in kept:
         move.wait()
 
 
-def back(gd, gd_came, gu, dn, ff, resid, cots, normed_two, rate_two, attended, out_rel, qkv, att, lse, bias, w_head, whole, x):
+def back(gd, d_up, second, act, down, dn, resid, cots, normed_two, rate_two, attended, out_rel, qkv, att, lse, bias, w_head, whole, x, w_query, w_key, w_value, w_up, gain_one, gain_two):
     rows, width = x.shape
     quarter, half = rows // 4, rows // 2
     part = width // (2 * SEQ)
@@ -905,9 +996,16 @@
         (shape((2 * side, part), f32), vmem),
         (shape((part, 2 * side), f32), vmem),
         (shape((inner, part), f32), vmem),
-        (shape((SEQ, three, part), bf16), any_),
+        (shape((part, inner), f32), vmem),
+        (shape((part, inner), f32), vmem),
+        (shape((part, inner), f32), vmem),
+        (shape((part, HEAD_DIM), f32), vmem),
         (shape((rows, width), bf16), any_),
         (shape((rows, width), bf16), any_),
+        (shape((width, side), bf16), any_),
+        (shape((2 * rows, width), bf16), any_),
+        (shape((SEQ, three, part), bf16), any_),
+        (shape((SEQ, part, side), bf16), any_),
         (shape((SEQ, part, side), bf16), any_),
         (shape((SEQ - 1, part, side), bf16), any_),
         (shape((SEQ - 1, part, side), bf16), any_),
@@ -920,7 +1018,7 @@
         (shape((SEQ, quarter, width), bf16), any_),
         (shape((SEQ - 1, quarter, width), bf16), any_),
     ]
-    count = 10 + 2 + 3 + 4 + 4 + 9 + 8 + 3 + 4 + 6
+    count = 10 + 2 + 3 + 4 + 4 + 4 + 9 + 8 + 3 + 4 + 6 + 2
     scratch = [
         ((SEQ, rows, width), bf16),
         ((3, part, side), bf16),
@@ -949,34 +1047,19 @@
         ((quarter, width), f32),
         ((SEQ, quarter, width), bf16),
         ((SEQ - 1, quarter, width), bf16),
-        ((2, quarter, width), bf16),
+        ((2, part, HEAD_DIM), f32),
+        ((2, part, HEAD_DIM), f32),
     ]
     return pl.pallas_call(
         back_kernel,
         out_shape=[o[0] for o in outs],
-        in_specs=[any_] * 8 + [vmem, vmem, any_] + [vmem] * 5 + [any_] * 2,
+        in_specs=[any_] * 9 + [vmem, vmem, any_, vmem, any_] + [vmem] * 3 + [any_] * 6 + [vmem] * 2,
         out_specs=[o[1] for o in outs],
         scratch_shapes=[pltpu.VMEM(*one) for one in scratch]
-        + [pltpu.SemaphoreType.DMA((count,)), pltpu.SemaphoreType.DMA((count,)), pltpu.SemaphoreType.DMA((SEQ + 3,)), pltpu.SemaphoreType.DMA((6,))],
+        + [pltpu.SemaphoreType.DMA((count,)), pltpu.SemaphoreType.DMA((count,)), pltpu.SemaphoreType.DMA((SEQ + 3,)), pltpu.SemaphoreType.DMA((8,)), pltpu.SemaphoreType.DMA((6,)), pltpu.SemaphoreType.DMA((2,))],
         compiler_params=pltpu.CompilerParams(collective_id=1, has_side_effects=True, vmem_limit_bytes=62 * 2**20),
         cost_estimate=pl.CostEstimate(flops=20 * 10**9, bytes_accessed=60 * 10**6, transcendentals=5 * 10**6),
-    )(gd, gd_came, gu, dn, ff, resid, cots, normed_two, rate_two, attended, out_rel, qkv, att, lse, bias, w_head, whole, x)[:6]
-
-
-def swap_dp(values):
-    return lax.ppermute(values, "dp", [(0, 1), (1, 0)])
-
-
-def swap_chip(values):
-    return lax.ppermute(values, "tensor", [(i, i ^ 2) for i in range(4)])
-
-
-def swap_core(values):
-    return lax.ppermute(values, "tensor", [(i, i ^ 1) for i in range(4)])
-
-
-def dyn(stack, index):
-    return lax.dynamic_index_in_dim(stack, index, 0, keepdims=False)
+    )(gd, d_up, second, act, down, dn, resid, cots, normed_two, rate_two, attended, out_rel, qkv, att, lse, bias, w_head, whole, x, w_query, w_key, w_value, w_up, gain_one, gain_two)[:9]
 
 
 def mm(left, right, dims=((1,), (0,)), out=jnp.bfloat16):
@@ -984,9 +1067,7 @@
 
 
 def local_fast(inputs, first_gain, w_query, w_key, w_value, w_out, second_gain, w_up, w_down, frame_mask, cotangent):
-    dp, z = lax.axis_index("dp"), lax.axis_index("seq")
-    rows, width = inputs.shape[1:]
-    heads = w_query.shape[1] // HEAD_DIM
+    rows = inputs.shape[1]
     f32, bf16 = jnp.float32, jnp.bfloat16
     gain_one, gain_two = first_gain.astype(f32)[:, None], second_gain.astype(f32)[:, None]
     bias = jnp.broadcast_to(jnp.where(frame_mask[0] == 1, 0.0, MASK_FILL).astype(f32)[:, None, None], (SEQ, 1, rows))
@@ -998,22 +1079,13 @@
     up_act = (up_pre * cdf).astype(bf16)
     slope = cdf + up_pre * jnp.exp(-0.5 * up_pre * up_pre) * ((2.0 * jnp.pi) ** -0.5)
     grad_down = mm(cots, up_act, ((0,), (0,)))
-    down_came = swap_dp(lax.dynamic_slice_in_dim(grad_down, (1 - dp) * (width // 2), width // 2, 0))
     d_up = (mm(cots, down_side, ((1,), (1,)), f32) * slope).astype(bf16)
-    grad_up = mm(second_in, d_up, ((0,), (0,)))
     d_normed_two = mm(d_up, up_side, ((1,), (1,)))
-    ff_part = mm(up_act, down_side)
-    down_sum, up_raw, out_sum, arrived, grad_in, result = back(
-        grad_down, down_came, grad_up, d_normed_two, ff_part, resid_mid, cots, normed_two, rate_two, attended, out_all, qkv, attended_f, lse, bias, w_head, whole, inputs[0]
-    )
-    by_head = [dyn(arrived, lax.rem(z - h + SEQ, SEQ)).astype(f32).T for h in range(heads)]
-    raw = [jnp.concatenate([one[:, n * HEAD_DIM : (n + 1) * HEAD_DIM] for one in by_head], axis=1) for n in range(3)]
-    d_gain_one = sum(jnp.sum(weight.astype(f32) * one, axis=1) for weight, one in zip((w_query, w_key, w_value), raw))
-    d_gain_two = jnp.sum(w_up.astype(f32) * up_raw, axis=1)
-    gains = jnp.stack([d_gain_one, d_gain_two])
-    gains = gains + swap_core(gains)
-    gains = gains + swap_chip(gains)
-    return (result[None], grad_in[None], gains[0], raw[0] * gain_one, raw[1] * gain_one, raw[2] * gain_one, out_sum, gains[1], up_raw * gain_two, down_sum)
+    down_sum, up_sum, out_sum, grad_query, grad_key, grad_value, gains, grad_in, result = back(
+        grad_down, d_up, second_in, up_act, down_side, d_normed_two, resid_mid, cots, normed_two, rate_two, attended, out_all, qkv, attended_f, lse, bias, w_head, whole, inputs[0],
+        w_query, w_key, w_value, w_up, gain_one, gain_two,
+    )
+    return (result[None], grad_in[None], gains[:, 0], grad_query, grad_key, grad_value, out_sum, gains[:, 1], up_sum, down_sum)
 
 
 SEQ = 4

time: 609 us -> 546 us (0.90)
  the two profiles are of different devices: /device:TPU:0 before, /device:TPU:9 now
where the time goes in v5:
time: 546 us; the launch traced here: 537 us
  Pallas kernels  487 us (89%)
  matrix products  31.8 us (6%)
  local copies, waits for them, and re-layouts  15.2 us (3%)
    pallas_call x1, Pallas kernels, back(): pl.pallas_call(back_kernel, out_shape=[o[0] for o in outs], in_specs=[any...  264 us
    pallas_call x1, Pallas kernels, front(): pl.pallas_call(front_kernel, out_shape=[o[0] for o in outs], in_specs=[an...  223 us
    dot_general x4, matrix products, mm(): lax.dot_general(left, right, (dims, ((), ())), preferred_element_type=jnp...  31.8 us
    unnamed x32, local copies, waits for them, and re-layouts  11 us

profile of v5, /device:TPU:9, one launch (start us, length us, event | category | flops | bytes accessed | tf_op | source)
XLA Modules:
  0.0 536.6 jit_solution(13755681559203098294)
XLA Ops:
  0.6 0.7 fusion.6
  1.3 0.7 broadcast_in_dim.39
  2.0 0.7 broadcast_in_dim.40
  2.6 0.7 broadcast_in_dim.36.bias_ref
  3.3 0.8 copy.22.gain_two_ref
  4.1 0.8 copy.21.gain_one_ref
  4.9 222.8 %shard_map.186 = (bf16[4,640,2048]{2,1,0:T(8,128)(2,1)}, bf16[2048,384]{1,0:T(8,128)(2,1)}, bf16[4,640,384]{2,1,0:T(8,128)(2,1)}, f32[4,640,128]{2,1,0:T(8,128)}...) custom-call(bf16[640,2048]{1,0:T(8,128)(2,1)} %bitcast.21, ...), custom_call_target="tpu_custom_call" | custom-call | flops 8000000000 | bytes 50000000 | tf_op jit(solution)/shard_map/pallas_call | solution.py:566
  227.7 9.2 %multiply_convert_fusion = (bf16[1280,1024]{1,0:T(8,128)(2,1)S(1)}, f32[1280,1024]{1,0:T(8,128)S(1)}) fusion(bf16[1280,2048]{1,0:T(8,128)(2,1)} %get-tuple-element.34.second_ref, bf16[2048,1024]{1,0:T(8,128)(2,1)} %get-tuple-element.35), kind=kOutput, calls=%fused_computation.8 | convolution fusion | flops 5375262720 | bytes 17301504 | tf_op jit(solution)/shard_map/dot_general | solution.py:1066
  236.9 0.0 copy-start.10
  237.0 7.8 %fusion.5.d_up_ref = bf16[1280,1024]{1,0:T(8,128)(2,1)S(1)} fusion(f32[1280,1024]{1,0:T(8,128)S(1)} %get-tuple-element.59, bf16[1280,2048]{1,0:T(8,128)(2,1)S(1)} %copy-done.7, bf16[1024,2048]{1,0:T(8,128)(2,1)S(1)} %copy-done.8), kind=kOutput, calls=%fused_computation.7 | convolution fusion | flops 5381816320 | bytes 17301504 | tf_op jit(solution)/shard_map/dot_general | solution.py:1066
  244.7 0.0 copy-done.9
  244.7 0.0 copy-start.11
  244.8 7.5 %convolution_convert_fusion.dn_ref = bf16[1280,2048]{1,0:T(8,128)(2,1)} fusion(bf16[1280,1024]{1,0:T(8,128)(2,1)S(1)} %fusion.5.d_up_ref, bf16[2048,1024]{1,0:T(8,128)(2,1)S(1)} %copy-done.9), kind=kOutput, calls=%fused_computation.1 | convolution fusion | flops 5371330560 | bytes 12058624 | tf_op jit(solution)/shard_map/dot_general | solution.py:1066
  252.2 7.4 %convolution_convert_fusion.1.gd_ref = bf16[2048,1024]{1,0:T(8,128)(2,1)} fusion(bf16[1280,2048]{1,0:T(8,128)(2,1)S(1)} %copy-done.7, bf16[1280,1024]{1,0:T(8,128)(2,1)S(1)} %get-tuple-element.58.act_ref), kind=kOutput, calls=%fused_computation.10 | convolution fusion | flops 5370806272 | bytes 12058624 | tf_op jit(solution)/shard_map/dot_general | solution.py:1066
  259.6 263.9 %shard_map.187 = (f32[2048,256]{1,0:T(8,128)}, f32[256,2048]{1,0:T(8,128)}, f32[512,256]{1,0:T(8,128)}, f32[256,512]{1,0:T(8,128)}, f32[256,512]{1,0:T(8,128)}, ...) custom-call(bf16[2048,1024]{1,0:T(8,128)(2,1)} %convolution_convert_, ...), custom_call_target="tpu_custom_call" | custom-call | flops 20000000000 | bytes 60000000 | tf_op jit(solution)/shard_map/pallas_call | solution.py:1053
  523.5 1.9 slice_reduce_fusion
  525.4 3.6 copy.33
  529.1 1.5 copy.34
  530.6 0.8 copy.35
  531.4 0.8 copy.36
  532.2 0.8 copy.37
  532.9 0.8 copy.38
  533.7 1.3 copy.39
  535.1 1.3 copy.40
  (21 shorter events, 0.0 us)
Async XLA Ops:
  227.7 9.3 %copy-start.7 = (bf16[1280,2048]{1,0:T(8,128)(2,1)S(1)}, bf16[1280,2048]{1,0:T(8,128)(2,1)}, u32[]{:S(2)}) copy-start(bf16[1280,2048]{1,0:T(8,128)(2,1)} %get-tuple-element.33.cots_ref) | copy-start | bytes 15728644
  227.7 9.3 %copy-start.8 = (bf16[1024,2048]{1,0:T(8,128)(2,1)S(1)}, bf16[1024,2048]{1,0:T(8,128)(2,1)}, u32[]{:S(2)}) copy-start(bf16[1024,2048]{1,0:T(8,128)(2,1)} %get-tuple-element.36.down_ref) | copy-start | bytes 12582916
  236.9 15.3 %copy-start.10 = (bf16[1280,1024]{1,0:T(8,128)(2,1)}, bf16[1280,1024]{1,0:T(8,128)(2,1)S(1)}, u32[]{:S(2)}) copy-start(bf16[1280,1024]{1,0:T(8,128)(2,1)S(1)} %get-tuple-element.58.act_ref) | copy-start | bytes 7864324
  236.9 7.8 %copy-start.9 = (bf16[2048,1024]{1,0:T(8,128)(2,1)S(1)}, bf16[2048,1024]{1,0:T(8,128)(2,1)}, u32[]{:S(2)}) copy-start(bf16[2048,1024]{1,0:T(8,128)(2,1)} %get-tuple-element.35) | copy-start | bytes 12582916
  244.7 7.5 %copy-start.11 = (bf16[1280,1024]{1,0:T(8,128)(2,1)}, bf16[1280,1024]{1,0:T(8,128)(2,1)S(1)}, u32[]{:S(2)}) copy-start(bf16[1280,1024]{1,0:T(8,128)(2,1)S(1)} %fusion.5.d_up_ref) | copy-start | bytes 7864324
  523.5 5.5 %copy-start = (bf16[640,2048]{1,0:T(8,128)(2,1)S(1)}, bf16[640,2048]{1,0:T(8,128)(2,1)}, u32[]{:S(2)}) copy-start(bf16[640,2048]{1,0:T(8,128)(2,1)} %get-tuple-element.48) | copy-start | bytes 7864324
  525.4 5.1 copy-start.6
  529.0 2.3 copy-start.5
  529.0 3.1 copy-start.4
  529.0 3.9 copy-start.3
  529.1 4.7 copy-start.2
  530.6 4.5 copy-start.1

commit v6 on v5

--- a/solution.py
+++ b/solution.py
@@ -292,6 +292,11 @@
         self.flush(*self.all)
 
 
+def column(row_ref):
+    row = jnp.broadcast_to(row_ref[...].astype(jnp.float32), (8, row_ref.shape[1]))
+    return row.T[:, 0:1]
+
+
 def greet(peers):
     barrier = pltpu.get_barrier_semaphore()
     for peer in peers:
@@ -300,7 +305,7 @@
 
 
 def front_kernel(
-    x_ref, w_query_ref, w_key_ref, w_value_ref, w_out_ref, w_up_ref, w_down_ref, gain_one_ref, gain_two_ref, cot_ref, bias_ref,
+    x_ref, w_query_ref, w_key_ref, w_value_ref, w_out_ref, w_up_ref, w_down_ref, gain_one_ref, gain_two_ref, cot_ref, valid_ref,
     whole_ref, w_head_ref, qkv_ref, att_ref, lse_ref, attended_ref, out_ref, resid_ref, normed_ref, rate_ref, second_ref, up_ref, down_ref, cots_ref,
     tokens, frames, w_own, w_head, up_own, out_all, att_low, came, part_low, core_in, half_low, chip_in, second, peak, total, acc, send, recv, local_sem,
 ):
@@ -375,7 +380,7 @@
     load_tokens[0].wait()
     lax.fori_loop(0, 1, norm_piece, 0)
     token[1].start()
-    gain = gain_one_ref[...]
+    gain = column(gain_one_ref)
     for h in range(SEQ):
         at = slice(h * HEAD_DIM, (h + 1) * HEAD_DIM)
         for n, ref in enumerate((w_query_ref, w_key_ref, w_value_ref)):
@@ -383,7 +388,7 @@
     for k in range(1, SEQ):
         head[k].start()
     w_head[pl.ds(owner(0), part), :] = w_own[z]
-    gain = gain_two_ref[...]
+    gain = column(gain_two_ref)
     for h in range(2):
         up_own[h] = (w_up_ref[:, h * side : (h + 1) * side].astype(f32) * gain).astype(bf16)
     keep(up_own.at[lax.rem(z, 2)], up_ref.at[pl.ds(owner(0), part), :])
@@ -415,7 +420,7 @@
 
         def key_frame(j, inner):
             here = lax.rem(z - j + SEQ, SEQ)
-            scores = lax.dot_general(qkv_ref[here, :, HEAD_DIM : 2 * HEAD_DIM], query, (((1,), (1,)), ((), ())), preferred_element_type=f32) * scale + bias_ref[j]
+            scores = lax.dot_general(qkv_ref[here, :, HEAD_DIM : 2 * HEAD_DIM], query, (((1,), (1,)), ((), ())), preferred_element_type=f32) * scale + (valid_ref[0, j] - 1).astype(f32) * -MASK_FILL
             before = peak[...]
             after = jnp.maximum(before, jnp.max(scores, axis=0, keepdims=True))
             terms = jnp.exp(scores - after)
@@ -451,7 +456,7 @@
     head_dp.start()
     arrive(token[1], token[2], token_chip[1])
     up_dp[0].start()
-    arrive(token[2], token[3], token_chip[2])
+    arrive(token[2], token[3], token_chip[2], out_step[1])
     arrive(token_chip[1], token_core[1])
     copies.wait(head_dp)
     keep(w_head, w_head_ref)
@@ -460,7 +465,7 @@
     keep(frames.at[1], whole_ref.at[1])
     project(1)
     arrive(token_chip[2], token_core[2])
-    arrive(token[3], token_chip[3], out_step[1], out_step[2], cot_pair)
+    arrive(token[3], token_chip[3], out_step[2], cot_pair)
     arrive(token_core[2])
     keep(frames.at[2], whole_ref.at[2])
     project(2)
@@ -490,7 +495,7 @@
     copies.wait(sum_core)
     half_low[...] = (part_low[quarter:half, :].astype(f32) + core_in[quarter:half, :].astype(f32)).astype(bf16)
     sum_chip.start()
-    arrive(up_step[1], up_step[3], up_dp[1])
+    arrive(up_step[1], up_step[3], up_dp[1], down_step[1])
     arrive(cot_chip, cot_core)
     copies.wait(sum_chip)
     resid = tokens[first, :].astype(f32) + (part_low[first, :].astype(f32) + core_in[first, :].astype(f32)) + chip_in[...].astype(f32)
@@ -503,10 +508,10 @@
     resid_ref[...] = resid
     rate_ref[...] = rate
     normed_ref[...] = normed
-    arrive(up_step[2], down_step[1], up_dp[2])
+    arrive(up_step[2], down_step[2], up_dp[2])
     arrive(second_chip[0], second_core[0])
-    arrive(second_pair, second_chip[1], down_step[2])
-    arrive(up_step[3], up_dp[3], down_step[3])
+    arrive(second_pair, second_chip[1], down_step[3])
+    arrive(up_step[3], up_dp[3])
     arrive(down_step[1], down_dp[1])
     arrive(second_chip[1], second_core[1])
     arrive(down_step[2], down_dp[2])
@@ -519,7 +524,7 @@
             copy.wait()
 
 
-def front(x, w_query, w_key, w_value, w_out, w_up, w_down, gain_one, gain_two, cot, bias):
+def front(x, w_query, w_key, w_value, w_out, w_up, w_down, gain_one, gain_two, cot, valid):
     rows, width = x.shape
     quarter, half = rows // 4, rows // 2
     part, hidden = w_up.shape
@@ -566,16 +571,16 @@
     return pl.pallas_call(
         front_kernel,
         out_shape=[o[0] for o in outs],
-        in_specs=[any_] + [vmem] * 3 + [any_, vmem, any_, vmem, vmem, any_, vmem],
+        in_specs=[any_] + [vmem] * 3 + [any_, vmem, any_, vmem, vmem, any_, pl.BlockSpec(memory_space=pltpu.SMEM)],
         out_specs=[o[1] for o in outs],
         scratch_shapes=[pltpu.VMEM(*one) for one in scratch] + [pltpu.SemaphoreType.DMA((count,)), pltpu.SemaphoreType.DMA((count,)), pltpu.SemaphoreType.DMA((24,))],
         compiler_params=pltpu.CompilerParams(collective_id=0, has_side_effects=True, vmem_limit_bytes=58 * 2**20),
         cost_estimate=pl.CostEstimate(flops=8 * 10**9, bytes_accessed=50 * 10**6, transcendentals=5 * 10**6),
-    )(x, w_query, w_key, w_value, w_out, w_up, w_down, gain_one, gain_two, cot, bias)
+    )(x, w_query, w_key, w_value, w_out, w_up, w_down, gain_one, gain_two, cot, valid)
 
 
 def back_kernel(
-    gd_ref, d_up_ref, second_ref, act_ref, down_ref, dn_ref, resid_ref, cots_ref, normed_two_ref, rate_two_ref, attended_ref, out_ref, qkv_ref, att_ref, lse_ref, bias_ref, w_head_ref, whole_ref, x_ref,
+    gd_ref, d_up_ref, second_ref, act_ref, down_ref, dn_ref, resid_ref, cots_ref, normed_two_ref, rate_two_ref, attended_ref, out_ref, qkv_ref, att_ref, lse_ref, valid_ref, w_head_ref, whole_ref, x_ref,
     w_query_ref, w_key_ref, w_value_ref, w_up_ref, gain_one_ref, gain_two_ref,
     down_sum_ref, up_sum_ref, out_sum_ref, grad_query_ref, grad_key_ref, grad_value_ref, gains_ref, grad_in_ref, result_ref,
     gu_ref, ff_ref, arrived_ref, cross_down_ref, cross_up_ref, far_down_ref, far_up_ref, dn_core_ref, dn_chip_ref, ff_core_ref, ff_chip_ref, pair_ref, first_core_ref, first_chip_ref, first_ring_ref,
@@ -675,17 +680,18 @@
         total = quarter_of(part_ref, core_ref, chip_ref, to_chip, 0, (pair_ref.at[n], held_b.at[rows_at(1), :]), (extra, spare))
         return total + held_b[later, :].astype(f32)
 
-    def scatter(k, own_ref, cross_at, crossing, box, far):
+    def scatter(k, own_ref, cross_at, crossing, box, far, go=True):
         copies.wait(crossing)
         load((cross_at, temp.at[0]), (own_ref.at[pl.ds(block(dp, k), part), :], temp.at[1]))
         box[k - 1] = (temp[0].astype(f32) + temp[1].astype(f32)).astype(bf16)
-        far[k].start()
+        if go:
+            far[k].start()
 
     def scatter_down(k):
         scatter(k, gd_ref, cross_down_ref.at[k], cross_down[k], box_down, far_down)
 
-    def scatter_up(k):
-        scatter(k, gu_ref, cross_up_ref.at[k], cross_up[k], box_up, far_up)
+    def scatter_up(k, go=True):
+        scatter(k, gu_ref, cross_up_ref.at[k], cross_up[k], box_up, far_up, go)
 
     same = pl.multiple_of(lax.rem(z, 2) * side, side)
     unlike = pl.multiple_of((1 - lax.rem(z, 2)) * side, side)
@@ -706,7 +712,7 @@
     def store_plain(base, value):
         raw = value(slice(0, side))
         gain_sums.append(jnp.sum(held_a[0:part, pl.ds(base, side)].astype(f32) * raw, axis=1, keepdims=True))
-        up_sum_ref[:, pl.ds(base, side)] = raw * gain_two_ref[...]
+        up_sum_ref[:, pl.ds(base, side)] = raw * column(gain_two_ref)
 
     def out_block(start):
         return lax.dot_general(attended_ref[...], mix[:, pl.ds(start, part)], (((0,), (0,)), ((), ())), preferred_element_type=f32)
@@ -716,7 +722,7 @@
         out_box[k - 1] = (out_block(block(dp, k)) + out_cross[k].astype(f32)).astype(bf16)
         far_out[k].start()
 
-    for copy in (dn_core[1], dn_core[0], cross_down[1], cross_down[2]):
+    for copy in (dn_core[1], dn_core[0], cross_down[1]):
         copy.start()
 
     def place(*pairs):
@@ -731,6 +737,7 @@
     arena = place(*sides(d_up_ref, 0), *sides(act_ref, 3), *[(second_ref.at[pl.ds(n * rows, rows), :], frames.at[1 + n]) for n in range(2)])
     spare = head_acc.at[pl.ds(0, quarter), :]
     half_of(dn_ref, dn_core_ref, dn_core, dn_chip, 1, 0)
+    cross_down[2].start()
     load(*[(out_ref.at[pl.ds(h * HEAD_DIM, HEAD_DIM), :], quart_box.at[h, pl.ds(0, HEAD_DIM), :]) for h in range(SEQ)])
     for move in arena:
         move.wait()
@@ -740,7 +747,7 @@
         slot = lax.rem(b, 2)
         move = pltpu.make_async_copy(temp.at[slot], gu_ref.at[at, :], stage_sem.at[slot])
 
-        @pl.when(b >= 2)
+        @pl.when(lax.rem(b, SEQ) >= 2)
         def _():
             move.wait()
 
@@ -751,15 +758,18 @@
         move.start()
         return carry
 
-    lax.fori_loop(0, 2 * SEQ, up_piece, 0)
+    lax.fori_loop(0, SEQ, up_piece, 0)
+    for slot in range(2):
+        pltpu.make_async_copy(temp.at[slot], gu_ref.at[pl.ds(0, part), :], stage_sem.at[slot]).wait()
+    scatter_down(1)
+    cross_down[3].start()
+    lax.fori_loop(SEQ, 2 * SEQ, up_piece, 0)
     for slot in range(2):
         pltpu.make_async_copy(temp.at[slot], gu_ref.at[pl.ds(0, part), :], stage_sem.at[slot]).wait()
     arena = place((down_ref.at[pl.ds(0, rows), :], frames.at[1]), (down_ref.at[pl.ds(rows, side - rows), :], frames.at[2, pl.ds(0, side - rows), :]))
-    scatter_down(1)
     copies.wait(dn_chip[1])
     half_of(dn_ref, dn_core_ref, dn_core, dn_chip, 0, 0)
     pair_sum(dn_ref, dn_core_ref, dn_chip_ref, dn_chip, dn_pair, 0)
-    cross_down[3].start()
     cross_up[1].start()
     scatter_down(2)
     grad = own_sum(dn_ref, dn_core_ref, dn_chip_ref, dn_chip, dn_pair, 0, normed_two_ref)
@@ -776,14 +786,18 @@
     scatter_up(1)
     copies.wait(mix_chip)
     mix_core.start()
+
+    def to_head(k, at):
+        h = lax.rem(z + k, SEQ)
+        d_head[h, at, :] = lax.dot_general(mix[at, :], quart_box[h, 0:HEAD_DIM, :], (((1,), (1,)), ((), ())), preferred_element_type=f32).astype(bf16)
+
+    for k in (1, 2, 3, 0):
+        to_head(k, slice(0, half))
     copies.wait(mix_core)
-
-    for n in range(4):
-        at = slice(n * quarter, (n + 1) * quarter)
-        for h in range(SEQ):
-            d_head[h, at, :] = lax.dot_general(mix[at, :], quart_box[h, 0:HEAD_DIM, :], (((1,), (1,)), ((), ())), preferred_element_type=f32).astype(bf16)
-    for k in range(1, SEQ):
-        spread[k].start()
+    for k in (1, 2, 3, 0):
+        to_head(k, slice(half, rows))
+        if k:
+            spread[k].start()
     d_out[0] = d_head[z]
     for move in arena:
         move.wait()
@@ -820,7 +834,10 @@
     high = head_acc.shape[0]
     pieces = [(f, slice(0, high) if n == 0 else slice(high, rows), slice((2 * f + n) * HEAD_DIM, (2 * f + n + 1) * HEAD_DIM)) for f in range(SEQ) for n in range(2)]
     load(*[(att_ref.at[f, pl.ds(at.start, at.stop - at.start), :], head_acc.at[pl.ds(0, at.stop - at.start), pl.ds(lanes.start, HEAD_DIM)]) for f, at, lanes in pieces])
+    scatter_up(2, False)
+    scatter_up(3, False)
     copies.wait(*spread[1:])
+    far_up[2].start()
     dq[...] = jnp.zeros_like(dq)
     for f, at, lanes in pieces:
         delta[f, :, at] = jnp.sum((d_out[f, at, :].astype(f32) * head_acc[0 : at.stop - at.start, lanes]).T, axis=0, keepdims=True)
@@ -834,7 +851,7 @@
             at = lax.rem(z - i + SEQ, SEQ)
             query, key, value = qkv_ref[at, :, :HEAD_DIM], qkv_ref[here, :, HEAD_DIM : 2 * HEAD_DIM], qkv_ref[here, :, 2 * HEAD_DIM :]
             grad_out = d_out[at]
-            scores = lax.dot_general(key, query, (((1,), (1,)), ((), ())), preferred_element_type=f32) * scale + bias_ref[j]
+            scores = lax.dot_general(key, query, (((1,), (1,)), ((), ())), preferred_element_type=f32) * scale + (valid_ref[0, j] - 1).astype(f32) * -MASK_FILL
             prob = jnp.exp(scores - lse_ref[at])
             d_prob = lax.dot_general(value, grad_out, (((1,), (1,)), ((), ())), preferred_element_type=f32)
             d_scores = (prob * (d_prob - delta[at])).astype(bf16)
@@ -848,12 +865,12 @@
         d_three[here, :, 2 * HEAD_DIM :] = dv[...].astype(bf16)
 
     key_frame(0)
-    scatter_up(2)
+    far_up[3].start()
+    scatter_out(1)
     key_frame(1)
     half_of(ff_ref, ff_core_ref, ff_core, ff_chip, 0, 1)
-    scatter_up(3)
+    scatter_out(2)
     key_frame(2)
-    scatter_out(1)
     key_frame(3)
     pair_sum(ff_ref, ff_core_ref, ff_chip_ref, ff_chip, ff_pair, 1)
     for f in range(SEQ):
@@ -899,33 +916,34 @@
         return sum_
 
     project_back(1)
-    scatter_out(2)
+    scatter_out(3)
     project_back(2)
     half_sum(1)
-    scatter_out(3)
     project_back(3)
     project_back(0)
     for n in range(2):
         head_low[n] = head_acc[:, n * (width // 2) : (n + 1) * (width // 2)].astype(bf16)
     head_dp.start()
-    copies.wait(first_chip[1])
     half_sum(2)
     in_box[0] = quarter_sum(1).astype(bf16)
     first_ring[1].start()
     total_of(gd_ref, cross_down_ref.at[0], far_down_ref, far_down, cross_down[0], store_turned)
-    copies.wait(first_chip[2])
     half_sum(3)
+    load((w_up_ref, held_a.at[pl.ds(0, part), :]))
+    total_of(gu_ref, cross_up_ref.at[0], far_up_ref, far_up, cross_up[0], store_plain)
     in_box[1] = quarter_sum(2).astype(bf16)
     first_ring[2].start()
+    half_sum(0)
     copies.wait(head_dp)
     for j in range(SEQ):
         at = slice(j * part, (j + 1) * part)
         head_sum[j] = (head_low[dp, :, at].astype(f32) + head_cross[:, at].astype(f32)).astype(bf16)
+    keep(head_sum.at[z], arrived_ref.at[0])
+    copies.wait(cross_out[0], *far_out[1:])
+    sum_ = out_block(block(dp, 0)) + out_cross[0].astype(f32)
     for k in range(1, SEQ):
-        head_out[k].start()
-    keep(head_sum.at[z], arrived_ref.at[0])
-    copies.wait(first_chip[3])
-    half_sum(0)
+        sum_ = sum_ + out_far[k - 1].astype(f32)
+    out_sum_ref[...] = sum_
     in_box[2] = quarter_sum(3).astype(bf16)
     first_ring[3].start()
     total = own_sum(ff_ref, ff_core_ref, ff_chip_ref, ff_chip, ff_pair, 1, resid_ref)
@@ -934,55 +952,52 @@
     result_out[0].start()
     result_out[1].start()
     keep(*result_own)
-    load((w_up_ref, held_a.at[pl.ds(0, part), :]))
-    total_of(gu_ref, cross_up_ref.at[0], far_up_ref, far_up, cross_up[0], store_plain)
-    copies.wait(cross_out[0], *far_out[1:])
-    sum_ = out_block(block(dp, 0)) + out_cross[0].astype(f32)
+    load((x_ref.at[pl.ds(t * quarter, quarter), :], held_a.at[rows_at(0), :]))
+    center = held_a[first, :].astype(f32)
+    center = center - jnp.mean(center, axis=1, keepdims=True)
+    rate = lax.rsqrt(jnp.mean(center * center, axis=1, keepdims=True) + NORM_EPS)
+    head_acc[later, :] = center * rate
     for k in range(1, SEQ):
-        sum_ = sum_ + out_far[k - 1].astype(f32)
-    out_sum_ref[...] = sum_
+        head_out[k].start()
+    grad = quarter_sum(0)
+    normed = head_acc[later, :]
+    grad = rate * (grad - jnp.mean(grad, axis=1, keepdims=True) - normed * jnp.mean(grad * normed, axis=1, keepdims=True))
+    half_box[1] = (mid[...] + grad).astype(bf16)
+    grad_out_copies[0].start()
+    grad_out_copies[1].start()
+    keep(*grad_own)
+    copies.wait(result_out[0])
+    result_out[2].start()
     copies.wait(*head_out[1:])
     kept.pop(0).wait()
     load(
         *[(arrived_ref.at[k], head_cross.at[:, pl.ds(k * part, part)]) for k in range(SEQ)],
         *[(ref, held_a.at[pl.ds(0, part), pl.ds(n * inner, inner)]) for n, ref in enumerate((w_query_ref, w_key_ref, w_value_ref))],
     )
-    gain_first = jnp.zeros((part, 1), f32)
+    gain_first, gain = jnp.zeros((part, 1), f32), column(gain_one_ref)
     for h in range(SEQ):
         raw = head_cross[:, pl.ds(pl.multiple_of(lax.rem(z - h + SEQ, SEQ) * part, part), part)].astype(f32).T
         for n, ref in enumerate((grad_query_ref, grad_key_ref, grad_value_ref)):
             one = raw[:, n * HEAD_DIM : (n + 1) * HEAD_DIM]
             weight = held_a[0:part, n * inner + h * HEAD_DIM : n * inner + (h + 1) * HEAD_DIM].astype(f32)
             gain_first = gain_first + jnp.sum(weight * one, axis=1, keepdims=True)
-            ref[:, h * HEAD_DIM : (h + 1) * HEAD_DIM] = one * gain_one_ref[...]
+            ref[:, h * HEAD_DIM : (h + 1) * HEAD_DIM] = one * gain
     lane = lax.broadcasted_iota(jnp.int32, (part, HEAD_DIM), 1)
     gain_box[0] = jnp.where(lane == 0, gain_first, gain_sums[0] + gain_sums[1])
     gain_core.start()
     copies.wait(gain_core)
     gain_box[1] = gain_box[0] + gain_came[0]
     gain_chip.start()
-    grad = quarter_sum(0)
-    load((x_ref.at[pl.ds(t * quarter, quarter), :], held_a.at[rows_at(0), :]))
-    center = held_a[first, :].astype(f32)
-    center = center - jnp.mean(center, axis=1, keepdims=True)
-    rate = lax.rsqrt(jnp.mean(center * center, axis=1, keepdims=True) + NORM_EPS)
-    normed = center * rate
-    grad = rate * (grad - jnp.mean(grad, axis=1, keepdims=True) - normed * jnp.mean(grad * normed, axis=1, keepdims=True))
-    half_box[1] = (mid[...] + grad).astype(bf16)
-    grad_out_copies[0].start()
-    grad_out_copies[1].start()
-    keep(*grad_own)
-    copies.wait(result_out[0], gain_chip)
-    result_out[2].start()
-    gains_ref[...] = gain_box[1] + gain_came[1]
     copies.wait(grad_out_copies[0])
     grad_out_copies[2].start()
+    copies.wait(gain_chip)
+    gains_ref[...] = (gain_box[1] + gain_came[1]).T[0:8]
     copies.finish()
     for move in kept:
         move.wait()
 
 
-def back(gd, d_up, second, act, down, dn, resid, cots, normed_two, rate_two, attended, out_rel, qkv, att, lse, bias, w_head, whole, x, w_query, w_key, w_value, w_up, gain_one, gain_two):
+def back(gd, d_up, second, act, down, dn, resid, cots, normed_two, rate_two, attended, out_rel, qkv, att, lse, valid, w_head, whole, x, w_query, w_key, w_value, w_up, gain_one, gain_two):
     rows, width = x.shape
     quarter, half = rows // 4, rows // 2
     part = width // (2 * SEQ)
@@ -999,7 +1014,7 @@
         (shape((part, inner), f32), vmem),
         (shape((part, inner), f32), vmem),
         (shape((part, inner), f32), vmem),
-        (shape((part, HEAD_DIM), f32), vmem),
+        (shape((8, part), f32), vmem),
         (shape((rows, width), bf16), any_),
         (shape((rows, width), bf16), any_),
         (shape((width, side), bf16), any_),
@@ -1053,13 +1068,13 @@
     return pl.pallas_call(
         back_kernel,
         out_shape=[o[0] for o in outs],
-        in_specs=[any_] * 9 + [vmem, vmem, any_, vmem, any_] + [vmem] * 3 + [any_] * 6 + [vmem] * 2,
+        in_specs=[any_] * 9 + [vmem, vmem, any_, vmem, any_, vmem, pl.BlockSpec(memory_space=pltpu.SMEM), vmem] + [any_] * 6 + [vmem] * 2,
         out_specs=[o[1] for o in outs],
         scratch_shapes=[pltpu.VMEM(*one) for one in scratch]
         + [pltpu.SemaphoreType.DMA((count,)), pltpu.SemaphoreType.DMA((count,)), pltpu.SemaphoreType.DMA((SEQ + 3,)), pltpu.SemaphoreType.DMA((8,)), pltpu.SemaphoreType.DMA((6,)), pltpu.SemaphoreType.DMA((2,))],
         compiler_params=pltpu.CompilerParams(collective_id=1, has_side_effects=True, vmem_limit_bytes=62 * 2**20),
         cost_estimate=pl.CostEstimate(flops=20 * 10**9, bytes_accessed=60 * 10**6, transcendentals=5 * 10**6),
-    )(gd, d_up, second, act, down, dn, resid, cots, normed_two, rate_two, attended, out_rel, qkv, att, lse, bias, w_head, whole, x, w_query, w_key, w_value, w_up, gain_one, gain_two)[:9]
+    )(gd, d_up, second, act, down, dn, resid, cots, normed_two, rate_two, attended, out_rel, qkv, att, lse, valid, w_head, whole, x, w_query, w_key, w_value, w_up, gain_one, gain_two)[:9]
 
 
 def mm(left, right, dims=((1,), (0,)), out=jnp.bfloat16):
@@ -1069,10 +1084,10 @@
 def local_fast(inputs, first_gain, w_query, w_key, w_value, w_out, second_gain, w_up, w_down, frame_mask, cotangent):
     rows = inputs.shape[1]
     f32, bf16 = jnp.float32, jnp.bfloat16
-    gain_one, gain_two = first_gain.astype(f32)[:, None], second_gain.astype(f32)[:, None]
-    bias = jnp.broadcast_to(jnp.where(frame_mask[0] == 1, 0.0, MASK_FILL).astype(f32)[:, None, None], (SEQ, 1, rows))
+    gain_one, gain_two = first_gain[None], second_gain[None]
+    valid = frame_mask
     whole, w_head, qkv, attended_f, lse, attended, out_all, resid_mid, normed_two, rate_two, second_in, up_side, down_side, cots = front(
-        inputs[0], w_query, w_key, w_value, w_out, w_up, w_down, gain_one, gain_two, cotangent[0], bias
+        inputs[0], w_query, w_key, w_value, w_out, w_up, w_down, gain_one, gain_two, cotangent[0], valid
     )
     up_pre = mm(second_in, up_side, out=f32)
     cdf = 0.5 * (1.0 + lax.erf(up_pre * (0.5**0.5)))
@@ -1082,10 +1097,10 @@
     d_up = (mm(cots, down_side, ((1,), (1,)), f32) * slope).astype(bf16)
     d_normed_two = mm(d_up, up_side, ((1,), (1,)))
     down_sum, up_sum, out_sum, grad_query, grad_key, grad_value, gains, grad_in, result = back(
-        grad_down, d_up, second_in, up_act, down_side, d_normed_two, resid_mid, cots, normed_two, rate_two, attended, out_all, qkv, attended_f, lse, bias, w_head, whole, inputs[0],
+        grad_down, d_up, second_in, up_act, down_side, d_normed_two, resid_mid, cots, normed_two, rate_two, attended, out_all, qkv, attended_f, lse, valid, w_head, whole, inputs[0],
         w_query, w_key, w_value, w_up, gain_one, gain_two,
     )
-    return (result[None], grad_in[None], gains[:, 0], grad_query, grad_key, grad_value, out_sum, gains[:, 1], up_sum, down_sum)
+    return (result[None], grad_in[None], gains[0], grad_query, grad_key, grad_value, out_sum, gains[1], up_sum, down_sum)
 
 
 SEQ = 4

time: 546 us -> 519 us (0.951)
  the two profiles are of different devices: /device:TPU:9 before, /device:TPU:0 now
where the time goes in v6:
time: 519 us; the launch traced here: 509 us
  Pallas kernels  462 us (89%)
  matrix products  31.9 us (6%)
  local copies, waits for them, and re-layouts  14.8 us (3%)
    pallas_call x1, Pallas kernels, back(): pl.pallas_call(back_kernel, out_shape=[o[0] for o in outs], in_specs=[any...  235 us
    pallas_call x1, Pallas kernels, front(): pl.pallas_call(front_kernel, out_shape=[o[0] for o in outs], in_specs=[an...  227 us
    dot_general x4, matrix products, mm(): lax.dot_general(left, right, (dims, ((), ())), preferred_element_type=jnp...  31.9 us
    unnamed x32, local copies, waits for them, and re-layouts  11 us

profile of v6, /device:TPU:0, one launch (start us, length us, event | category | flops | bytes accessed | tf_op | source)
XLA Modules:
  0.0 509.4 jit_solution(15344443945206784968)
XLA Ops:
  0.6 1.2 broadcast_in_dim.12.gain_one_ref
  1.9 1.2 broadcast_in_dim.13.gain_two_ref
  3.1 227.0 %shard_map.186 = (bf16[4,640,2048]{2,1,0:T(8,128)(2,1)}, bf16[2048,384]{1,0:T(8,128)(2,1)}, bf16[4,640,384]{2,1,0:T(8,128)(2,1)}, f32[4,640,128]{2,1,0:T(8,128)}...) custom-call(bf16[640,2048]{1,0:T(8,128)(2,1)} %bitcast.19, ...), custom_call_target="tpu_custom_call" | custom-call | flops 8000000000 | bytes 50000000 | tf_op jit(solution)/shard_map/pallas_call | solution.py:571
  230.2 9.2 %multiply_convert_fusion = (bf16[1280,1024]{1,0:T(8,128)(2,1)S(1)}, f32[1280,1024]{1,0:T(8,128)S(1)}) fusion(bf16[1280,2048]{1,0:T(8,128)(2,1)} %get-tuple-element.34.second_ref, bf16[2048,1024]{1,0:T(8,128)(2,1)} %get-tuple-element.35), kind=kOutput, calls=%fused_computation.8 | convolution fusion | flops 5375262720 | bytes 17301504 | tf_op jit(solution)/shard_map/dot_general | solution.py:1081
  239.4 0.0 copy-start.10
  239.4 0.0 copy-done.7
  239.4 0.0 copy-done.8
  239.4 0.0 copy-start.9
  239.4 7.8 %fusion.5.d_up_ref = bf16[1280,1024]{1,0:T(8,128)(2,1)S(1)} fusion(f32[1280,1024]{1,0:T(8,128)S(1)} %get-tuple-element.59, bf16[1280,2048]{1,0:T(8,128)(2,1)S(1)} %copy-done.7, bf16[1024,2048]{1,0:T(8,128)(2,1)S(1)} %copy-done.8), kind=kOutput, calls=%fused_computation.7 | convolution fusion | flops 5381816320 | bytes 17301504 | tf_op jit(solution)/shard_map/dot_general | solution.py:1081
  247.2 0.0 copy-start.11
  247.2 7.5 %convolution_convert_fusion.dn_ref = bf16[1280,2048]{1,0:T(8,128)(2,1)} fusion(bf16[1280,1024]{1,0:T(8,128)(2,1)S(1)} %fusion.5.d_up_ref, bf16[2048,1024]{1,0:T(8,128)(2,1)S(1)} %copy-done.9), kind=kOutput, calls=%fused_computation.1 | convolution fusion | flops 5371330560 | bytes 12058624 | tf_op jit(solution)/shard_map/dot_general | solution.py:1081
  254.7 0.0 copy-done.11
  254.7 7.4 %convolution_convert_fusion.1.gd_ref = bf16[2048,1024]{1,0:T(8,128)(2,1)} fusion(bf16[1280,2048]{1,0:T(8,128)(2,1)S(1)} %copy-done.7, bf16[1280,1024]{1,0:T(8,128)(2,1)S(1)} %get-tuple-element.58.act_ref), kind=kOutput, calls=%fused_computation.10 | convolution fusion | flops 5370806272 | bytes 12058624 | tf_op jit(solution)/shard_map/dot_general | solution.py:1081
  262.1 234.7 %shard_map.187 = (f32[2048,256]{1,0:T(8,128)}, f32[256,2048]{1,0:T(8,128)}, f32[512,256]{1,0:T(8,128)}, f32[256,512]{1,0:T(8,128)}, f32[256,512]{1,0:T(8,128)}, ...) custom-call(bf16[2048,1024]{1,0:T(8,128)(2,1)} %convolution_convert_, ...), custom_call_target="tpu_custom_call" | custom-call | flops 20000000000 | bytes 60000000 | tf_op jit(solution)/shard_map/pallas_call | solution.py:1068
  496.8 1.4 fusion.6
  498.2 3.6 copy.29
  501.9 1.5 copy.30
  503.4 0.8 copy.31
  504.2 0.8 copy.32
  505.0 0.8 copy.33
  505.8 0.8 copy.34
  506.6 0.0 copy-done.2
  506.6 1.3 copy.35
  507.9 1.3 copy.36
  (17 shorter events, 0.0 us)
Async XLA Ops:
  230.1 9.3 %copy-start.7 = (bf16[1280,2048]{1,0:T(8,128)(2,1)S(1)}, bf16[1280,2048]{1,0:T(8,128)(2,1)}, u32[]{:S(2)}) copy-start(bf16[1280,2048]{1,0:T(8,128)(2,1)} %get-tuple-element.33.cots_ref) | copy-start | bytes 15728644
  230.1 9.3 %copy-start.8 = (bf16[1024,2048]{1,0:T(8,128)(2,1)S(1)}, bf16[1024,2048]{1,0:T(8,128)(2,1)}, u32[]{:S(2)}) copy-start(bf16[1024,2048]{1,0:T(8,128)(2,1)} %get-tuple-element.36.down_ref) | copy-start | bytes 12582916
  239.4 15.3 %copy-start.10 = (bf16[1280,1024]{1,0:T(8,128)(2,1)}, bf16[1280,1024]{1,0:T(8,128)(2,1)S(1)}, u32[]{:S(2)}) copy-start(bf16[1280,1024]{1,0:T(8,128)(2,1)S(1)} %get-tuple-element.58.act_ref) | copy-start | bytes 7864324
  239.4 7.8 %copy-start.9 = (bf16[2048,1024]{1,0:T(8,128)(2,1)S(1)}, bf16[2048,1024]{1,0:T(8,128)(2,1)}, u32[]{:S(2)}) copy-start(bf16[2048,1024]{1,0:T(8,128)(2,1)} %get-tuple-element.35) | copy-start | bytes 12582916
  247.2 7.5 %copy-start.11 = (bf16[1280,1024]{1,0:T(8,128)(2,1)}, bf16[1280,1024]{1,0:T(8,128)(2,1)S(1)}, u32[]{:S(2)}) copy-start(bf16[1280,1024]{1,0:T(8,128)(2,1)S(1)} %fusion.5.d_up_ref) | copy-start | bytes 7864324
  496.8 5.1 copy-start
  498.2 5.1 %copy-start.6 = (f32[256,512]{1,0:T(8,128)S(1)}, f32[256,512]{1,0:T(8,128)}, u32[]{:S(2)}) copy-start(f32[256,512]{1,0:T(8,128)} %get-tuple-element.73) | copy-start | bytes 1572868
  501.9 2.3 copy-start.5
  501.9 3.1 copy-start.4
  501.9 3.9 copy-start.3
  501.9 4.7 copy-start.2
  503.4 4.5 copy-start.1

commit v7 on v6

--- a/solution.py
+++ b/solution.py
@@ -306,8 +306,8 @@
 
 def front_kernel(
     x_ref, w_query_ref, w_key_ref, w_value_ref, w_out_ref, w_up_ref, w_down_ref, gain_one_ref, gain_two_ref, cot_ref, valid_ref,
-    whole_ref, w_head_ref, qkv_ref, att_ref, lse_ref, attended_ref, out_ref, resid_ref, normed_ref, rate_ref, second_ref, up_ref, down_ref, cots_ref,
-    tokens, frames, w_own, w_head, up_own, out_all, att_low, came, part_low, core_in, half_low, chip_in, second, peak, total, acc, send, recv, local_sem,
+    whole_ref, w_head_ref, qkv_out, att_out, lse_ref, attended_out, out_ref, resid_out, normed_out, rate_ref, second_ref, up_ref, down_ref, cots_ref,
+    tokens, frames, w_own, w_head, up_own, out_all, att_low, came, part_low, core_in, half_low, chip_in, second, peak, total, acc, qkv_ref, att_ref, attended_ref, resid_ref, normed_ref, send, recv, local_sem,
 ):
     f32, bf16 = jnp.float32, jnp.bfloat16
     dp, z, t, other_dp, chip, core, pair = axes_of()
@@ -473,6 +473,7 @@
     arrive(token_core[3])
     keep(frames.at[3], whole_ref.at[3])
     project(3)
+    keep(qkv_ref, qkv_out)
     query_frame(0)
     arrive(out_step[1], out_step[3], out_dp[1])
     query_frame(1)
@@ -480,11 +481,13 @@
     arrive(cot_pair, cot_chip)
     query_frame(2)
     query_frame(3)
+    keep(att_ref, att_out)
     came[0] = att_low[0]
     arrive(out_step[3], out_dp[3], up_step[2])
     copies.wait(*back_home[1:])
     for h in range(SEQ):
         attended_ref[:, h * HEAD_DIM : (h + 1) * HEAD_DIM] = came[lax.rem(h - z + SEQ, SEQ)]
+    keep(attended_ref, attended_out)
     own_out.wait()
     copies.wait(*out_dp)
     keep(out_all, out_ref)
@@ -508,6 +511,8 @@
     resid_ref[...] = resid
     rate_ref[...] = rate
     normed_ref[...] = normed
+    keep(resid_ref, resid_out)
+    keep(normed_ref, normed_out)
     arrive(up_step[2], down_step[2], up_dp[2])
     arrive(second_chip[0], second_core[0])
     arrive(second_pair, second_chip[1], down_step[3])
@@ -536,13 +541,13 @@
     outs = [
         (shape((SEQ, rows, width), bf16), any_),
         (shape((width, three), bf16), any_),
-        (shape((SEQ, rows, three), bf16), vmem),
-        (shape((SEQ, rows, HEAD_DIM), f32), vmem),
+        (shape((SEQ, rows, three), bf16), any_),
+        (shape((SEQ, rows, HEAD_DIM), f32), any_),
         (shape((SEQ, 1, rows), f32), vmem),
-        (shape((rows, inner), bf16), vmem),
+        (shape((rows, inner), bf16), any_),
         (shape((inner, width), bf16), any_),
-        (shape((quarter, width), f32), vmem),
-        (shape((quarter, width), f32), vmem),
+        (shape((quarter, width), f32), any_),
+        (shape((quarter, width), f32), any_),
         (shape((quarter, 1), f32), vmem),
         (shape((2 * rows, width), bf16), any_),
         (shape((width, hidden // 2), bf16), any_),
@@ -566,6 +571,11 @@
         ((1, rows), f32),
         ((1, rows), f32),
         ((HEAD_DIM, rows), f32),
+        ((SEQ, rows, three), bf16),
+        ((SEQ, rows, HEAD_DIM), f32),
+        ((rows, inner), bf16),
+        ((quarter, width), f32),
+        ((quarter, width), f32),
     ]
     count = 3 * 3 + 4 + 3 * 7 + 3 + 2 + 5 + 3
     return pl.pallas_call(
@@ -582,10 +592,10 @@
 def back_kernel(
     gd_ref, d_up_ref, second_ref, act_ref, down_ref, dn_ref, resid_ref, cots_ref, normed_two_ref, rate_two_ref, attended_ref, out_ref, qkv_ref, att_ref, lse_ref, valid_ref, w_head_ref, whole_ref, x_ref,
     w_query_ref, w_key_ref, w_value_ref, w_up_ref, gain_one_ref, gain_two_ref,
-    down_sum_ref, up_sum_ref, out_sum_ref, grad_query_ref, grad_key_ref, grad_value_ref, gains_ref, grad_in_ref, result_ref,
+    down_sum_out, up_sum_out, out_sum_out, grad_query_out, grad_key_out, grad_value_out, gains_ref, grad_in_ref, result_ref,
     gu_ref, ff_ref, arrived_ref, cross_down_ref, cross_up_ref, far_down_ref, far_up_ref, dn_core_ref, dn_chip_ref, ff_core_ref, ff_chip_ref, pair_ref, first_core_ref, first_chip_ref, first_ring_ref,
     frames, temp, box_down, box_up, mix, d_head, d_out, dq, dk, dv, delta, d_three, out_send, out_cross, out_far, out_box,
-    head_acc, head_low, head_cross, head_sum, held_a, held_b, half_box, pair_box, mid, quart_box, in_box, gain_box, gain_came,
+    head_acc, head_low, head_cross, head_sum, held_a, held_b, half_box, pair_box, mid, quart_box, in_box, gain_box, gain_came, down_sum_ref, up_sum_ref, out_sum_ref, grad_query_ref, grad_key_ref, grad_value_ref,
     send, recv, keep_sem, load_sem, arena_sem, stage_sem,
 ):
     f32, bf16 = jnp.float32, jnp.bfloat16
@@ -639,7 +649,7 @@
     first_ring = [None] + [copies.make(in_box.at[k - 1], first_ring_ref.at[k - 1], along(1)) for k in range(1, SEQ)]
     head_dp = copies.make(head_low.at[1 - dp], head_cross, other_dp)
     head_out = [None] + [copies.make(head_sum.at[lax.rem(z + k, SEQ)], arrived_ref.at[k], along(k)) for k in range(1, SEQ)]
-    kept, numbered = [], []
+    kept = []
 
     def publish(n, ref):
         mine = ref.at[pl.ds(t * quarter, quarter), :]
@@ -652,10 +662,10 @@
     grad_out_copies, grad_own = publish(1, grad_in_ref)
 
     def keep(src, dst):
-        move = pltpu.make_async_copy(src, dst, keep_sem.at[SEQ + len(numbered)])
-        numbered.append(move)
+        move = pltpu.make_async_copy(src, dst, keep_sem.at[SEQ + len(kept)])
         kept.append(move)
         move.start()
+        return move
 
     def half_of(part_ref, core_ref, to_core, to_chip, i, n):
         copies.wait(to_core[i])
@@ -928,9 +938,11 @@
     in_box[0] = quarter_sum(1).astype(bf16)
     first_ring[1].start()
     total_of(gd_ref, cross_down_ref.at[0], far_down_ref, far_down, cross_down[0], store_turned)
+    keep(down_sum_ref, down_sum_out)
     half_sum(3)
     load((w_up_ref, held_a.at[pl.ds(0, part), :]))
     total_of(gu_ref, cross_up_ref.at[0], far_up_ref, far_up, cross_up[0], store_plain)
+    keep(up_sum_ref, up_sum_out)
     in_box[1] = quarter_sum(2).astype(bf16)
     first_ring[2].start()
     half_sum(0)
@@ -938,12 +950,13 @@
     for j in range(SEQ):
         at = slice(j * part, (j + 1) * part)
         head_sum[j] = (head_low[dp, :, at].astype(f32) + head_cross[:, at].astype(f32)).astype(bf16)
-    keep(head_sum.at[z], arrived_ref.at[0])
+    own_head = keep(head_sum.at[z], arrived_ref.at[0])
     copies.wait(cross_out[0], *far_out[1:])
     sum_ = out_block(block(dp, 0)) + out_cross[0].astype(f32)
     for k in range(1, SEQ):
         sum_ = sum_ + out_far[k - 1].astype(f32)
     out_sum_ref[...] = sum_
+    keep(out_sum_ref, out_sum_out)
     in_box[2] = quarter_sum(3).astype(bf16)
     first_ring[3].start()
     total = own_sum(ff_ref, ff_core_ref, ff_chip_ref, ff_chip, ff_pair, 1, resid_ref)
@@ -969,7 +982,7 @@
     copies.wait(result_out[0])
     result_out[2].start()
     copies.wait(*head_out[1:])
-    kept.pop(0).wait()
+    own_head.wait()
     load(
         *[(arrived_ref.at[k], head_cross.at[:, pl.ds(k * part, part)]) for k in range(SEQ)],
         *[(ref, held_a.at[pl.ds(0, part), pl.ds(n * inner, inner)]) for n, ref in enumerate((w_query_ref, w_key_ref, w_value_ref))],
@@ -982,6 +995,9 @@
             weight = held_a[0:part, n * inner + h * HEAD_DIM : n * inner + (h + 1) * HEAD_DIM].astype(f32)
             gain_first = gain_first + jnp.sum(weight * one, axis=1, keepdims=True)
             ref[:, h * HEAD_DIM : (h + 1) * HEAD_DIM] = one * gain
+    keep(grad_query_ref, grad_query_out)
+    keep(grad_key_ref, grad_key_out)
+    keep(grad_value_ref, grad_value_out)
     lane = lax.broadcasted_iota(jnp.int32, (part, HEAD_DIM), 1)
     gain_box[0] = jnp.where(lane == 0, gain_first, gain_sums[0] + gain_sums[1])
     gain_core.start()
@@ -994,7 +1010,8 @@
     gains_ref[...] = (gain_box[1] + gain_came[1]).T[0:8]
     copies.finish()
     for move in kept:
-        move.wait()
+        if move is not own_head:
+            move.wait()
 
 
 def back(gd, d_up, second, act, down, dn, resid, cots, normed_two, rate_two, attended, out_rel, qkv, att, lse, valid, w_head, whole, x, w_query, w_key, w_value, w_up, gain_one, gain_two):
@@ -1008,12 +1025,12 @@
     any_, vmem = pl.BlockSpec(memory_space=pl.ANY), pl.BlockSpec(memory_space=pltpu.VMEM)
     shape = jax.ShapeDtypeStruct
     outs = [
-        (shape((2 * side, part), f32), vmem),
-        (shape((part, 2 * side), f32), vmem),
-        (shape((inner, part), f32), vmem),
-        (shape((part, inner), f32), vmem),
-        (shape((part, inner), f32), vmem),
-        (shape((part, inner), f32), vmem),
+        (shape((2 * side, part), f32), any_),
+        (shape((part, 2 * side), f32), any_),
+        (shape((inner, part), f32), any_),
+        (shape((part, inner), f32), any_),
+        (shape((part, inner), f32), any_),
+        (shape((part, inner), f32), any_),
         (shape((8, part), f32), vmem),
         (shape((rows, width), bf16), any_),
         (shape((rows, width), bf16), any_),
@@ -1064,6 +1081,12 @@
         ((SEQ - 1, quarter, width), bf16),
         ((2, part, HEAD_DIM), f32),
         ((2, part, HEAD_DIM), f32),
+        ((2 * side, part), f32),
+        ((part, 2 * side), f32),
+        ((inner, part), f32),
+        ((part, inner), f32),
+        ((part, inner), f32),
+        ((part, inner), f32),
     ]
     return pl.pallas_call(
         back_kernel,
@@ -1071,7 +1094,7 @@
         in_specs=[any_] * 9 + [vmem, vmem, any_, vmem, any_, vmem, pl.BlockSpec(memory_space=pltpu.SMEM), vmem] + [any_] * 6 + [vmem] * 2,
         out_specs=[o[1] for o in outs],
         scratch_shapes=[pltpu.VMEM(*one) for one in scratch]
-        + [pltpu.SemaphoreType.DMA((count,)), pltpu.SemaphoreType.DMA((count,)), pltpu.SemaphoreType.DMA((SEQ + 3,)), pltpu.SemaphoreType.DMA((8,)), pltpu.SemaphoreType.DMA((6,)), pltpu.SemaphoreType.DMA((2,))],
+        + [pltpu.SemaphoreType.DMA((count,)), pltpu.SemaphoreType.DMA((count,)), pltpu.SemaphoreType.DMA((SEQ + 9,)), pltpu.SemaphoreType.DMA((8,)), pltpu.SemaphoreType.DMA((6,)), pltpu.SemaphoreType.DMA((2,))],
         compiler_params=pltpu.CompilerParams(collective_id=1, has_side_effects=True, vmem_limit_bytes=62 * 2**20),
         cost_estimate=pl.CostEstimate(flops=20 * 10**9, bytes_accessed=60 * 10**6, transcendentals=5 * 10**6),
     )(gd, d_up, second, act, down, dn, resid, cots, normed_two, rate_two, attended, out_rel, qkv, att, lse, valid, w_head, whole, x, w_query, w_key, w_value, w_up, gain_one, gain_two)[:9]

time: 519 us -> 515 us (level)
  no operation moved by 1% of the time
where the time goes in v7:
time: 515 us; the launch traced here: 505 us
  Pallas kernels  458 us (89%)
  matrix products  31.9 us (6%)
  local copies, waits for them, and re-layouts  14.8 us (3%)
    pallas_call x1, Pallas kernels, back(): pl.pallas_call(back_kernel, out_shape=[o[0] for o in outs], in_specs=[any...  233 us
    pallas_call x1, Pallas kernels, front(): pl.pallas_call(front_kernel, out_shape=[o[0] for o in outs], in_specs=[an...  225 us
    dot_general x4, matrix products, mm(): lax.dot_general(left, right, (dims, ((), ())), preferred_element_type=jnp...  31.9 us
    unnamed x32, local copies, waits for them, and re-layouts  11 us

profile of v7, /device:TPU:0, one launch (start us, length us, event | category | flops | bytes accessed | tf_op | source)
XLA Modules:
  0.0 505.3 jit_solution(3889069391071524021)
XLA Ops:
  0.6 1.2 broadcast_in_dim.12.gain_one_ref
  1.9 1.2 broadcast_in_dim.13.gain_two_ref
  3.1 224.9 %shard_map.186 = (bf16[4,640,2048]{2,1,0:T(8,128)(2,1)}, bf16[2048,384]{1,0:T(8,128)(2,1)}, bf16[4,640,384]{2,1,0:T(8,128)(2,1)}, f32[4,640,128]{2,1,0:T(8,128)}...) custom-call(bf16[640,2048]{1,0:T(8,128)(2,1)} %bitcast.19, ...), custom_call_target="tpu_custom_call" | custom-call | flops 8000000000 | bytes 50000000 | tf_op jit(solution)/shard_map/pallas_call | solution.py:581
  228.0 0.0 copy-start.7
  228.0 0.0 copy-start.8
  228.0 9.2 %multiply_convert_fusion = (bf16[1280,1024]{1,0:T(8,128)(2,1)S(1)}, f32[1280,1024]{1,0:T(8,128)S(1)}) fusion(bf16[1280,2048]{1,0:T(8,128)(2,1)} %get-tuple-element.34.second_ref, bf16[2048,1024]{1,0:T(8,128)(2,1)} %get-tuple-element.35), kind=kOutput, calls=%fused_computation.8 | convolution fusion | flops 5375262720 | bytes 17301504 | tf_op jit(solution)/shard_map/dot_general | solution.py:1104
  237.3 0.0 copy-start.10
  237.3 7.8 %fusion.5.d_up_ref = bf16[1280,1024]{1,0:T(8,128)(2,1)S(1)} fusion(f32[1280,1024]{1,0:T(8,128)S(1)} %get-tuple-element.59, bf16[1280,2048]{1,0:T(8,128)(2,1)S(1)} %copy-done.7, bf16[1024,2048]{1,0:T(8,128)(2,1)S(1)} %copy-done.8), kind=kOutput, calls=%fused_computation.7 | convolution fusion | flops 5381816320 | bytes 17301504 | tf_op jit(solution)/shard_map/dot_general | solution.py:1104
  245.1 0.0 copy-start.11
  245.1 7.5 %convolution_convert_fusion.dn_ref = bf16[1280,2048]{1,0:T(8,128)(2,1)} fusion(bf16[1280,1024]{1,0:T(8,128)(2,1)S(1)} %fusion.5.d_up_ref, bf16[2048,1024]{1,0:T(8,128)(2,1)S(1)} %copy-done.9), kind=kOutput, calls=%fused_computation.1 | convolution fusion | flops 5371330560 | bytes 12058624 | tf_op jit(solution)/shard_map/dot_general | solution.py:1104
  252.6 7.4 %convolution_convert_fusion.1.gd_ref = bf16[2048,1024]{1,0:T(8,128)(2,1)} fusion(bf16[1280,2048]{1,0:T(8,128)(2,1)S(1)} %copy-done.7, bf16[1280,1024]{1,0:T(8,128)(2,1)S(1)} %get-tuple-element.58.act_ref), kind=kOutput, calls=%fused_computation.10 | convolution fusion | flops 5370806272 | bytes 12058624 | tf_op jit(solution)/shard_map/dot_general | solution.py:1104
  260.0 232.7 %shard_map.187 = (f32[2048,256]{1,0:T(8,128)}, f32[256,2048]{1,0:T(8,128)}, f32[512,256]{1,0:T(8,128)}, f32[256,512]{1,0:T(8,128)}, f32[256,512]{1,0:T(8,128)}, ...) custom-call(bf16[2048,1024]{1,0:T(8,128)(2,1)} %convolution_convert_, ...), custom_call_target="tpu_custom_call" | custom-call | flops 20000000000 | bytes 60000000 | tf_op jit(solution)/shard_map/pallas_call | solution.py:1091
  492.7 1.4 fusion.6
  494.2 3.6 copy.29
  497.8 0.0 copy-done
  497.8 1.5 copy.30
  499.3 0.0 copy-done.6
  499.3 0.8 copy.31
  500.1 0.0 copy-done.5
  500.1 0.8 copy.32
  500.9 0.8 copy.33
  501.7 0.8 copy.34
  502.5 1.3 copy.35
  503.8 1.3 copy.36
  (17 shorter events, 0.0 us)
Async XLA Ops:
  228.0 9.3 %copy-start.7 = (bf16[1280,2048]{1,0:T(8,128)(2,1)S(1)}, bf16[1280,2048]{1,0:T(8,128)(2,1)}, u32[]{:S(2)}) copy-start(bf16[1280,2048]{1,0:T(8,128)(2,1)} %get-tuple-element.33.cots_ref) | copy-start | bytes 15728644
  228.0 9.3 %copy-start.8 = (bf16[1024,2048]{1,0:T(8,128)(2,1)S(1)}, bf16[1024,2048]{1,0:T(8,128)(2,1)}, u32[]{:S(2)}) copy-start(bf16[1024,2048]{1,0:T(8,128)(2,1)} %get-tuple-element.36.down_ref) | copy-start | bytes 12582916
  237.3 15.3 %copy-start.10 = (bf16[1280,1024]{1,0:T(8,128)(2,1)}, bf16[1280,1024]{1,0:T(8,128)(2,1)S(1)}, u32[]{:S(2)}) copy-start(bf16[1280,1024]{1,0:T(8,128)(2,1)S(1)} %get-tuple-element.58.act_ref) | copy-start | bytes 7864324
  237.3 7.8 %copy-start.9 = (bf16[2048,1024]{1,0:T(8,128)(2,1)S(1)}, bf16[2048,1024]{1,0:T(8,128)(2,1)}, u32[]{:S(2)}) copy-start(bf16[2048,1024]{1,0:T(8,128)(2,1)} %get-tuple-element.35) | copy-start | bytes 12582916
  245.1 7.5 %copy-start.11 = (bf16[1280,1024]{1,0:T(8,128)(2,1)}, bf16[1280,1024]{1,0:T(8,128)(2,1)S(1)}, u32[]{:S(2)}) copy-start(bf16[1280,1024]{1,0:T(8,128)(2,1)S(1)} %fusion.5.d_up_ref) | copy-start | bytes 7864324
  492.7 5.1 %copy-start = (bf16[640,2048]{1,0:T(8,128)(2,1)S(1)}, bf16[640,2048]{1,0:T(8,128)(2,1)}, u32[]{:S(2)}) copy-start(bf16[640,2048]{1,0:T(8,128)(2,1)} %get-tuple-element.48) | copy-start | bytes 7864324
  494.2 5.1 %copy-start.6 = (f32[256,512]{1,0:T(8,128)S(1)}, f32[256,512]{1,0:T(8,128)}, u32[]{:S(2)}) copy-start(f32[256,512]{1,0:T(8,128)} %get-tuple-element.73) | copy-start | bytes 1572868
  497.8 2.3 copy-start.5
  497.8 3.1 copy-start.4
  497.8 3.9 copy-start.3
  497.8 4.7 copy-start.2
  499.3 4.5 copy-start.1

commit v8 on v7

--- a/solution.py
+++ b/solution.py
@@ -293,7 +293,7 @@
 
 
 def column(row_ref):
-    row = jnp.broadcast_to(row_ref[...].astype(jnp.float32), (8, row_ref.shape[1]))
+    row = jnp.broadcast_to(row_ref[...].astype(jnp.float32)[None], (8, row_ref.shape[0]))
     return row.T[:, 0:1]
 
 
@@ -1107,7 +1107,7 @@
 def local_fast(inputs, first_gain, w_query, w_key, w_value, w_out, second_gain, w_up, w_down, frame_mask, cotangent):
     rows = inputs.shape[1]
     f32, bf16 = jnp.float32, jnp.bfloat16
-    gain_one, gain_two = first_gain[None], second_gain[None]
+    gain_one, gain_two = first_gain, second_gain
     valid = frame_mask
     whole, w_head, qkv, attended_f, lse, attended, out_all, resid_mid, normed_two, rate_two, second_in, up_side, down_side, cots = front(
         inputs[0], w_query, w_key, w_value, w_out, w_up, w_down, gain_one, gain_two, cotangent[0], valid

time: 515 us -> 512 us (level)
  no operation moved by 1% of the time
where the time goes in v8:
time: 512 us; the launch traced here: 503 us
  Pallas kernels  458 us (89%)
  matrix products  31.9 us (6%)
  local copies, waits for them, and re-layouts  12.4 us (2%)
    pallas_call x1, Pallas kernels, back(): pl.pallas_call(back_kernel, out_shape=[o[0] for o in outs], in_specs=[any...  233 us
    pallas_call x1, Pallas kernels, front(): pl.pallas_call(front_kernel, out_shape=[o[0] for o in outs], in_specs=[an...  225 us
    dot_general x4, matrix products, mm(): lax.dot_general(left, right, (dims, ((), ())), preferred_element_type=jnp...  31.9 us
    unnamed x32, local copies, waits for them, and re-layouts  11 us

profile of v8, /device:TPU:0, one launch (start us, length us, event | category | flops | bytes accessed | tf_op | source)
XLA Modules:
  0.0 502.9 jit_solution(357764630116315966)
XLA Ops:
  0.6 224.7 %shard_map.186 = (bf16[4,640,2048]{2,1,0:T(8,128)(2,1)}, bf16[2048,384]{1,0:T(8,128)(2,1)}, bf16[4,640,384]{2,1,0:T(8,128)(2,1)}, f32[4,640,128]{2,1,0:T(8,128)}...) custom-call(bf16[640,2048]{1,0:T(8,128)(2,1)} %bitcast.19, ...), custom_call_target="tpu_custom_call" | custom-call | flops 8000000000 | bytes 50000000 | tf_op jit(solution)/shard_map/pallas_call | solution.py:581
  225.4 0.0 copy-start.7
  225.4 0.0 copy-start.8
  225.4 9.2 %multiply_convert_fusion = (bf16[1280,1024]{1,0:T(8,128)(2,1)S(1)}, f32[1280,1024]{1,0:T(8,128)S(1)}) fusion(bf16[1280,2048]{1,0:T(8,128)(2,1)} %get-tuple-element.34.second_ref, bf16[2048,1024]{1,0:T(8,128)(2,1)} %get-tuple-element.35), kind=kOutput, calls=%fused_computation.8 | convolution fusion | flops 5375262720 | bytes 17301504 | tf_op jit(solution)/shard_map/dot_general | solution.py:1104
  234.6 0.0 copy-start.10
  234.7 7.8 %fusion.5.d_up_ref = bf16[1280,1024]{1,0:T(8,128)(2,1)S(1)} fusion(f32[1280,1024]{1,0:T(8,128)S(1)} %get-tuple-element.59, bf16[1280,2048]{1,0:T(8,128)(2,1)S(1)} %copy-done.7, bf16[1024,2048]{1,0:T(8,128)(2,1)S(1)} %copy-done.8), kind=kOutput, calls=%fused_computation.7 | convolution fusion | flops 5381816320 | bytes 17301504 | tf_op jit(solution)/shard_map/dot_general | solution.py:1104
  242.4 0.0 copy-done.9
  242.5 0.0 copy-start.11
  242.5 7.5 %convolution_convert_fusion.dn_ref = bf16[1280,2048]{1,0:T(8,128)(2,1)} fusion(bf16[1280,1024]{1,0:T(8,128)(2,1)S(1)} %fusion.5.d_up_ref, bf16[2048,1024]{1,0:T(8,128)(2,1)S(1)} %copy-done.9), kind=kOutput, calls=%fused_computation.1 | convolution fusion | flops 5371330560 | bytes 12058624 | tf_op jit(solution)/shard_map/dot_general | solution.py:1104
  250.0 0.0 copy-done.10
  250.0 7.4 %convolution_convert_fusion.1.gd_ref = bf16[2048,1024]{1,0:T(8,128)(2,1)} fusion(bf16[1280,2048]{1,0:T(8,128)(2,1)S(1)} %copy-done.7, bf16[1280,1024]{1,0:T(8,128)(2,1)S(1)} %get-tuple-element.58.act_ref), kind=kOutput, calls=%fused_computation.10 | convolution fusion | flops 5370806272 | bytes 12058624 | tf_op jit(solution)/shard_map/dot_general | solution.py:1104
  257.3 233.0 %shard_map.187 = (f32[2048,256]{1,0:T(8,128)}, f32[256,2048]{1,0:T(8,128)}, f32[512,256]{1,0:T(8,128)}, f32[256,512]{1,0:T(8,128)}, f32[256,512]{1,0:T(8,128)}, ...) custom-call(bf16[2048,1024]{1,0:T(8,128)(2,1)} %convolution_convert_, ...), custom_call_target="tpu_custom_call" | custom-call | flops 20000000000 | bytes 60000000 | tf_op jit(solution)/shard_map/pallas_call | solution.py:1091
  490.3 0.0 copy-start
  490.3 1.4 fusion.6
  491.8 3.6 copy.29
  495.4 1.5 copy.30
  496.9 0.8 copy.31
  497.7 0.8 copy.32
  498.5 0.8 copy.33
  499.3 0.0 copy-done.3
  499.3 0.8 copy.34
  500.1 1.3 copy.35
  501.4 0.0 copy-done.1
  501.4 1.3 copy.36
  (15 shorter events, 0.0 us)
Async XLA Ops:
  225.4 9.3 %copy-start.7 = (bf16[1280,2048]{1,0:T(8,128)(2,1)S(1)}, bf16[1280,2048]{1,0:T(8,128)(2,1)}, u32[]{:S(2)}) copy-start(bf16[1280,2048]{1,0:T(8,128)(2,1)} %get-tuple-element.33.cots_ref) | copy-start | bytes 15728644
  225.4 9.3 %copy-start.8 = (bf16[1024,2048]{1,0:T(8,128)(2,1)S(1)}, bf16[1024,2048]{1,0:T(8,128)(2,1)}, u32[]{:S(2)}) copy-start(bf16[1024,2048]{1,0:T(8,128)(2,1)} %get-tuple-element.36.down_ref) | copy-start | bytes 12582916
  234.6 15.3 %copy-start.10 = (bf16[1280,1024]{1,0:T(8,128)(2,1)}, bf16[1280,1024]{1,0:T(8,128)(2,1)S(1)}, u32[]{:S(2)}) copy-start(bf16[1280,1024]{1,0:T(8,128)(2,1)S(1)} %get-tuple-element.58.act_ref) | copy-start | bytes 7864324
  234.6 7.8 %copy-start.9 = (bf16[2048,1024]{1,0:T(8,128)(2,1)S(1)}, bf16[2048,1024]{1,0:T(8,128)(2,1)}, u32[]{:S(2)}) copy-start(bf16[2048,1024]{1,0:T(8,128)(2,1)} %get-tuple-element.35) | copy-start | bytes 12582916
  242.5 7.5 %copy-start.11 = (bf16[1280,1024]{1,0:T(8,128)(2,1)}, bf16[1280,1024]{1,0:T(8,128)(2,1)S(1)}, u32[]{:S(2)}) copy-start(bf16[1280,1024]{1,0:T(8,128)(2,1)S(1)} %fusion.5.d_up_ref) | copy-start | bytes 7864324
  490.3 5.1 %copy-start = (bf16[640,2048]{1,0:T(8,128)(2,1)S(1)}, bf16[640,2048]{1,0:T(8,128)(2,1)}, u32[]{:S(2)}) copy-start(bf16[640,2048]{1,0:T(8,128)(2,1)} %get-tuple-element.48) | copy-start | bytes 7864324
  491.8 5.1 %copy-start.6 = (f32[256,512]{1,0:T(8,128)S(1)}, f32[256,512]{1,0:T(8,128)}, u32[]{:S(2)}) copy-start(f32[256,512]{1,0:T(8,128)} %get-tuple-element.73) | copy-start | bytes 1572868
  495.4 2.3 copy-start.5
  495.4 3.1 copy-start.4
  495.4 3.9 copy-start.3
  495.4 4.7 copy-start.2
  496.9 4.5 copy-start.1
